TPU v7x, 128 devices: a whole 4x4x4 slice. The times are simulated.
128 devices in a mesh: scan: 32 (over z, y, core), col: 4 (over x).
Axes of the slice: x: 4, y: 4, z: 4, core: 2. Of those that a mesh axis runs over, the one named last changes fastest.
Arguments:
- raw_stack: bfloat16 [512, 2048, 512], P('scan', None, 'col'), may hold values from -10 to 10
- offsets: int32 [512], P('scan'), may hold values from 0 to 1788, as said below
Outputs:
- resampled: bfloat16 [512, 2048, 512], P('scan', None, 'col')
Inputs may be any that keep to these rules, and one draw needn't show every extreme that they name: offsets[0] is 0 and every later entry exceeds the one before it by 3 or 4; by 4 in exactly (511) // 2 of these steps.
All inputs are finite; a program needn't handle non-finite values.
Results may differ from a plain program's by a relative error of at most 0.0056.
Values may be sent and summed in bfloat16 or wider, within the bound.
No kernel may reach another device: no remote copies, remote signals or barrier semaphores. Data moves between devices by JAX's collectives and lax.ppermute only.
A program may use at most 256 MiB of HBM per device.

v0:
```python
import jax
import jax.numpy as jnp
from jax import lax
from jax.sharding import PartitionSpec as P

EDGE = 0.25
MIDDLE = 0.5


def padded_2(x, sides, width):
    for axis, dim in sides:
        devices, length = (lax.axis_size(axis), x.shape[dim])
        up = [(i, (i + 1) % devices) for i in range(devices - 1)]
        down = [(j, i) for i, j in up]
        last = lax.slice_in_dim(x, length - width, length, axis=dim)
        initial = lax.slice_in_dim(x, 0, width, axis=dim)
        before = lax.ppermute(last, axis, up)
        after = lax.ppermute(initial, axis, down)
        x = jnp.concatenate([before, x, after], axis=dim)
    return x


def mix_padded(padded):
    planes_mixed = EDGE * padded[:-2] + MIDDLE * padded[1:-1] + EDGE * padded[2:]
    return (
        EDGE * planes_mixed[:, :, :-2]
        + MIDDLE * planes_mixed[:, :, 1:-1]
        + EDGE * planes_mixed[:, :, 2:]
    )


def plane_weights(whole_part, fraction, out_count, in_count):
    target = jnp.arange(out_count, dtype=jnp.int32)[None, :, None] + whole_part[:, None, None]
    source = jnp.arange(in_count, dtype=jnp.int32)[None, None, :]
    share = fraction[:, None, None]
    return jnp.where(source == target, 1.0 - share, 0.0) + jnp.where(
        source == target + 1, share, 0.0
    )


def apply_weights(weights, values):
    mixed = jnp.einsum(
        "yqp,pyx->qyx", weights, values.astype(jnp.float32), precision=lax.Precision.HIGHEST
    )
    return mixed.astype(jnp.bfloat16)


def shear_planes(values, row_start, plane_total, row_total):
    row_index = row_start + jnp.arange(values.shape[1], dtype=jnp.int32)
    numerator = (2 * row_index - row_total + 1) * plane_total
    whole_part = numerator // (4 * row_total)
    fraction = (numerator - whole_part * (4 * row_total)).astype(jnp.float32) / (4.0 * row_total)
    weights = plane_weights(whole_part, fraction, plane_total, values.shape[0])
    return apply_weights(weights, values)


def shear_rows(values, plane_start, plane_total):
    plane_index = plane_start + jnp.arange(values.shape[0], dtype=jnp.int32)
    numerator = (2 * plane_index - plane_total + 1) * 17
    whole_part = numerator // 64
    fraction = (numerator - whole_part * 64).astype(jnp.float32) / 64.0
    margin = 17 * plane_total // 64 + 2
    row_total = values.shape[1]
    padded = jnp.pad(values, ((0, 0), (margin, margin), (0, 0)))

    def one_plane(inputs):
        single_plane, start, share = inputs
        window = lax.dynamic_slice_in_dim(single_plane, start + margin, row_total + 1, 0)
        mixed = (1.0 - share) * window[:-1].astype(jnp.float32) + share * window[1:].astype(
            jnp.float32
        )
        return mixed.astype(jnp.bfloat16)

    return lax.map(one_plane, (padded, whole_part, fraction))


def deskew_slab(raw_stack, offsets, skew_total):
    row_total = raw_stack.shape[1]

    def deskew_plane(single_plane, shift_rows):
        padded = jnp.pad(single_plane, ((row_total, row_total), (0, 0)))
        return lax.dynamic_slice_in_dim(
            padded, row_total - shift_rows + skew_total // 2, row_total, 0
        )

    return jax.vmap(deskew_plane)(raw_stack, offsets)


def local(raw_stack, offsets):
    slab_count = raw_stack.shape[0]
    row_total = raw_stack.shape[1]
    scan_count = lax.axis_size("scan")
    plane_total = slab_count * scan_count
    skew_total = 3 * (plane_total - 1) + (plane_total - 1) // 2
    deskewed = deskew_slab(raw_stack, offsets, skew_total)
    edged = padded_2(deskewed, (("scan", 0), ("col", 2)), 1)
    smoothed = mix_padded(edged.astype(jnp.float32)).astype(jnp.bfloat16)
    banded = lax.all_to_all(smoothed, "scan", split_axis=1, concat_axis=0, tiled=True)
    row_start = lax.axis_index("scan") * banded.shape[1]
    sheared = shear_planes(banded, row_start, plane_total, row_total)
    returned = lax.all_to_all(sheared, "scan", split_axis=0, concat_axis=1, tiled=True)
    return shear_rows(returned, lax.axis_index("scan") * slab_count, plane_total)


def solution(mesh):
    placed = (P("scan", None, "col"), P("scan"))
    return jax.shard_map(
        local, mesh=mesh, in_specs=placed, out_specs=P("scan", None, "col"), check_vma=False
    )
```

profile of v0, /device:TPU:0, one launch (start us, length us, event | category | flops | bytes accessed | tf_op | source)
XLA Modules:
  0.0 629.0 jit_solution(2476585739342161676)
XLA Ops:
  0.7 16.2 %pad.9 = bf16[16,6144,128]{2,1,0:T(8,128)(2,1)} pad(bf16[16,2048,128]{2,1,0:T(8,128)(2,1)} %param.4, bf16[]{:T(256)} %constant.145.clone.1), padding=0_0x2048_2048x0_0 | pad | bytes 33554432 | tf_op jit(solution)/shard_map/vmap(jit(_pad))/pad | solution.py:81
  16.9 5.0 broadcast_in_dim.30.clone
  21.9 62.3 %while.15 = (s32[]{:T(128)}, bf16[16,6144,128]{2,1,0:T(8,128)(2,1)}, s32[16,3]{0,1:T(4,128)S(1)}, bf16[16,2048,128]{2,1,0:T(8,128)(2,1)}, s32[]{:T(128)}) while((s32[]{:T(128)}, bf16[16,6144,128]{2,1,0:T(8,128)(2,1)}, s32[16,3]{0,1:T(4,128)S(1)}, bf16[16,2048,128]{2,1,0:T(8,128)(2,1)}, s32[]{:T(128)}) %tuple.47), condition=%wide.while_cond, body=%wide.while_body.sunk | while | flops 2 | bytes 1050217 | solution.py:82
  22.6 3.2 dynamic-slice_dynamic-update-slice_fusion.2
  26.5 3.2 dynamic-slice_dynamic-update-slice_fusion.2
  30.4 3.2 dynamic-slice_dynamic-update-slice_fusion.2
  34.3 3.2 dynamic-slice_dynamic-update-slice_fusion.2
  38.1 3.2 dynamic-slice_dynamic-update-slice_fusion.2
  42.0 3.2 dynamic-slice_dynamic-update-slice_fusion.2
  45.9 3.2 dynamic-slice_dynamic-update-slice_fusion.2
  49.8 3.2 dynamic-slice_dynamic-update-slice_fusion.2
  53.7 3.2 dynamic-slice_dynamic-update-slice_fusion.2
  57.6 3.2 dynamic-slice_dynamic-update-slice_fusion.2
  61.5 3.2 dynamic-slice_dynamic-update-slice_fusion.2
  65.4 3.2 dynamic-slice_dynamic-update-slice_fusion.2
  69.3 3.2 dynamic-slice_dynamic-update-slice_fusion.2
  73.2 3.2 dynamic-slice_dynamic-update-slice_fusion.2
  77.1 3.2 dynamic-slice_dynamic-update-slice_fusion.2
  81.0 3.2 dynamic-slice_dynamic-update-slice_fusion.2
  88.1 12.6 %copy.21 = bf16[16,2048,128]{1,0,2:T(8,128)(2,1)} copy(bf16[16,2048,128]{2,1,0:T(8,128)(2,1)} %get-tuple-element.97) | data formatting | bytes 16777216 | tf_op jit(solution)/shard_map/vmap()/gather | solution.py:82
  103.6 3.9 collective-permute-start.2
  109.7 4.3 collective-permute-done.3
  114.0 17.1 %maximum_convert_fusion = f32[18,2048,130]{1,0,2:T(8,128)} fusion(bf16[18,2048,1]{1,0,2:T(8,128)(2,1)S(1)} %collective-permute-done.3, bf16[1,2048,128]{1,0,2:T(2,128)(2,1)S(1)} %copy.22, bf16[16,2048,128]{1,0,2:T(8,128)(2,1)} %copy.21, bf16[1,2048,128]{1,0,2:T(2,128)(2,1)S(1)} %copy.20, bf16[18,2048,1]{1,0,2:T(8,128)(2,1)S(1)} %collective-permute-done.2), kind=kLoop, calls=%fused_computation.26 | loop fusion | flops 47923200 | bytes 28753920 | tf_op jit(solution)/shard_map/convert_element_type | solution.py:97
  131.1 30.6 %fusion.10 = f32[16,2048,130]{1,0,2:T(8,128)} fusion(f32[18,2048,130]{1,0,2:T(8,128)} %maximum_convert_fusion), kind=kLoop, calls=%fused_computation.16 | loop fusion | flops 21299200 | bytes 68157440 | tf_op jit(solution)/shard_map/add | solution.py:24
  161.7 20.8 %fusion.13 = bf16[16,2048,128]{1,0,2:T(8,128)(2,1)} fusion(f32[16,2048,130]{1,0,2:T(8,128)} %fusion.10), kind=kLoop, calls=%fused_computation.22 | loop fusion | flops 25165824 | bytes 58720256 | tf_op jit(solution)/shard_map/convert_element_type | solution.py:97
  182.4 13.3 %copy.23 = bf16[16,2048,128]{2,0,1:T(8,128)(2,1)} copy(bf16[16,2048,128]{1,0,2:T(8,128)(2,1)} %fusion.13) | data formatting | bytes 16777216 | tf_op jit(solution)/shard_map/convert_element_type | solution.py:97
  195.7 11.1 %all-to-all-start = ((bf16[16,2048,128]{2,0,1:T(8,128)(2,1)}), bf16[16,2048,128]{2,0,1:T(8,128)(2,1)}, u32[]{:S(2)}, u32[]{:S(2)}) async-start(bf16[16,2048,128]{2,0,1:T(8,128)(2,1)} %copy.23), calls=%async_computation | async-start | bytes 16777216 | tf_op jit(solution)/shard_map/all_to_all | solution.py:98
  207.0 105.6 %all-to-all-done = bf16[16,2048,128]{2,0,1:T(8,128)(2,1)} async-done(((bf16[16,2048,128]{2,0,1:T(8,128)(2,1)}), bf16[16,2048,128]{2,0,1:T(8,128)(2,1)}, u32[]{:S(2)}, u32[]{:S(2)}) %all-to-all-start) | async-done | bytes 8388640 | tf_op jit(solution)/shard_map/all_to_all | solution.py:98
  312.6 8.9 %copy.25 = bf16[32,16,64,128]{3,2,1,0:T(8,128)(2,1)} copy(bf16[32,16,64,128]{3,1,2,0:T(8,128)(2,1)} %bitcast.6) | data formatting | bytes 16777216 | tf_op jit(solution)/shard_map/all_to_all | solution.py:98
  321.5 64.0 %convert_bitcast_fusion = bf16[512,64,128]{0,2,1:T(8,128)(2,1)} fusion(f32[64]{0:T(128)S(1)} %get-tuple-element.124, s32[64,512]{1,0:T(8,128)S(1)} %get-tuple-element.123, f32[64]{0:T(128)S(1)} %get-tuple-element.125, s32[64,512]{1,0:T(8,128)S(1)} %get-tuple-element.122, bf16[512,64,128]{2,1,0:T(8,128)(2,1)} %bitcast.29), kind=kOutput, calls=%fused_computation.28 | convolution fusion | flops 25857884160 | bytes 17039872 | tf_op jit(solution)/shard_map/yqp,pyx->qyx/dot_general | solution.py:42
  385.5 11.9 %copy.27 = bf16[512,64,128]{2,1,0:T(8,128)(2,1)} copy(bf16[512,64,128]{0,2,1:T(8,128)(2,1)} %convert_bitcast_fusion) | data formatting | bytes 16777216 | tf_op jit(solution)/shard_map/convert_element_type | solution.py:45
  397.4 5.2 all-to-all-start.1
  402.7 105.6 %all-to-all-done.1 = bf16[512,64,128]{2,1,0:T(8,128)(2,1)} async-done(((bf16[512,64,128]{2,1,0:T(8,128)(2,1)}), bf16[512,64,128]{2,1,0:T(8,128)(2,1)}, u32[]{:S(2)}, u32[]{:S(2)}) %all-to-all-start.1) | async-done | bytes 8388640 | tf_op jit(solution)/shard_map/all_to_all | solution.py:101
  508.3 9.7 %copy.28 = bf16[16,32,64,128]{3,2,1,0:T(8,128)(2,1)} copy(bf16[16,32,64,128]{3,2,0,1:T(8,128)(2,1)} %bitcast.10) | data formatting | bytes 16777216 | tf_op jit(solution)/shard_map/all_to_all | solution.py:101
  518.0 9.4 %pad.10 = bf16[16,2324,128]{2,1,0:T(8,128)(2,1)} pad(bf16[16,2048,128]{2,1,0:T(8,128)(2,1)} %bitcast.28, bf16[]{:T(256)} %constant.145.clone.1), padding=0_0x138_138x0_0 | pad | bytes 17907714 | tf_op jit(solution)/shard_map/jit(_pad)/pad | solution.py:64
  527.4 5.0 broadcast_in_dim.30
  532.4 96.6 %while.14 = (s32[]{:T(128)}, bf16[16,2048,128]{2,1,0:T(8,128)(2,1)}, f32[16]{0:T(128)S(1)}, s32[16]{0:T(128)S(1)}, bf16[16,2324,128]{2,1,0:T(8,128)(2,1)}, /*ind...) while((s32[]{:T(128)}, ...), condition=%wide.region_1.2_spmd, body=%wide.region_0.1_spmd.sunk | while | flops 1572874 | bytes 1574155 | solution.py:74
  535.5 3.0 fusion.29
  541.5 3.0 fusion.29
  547.5 3.0 fusion.29
  553.6 3.0 fusion.29
  559.6 3.0 fusion.29
  565.6 3.0 fusion.29
  571.7 3.0 fusion.29
  589.7 3.0 fusion.29
  601.8 3.1 fusion.29
  608.0 3.0 fusion.29
  614.0 3.0 fusion.29
  (87 shorter events, 54.3 us)
Async XLA Ops:
  85.5 15.2 %collective-permute-start = (bf16[1,2048,128]{2,1,0:T(8,128)(2,1)S(1)}, bf16[1,2048,128]{2,1,0:T(8,128)(2,1)S(1)}, u32[]{:S(2)}, u32[]{:S(2)}) collective-permute-start(bf16[1,2048,128]{2,1,0:T(8,128)(2,1)S(1)} %get-tuple-element.120), channel_id=1, source_target_pairs={{0,4},{4,8},{8,12},{12,16},{16,20},{20,24},{24,28},{28,32},{32,36}... | collective-permute-start | bytes 1572872 | tf_op jit(solution)/shard_map/ppermute | solution.py:17
  86.8 14.8 %collective-permute-start.1 = (bf16[1,2048,128]{2,1,0:T(8,128)(2,1)S(1)}, bf16[1,2048,128]{2,1,0:T(8,128)(2,1)S(1)}, u32[]{:S(2)}, u32[]{:S(2)}) collective-permute-start(bf16[1,2048,128]{2,1,0:T(8,128)(2,1)S(1)} %get-tuple-element.121), channel_id=1, source_target_pairs={{4,0},{8,4},{12,8},{16,12},{20,16},{24,20},{28,24},{32,28},{36,32}... | collective-permute-start | bytes 1572872 | tf_op jit(solution)/shard_map/ppermute | solution.py:18
  103.6 6.1 collective-permute-start.2
  107.5 6.5 %collective-permute-start.3 = (bf16[18,2048,1]{1,0,2:T(8,128)(2,1)S(1)}, bf16[18,2048,1]{1,0,2:T(8,128)(2,1)S(1)}, u32[]{:S(2)}, u32[]{:S(2)}) collective-permute-start(bf16[18,2048,1]{1,0,2:T(8,128)(2,1)S(1)} %get-tuple-element.119), channel_id=1, source_target_pairs={{1,0},{2,1},{3,2},{5,4},{6,5},{7,6},{9,8},{10,9},{11,10},{13,12},{... | collective-permute-start | bytes 221192 | tf_op jit(solution)/shard_map/ppermute | solution.py:18
  195.7 116.8 %all-to-all-start = ((bf16[16,2048,128]{2,0,1:T(8,128)(2,1)}), bf16[16,2048,128]{2,0,1:T(8,128)(2,1)}, u32[]{:S(2)}, u32[]{:S(2)}) async-start(bf16[16,2048,128]{2,0,1:T(8,128)(2,1)} %copy.23), calls=%async_computation | async-start | bytes 16777216 | tf_op jit(solution)/shard_map/all_to_all | solution.py:98
  397.4 110.9 %all-to-all-start.1 = ((bf16[512,64,128]{2,1,0:T(8,128)(2,1)}), bf16[512,64,128]{2,1,0:T(8,128)(2,1)}, u32[]{:S(2)}, u32[]{:S(2)}) async-start(bf16[512,64,128]{2,1,0:T(8,128)(2,1)} %copy.27), calls=%async_computation.1 | async-start | bytes 16777216 | tf_op jit(solution)/shard_map/all_to_all | solution.py:101
where the time goes:
time: 633 us; the launch traced here: 629 us
  waiting for transfers between devices  216 us (34%)
  local copies, waits for them, and re-layouts  177 us (28%)
  other arithmetic  118 us (19%)
  matrix products  64 us (10%)
  loops' own time  29.8 us (5%)
  starting transfers between devices  24.2 us (4%)
    all_to_all x1, waiting for transfers between devices, local(): lax.all_to_all(sheared, 'scan', split_axis=0, concat_axis=1, tiled=True)  106 us
    all_to_all x1, waiting for transfers between devices, local(): lax.all_to_all(smoothed, 'scan', split_axis=1, concat_axis=0, tiled=True)  106 us
    dot_general x1, matrix products, apply_weights(): jnp.einsum('yqp,pyx->qyx', weights, values.astype(jnp.float32), precision...  64 us
    gather x48, local copies, waits for them, and re-layouts  62.3 us
    dynamic_update_slice x16, other arithmetic, shear_rows(): return lax.map(one_plane, (padded, whole_part, fraction))  47.5 us
    convert_element_type x2, other arithmetic, local(): smoothed = mix_padded(edged.astype(jnp.float32)).astype(jnp.bfloat16)  37.8 us
    add x1, other arithmetic, mix_padded(): EDGE * padded[:-2] + MIDDLE * padded[1:-1] + EDGE * padded[2:]  30.6 us
    another operation x1, loops' own time, shear_rows(): return lax.map(one_plane, (padded, whole_part, fraction))  29.8 us
  transfers between devices with their start and end apart: 6, of which 4 were waited for; matrix products, arithmetic and copies ran while one was open for 2% of the time, Pallas kernels for 0%

commit v1 on v0

v1 whole, which is shorter than its diff:
```python
import functools

import jax
import jax.numpy as jnp
from jax import lax
from jax.experimental import pallas as pl
from jax.experimental.pallas import tpu as pltpu
from jax.sharding import PartitionSpec as P

SLAB = 16
ROWS = 2048
COLS = 128
BLOCK = 128
PARTS = ROWS // BLOCK
SENDS = PARTS + 1
HALF_SKEW = 894
SCANS = 32
HELD = SLAB + 3
PAD = 128
EDGE_ROWS = 512
MARGIN = 144
VMEM_LIMIT = 60 * 1024 * 1024

ORDER = (4, -4, 8, -8, 3, -3, 7, -7, 5, -5, 1, -1, 2, -2, 6, -6)


def dot(a, b):
    return jnp.dot(a, b, preferred_element_type=jnp.float32)


def pack_edges_kernel(raw_ref, out_ref, planes, sem):
    def fetch(p):
        return pltpu.make_async_copy(raw_ref.at[p], planes.at[p], sem.at[p])

    for p in range(SLAB):
        fetch(p).start()
    src = lax.broadcasted_iota(jnp.int32, (COLS, COLS), 0)
    dst = lax.broadcasted_iota(jnp.int32, (COLS, COLS), 1)
    acc = [jnp.zeros((EDGE_ROWS, COLS), jnp.float32)]

    def one(p, total):
        fetch(p).wait()
        for g in range(4):
            pick = ((src == COLS - 1) & (dst == 32 * g + p)) | ((src == 0) & (dst == 32 * g + 16 + p))
            pick = jnp.where(pick, 1.0, 0.0).astype(jnp.bfloat16)
            total = total + dot(planes[p, EDGE_ROWS * g : EDGE_ROWS * (g + 1), :], pick)
        return total

    out_ref[...] = lax.fori_loop(0, SLAB, one, acc[0]).astype(jnp.bfloat16)


def pack_edges(raw):
    return pl.pallas_call(
        pack_edges_kernel,
        out_shape=jax.ShapeDtypeStruct((EDGE_ROWS, COLS), jnp.bfloat16),
        in_specs=[pl.BlockSpec(memory_space=pl.ANY)],
        out_specs=pl.BlockSpec(memory_space=pltpu.VMEM),
        scratch_shapes=[
            pltpu.VMEM((SLAB, ROWS, COLS), jnp.bfloat16),
            pltpu.SemaphoreType.DMA((SLAB,)),
        ],
        compiler_params=pltpu.CompilerParams(vmem_limit_bytes=VMEM_LIMIT),
        cost_estimate=pl.CostEstimate(flops=2 * SLAB * ROWS * COLS * COLS, bytes_accessed=2 * SLAB * ROWS * COLS, transcendentals=0),
        name="pack_edges",
    )(raw)


def shear_kernel(meta, raw_ref, before_ref, after_ref, edge_ref, edge_before, edge_after, *rest):
    outs = rest[:SENDS]
    planes, held, packed, sem, out_sem = rest[SENDS:]
    device = meta[HELD]

    def fetch_own():
        return pltpu.make_async_copy(raw_ref, planes.at[pl.ds(1, SLAB)], sem.at[0])

    def fetch_before():
        return pltpu.make_async_copy(before_ref, planes.at[pl.ds(0, 1)], sem.at[1])

    def fetch_after():
        return pltpu.make_async_copy(after_ref, planes.at[pl.ds(SLAB + 1, 2)], sem.at[2])

    for f in (fetch_own, fetch_before, fetch_after):
        f().start()

    zeros = jnp.zeros((PAD, COLS), jnp.float32)

    def clear(p, _):
        held[p, 0:PAD, :] = zeros
        held[p, PAD + ROWS : PAD + ROWS + PAD, :] = zeros
        return 0

    lax.fori_loop(0, HELD, clear, 0)
    for f in (fetch_own, fetch_before, fetch_after):
        f().wait()

    src = lax.broadcasted_iota(jnp.int32, (COLS, COLS), 0)
    dst = lax.broadcasted_iota(jnp.int32, (COLS, COLS), 1)
    tri = jnp.where(src == dst, 0.125, jnp.where(jnp.abs(src - dst) == 1, 0.0625, 0.0)).astype(jnp.bfloat16)

    def smooth(slot, plane, edges):
        for g in range(4):
            hit = ((src == 32 * g + plane) & (dst == 0)) | ((src == 32 * g + 16 + plane) & (dst == COLS - 1))
            edge = jnp.where(hit, 0.0625, 0.0).astype(jnp.bfloat16)
            weights = jnp.concatenate([tri, edge], axis=0)
            values = jnp.concatenate([planes[slot, EDGE_ROWS * g : EDGE_ROWS * (g + 1), :], edges[...]], axis=1)
            held[slot, PAD + EDGE_ROWS * g : PAD + EDGE_ROWS * (g + 1), :] = dot(values, weights)

    smooth(0, SLAB - 1, edge_before)

    def own(p, _):
        smooth(p + 1, p, edge_ref)
        return 0

    lax.fori_loop(0, SLAB, own, 0)
    smooth(SLAB + 1, 0, edge_after)
    smooth(SLAB + 2, 1, edge_after)

    share = (2 * lax.broadcasted_iota(jnp.int32, (8, COLS), 0) + 1).astype(jnp.float32) * 0.0625
    last = device == SCANS - 1

    def send(b, _):
        low = b < SENDS // 2
        role = jnp.logical_and(last, low)
        end = jnp.logical_and(last, jnp.logical_not(low))
        keep_15 = jnp.where(role, 0.0, 1.0).astype(jnp.float32)
        keep_16 = jnp.where(end, 0.0, 1.0).astype(jnp.float32)

        def starts(block, none):
            found = []
            for slot in range(HELD):
                dead = jnp.logical_or(none, role if slot <= SLAB else end)
                start = PAD + HALF_SKEW + block * BLOCK - meta[slot]
                start = jnp.clip(start, 0, PAD + ROWS)
                found.append(jnp.where(dead, 0, start))
            return found

        here = starts(b, b == SENDS - 1)
        above = starts(b - 1, b == 0)

        def mixed(r, bases, first, stop):
            x = {p: held[p + 1, pl.ds(bases[p + 1] + 8 * r, 8), :] for p in range(first - 1, stop + 2)}
            u = {}
            for p in range(first, stop + 1):
                u[p] = x[p - 1] + x[p + 1] + (x[p] + x[p])
                if p == SLAB - 1:
                    u[p] = u[p] * keep_15
                if p == SLAB:
                    u[p] = u[p] * keep_16
            return {p: u[p] + share * (u[p + 1] - u[p]) for p in range(first, stop)}

        def both(r):
            got = dict(mixed(r, here, r, SLAB))
            if r:
                got.update({p + SLAB: v for p, v in mixed(r, above, 0, r).items()})
            return got

        for t in range(8):
            even, odd = both(2 * t), both(2 * t + 1)
            for q in range(SLAB):
                tile = jnp.concatenate([even[q + 2 * t], odd[q + 2 * t + 1]], axis=0)
                packed[b, q, 16 * t : 16 * t + 16, :] = tile.astype(jnp.bfloat16)
        for i in range(SENDS):

            @pl.when(b == i)
            def _():
                pltpu.make_async_copy(packed.at[i], outs[i], out_sem.at[i]).start()

        return 0

    lax.fori_loop(0, SENDS, send, 0)
    for i in range(SENDS):
        pltpu.make_async_copy(packed.at[i], outs[i], out_sem.at[i]).wait()


def shear(meta, raw, before, after, edges, edges_before, edges_after):
    part = jax.ShapeDtypeStruct((SLAB, BLOCK, COLS), jnp.bfloat16)
    hbm = pl.BlockSpec(memory_space=pl.ANY)
    vmem = pl.BlockSpec(memory_space=pltpu.VMEM)
    return pl.pallas_call(
        shear_kernel,
        out_shape=(part,) * SENDS,
        in_specs=[pl.BlockSpec(memory_space=pltpu.SMEM), hbm, hbm, hbm, vmem, vmem, vmem],
        out_specs=(hbm,) * SENDS,
        scratch_shapes=[
            pltpu.VMEM((HELD, ROWS, COLS), jnp.bfloat16),
            pltpu.VMEM((HELD, PAD + ROWS + PAD, COLS), jnp.float32),
            pltpu.VMEM((SENDS, SLAB, BLOCK, COLS), jnp.bfloat16),
            pltpu.SemaphoreType.DMA((3,)),
            pltpu.SemaphoreType.DMA((SENDS,)),
        ],
        compiler_params=pltpu.CompilerParams(vmem_limit_bytes=VMEM_LIMIT),
        name="shear_planes",
    )(meta, raw, before, after, edges, edges_before, edges_after)


def rows_kernel(meta, *rest):
    parts = [None] * SENDS
    for at, c in enumerate(ORDER + (0,)):
        parts[c + 8] = rest[at]
    out_ref, got, full, done, sem, out_sem = rest[SENDS:]
    device = meta[HELD]

    def fetch(i):
        return pltpu.make_async_copy(parts[i], got.at[i], sem.at[i])

    for i in range(SENDS):
        fetch(i).start()
    zeros = jnp.zeros((MARGIN, COLS), jnp.float32)

    def clear(q, _):
        full[q, 0:MARGIN, :] = zeros
        full[q, MARGIN + ROWS : MARGIN + ROWS + MARGIN, :] = zeros
        return 0

    lax.fori_loop(0, SLAB, clear, 0)
    for i in range(SENDS):
        fetch(i).wait()
    upper = lax.broadcasted_iota(jnp.int32, (16, COLS), 0) < 8

    def merge(b, _):
        for q in range(SLAB):
            for t in range(8):
                rows = slice(16 * t, 16 * t + 16)
                if q + 2 * t + 1 < SLAB:
                    tile = got[b, q, rows, :].astype(jnp.float32)
                elif q + 2 * t >= SLAB:
                    tile = got[b + 1, q, rows, :].astype(jnp.float32)
                else:
                    tile = jnp.where(upper, got[b, q, rows, :].astype(jnp.float32), got[b + 1, q, rows, :].astype(jnp.float32))
                full[q, pl.ds(pl.multiple_of(MARGIN + b * BLOCK + 16 * t, 16), 16), :] = tile
        return 0

    lax.fori_loop(0, PARTS, merge, 0)

    def put(q):
        return pltpu.make_async_copy(done.at[q], out_ref.at[q], out_sem.at[q])

    def plane(q, _):
        numerator = 17 * (2 * (device * SLAB + q) - (SLAB * SCANS - 1))
        start = MARGIN + lax.shift_right_arithmetic(numerator, 6)
        share = (numerator & 63).astype(jnp.float32) * (1.0 / 64.0)

        def rows(i, _):
            for t in range(16):
                base = start + i * 256 + 16 * t
                a = full[q, pl.ds(base, 16), :]
                c = full[q, pl.ds(base + 1, 16), :]
                done[q, pl.ds(pl.multiple_of(i * 256 + 16 * t, 16), 16), :] = (a + share * (c - a)).astype(jnp.bfloat16)
            return 0

        lax.fori_loop(0, ROWS // 256, rows, 0)
        put(q).start()
        return 0

    lax.fori_loop(0, SLAB, plane, 0)
    for q in range(SLAB):
        put(q).wait()


def shear_rows(meta, parts):
    hbm = pl.BlockSpec(memory_space=pl.ANY)
    return pl.pallas_call(
        rows_kernel,
        out_shape=jax.ShapeDtypeStruct((SLAB, ROWS, COLS), jnp.bfloat16),
        in_specs=[pl.BlockSpec(memory_space=pltpu.SMEM)] + [hbm] * SENDS,
        out_specs=hbm,
        scratch_shapes=[
            pltpu.VMEM((SENDS, SLAB, BLOCK, COLS), jnp.bfloat16),
            pltpu.VMEM((SLAB, MARGIN + ROWS + MARGIN, COLS), jnp.float32),
            pltpu.VMEM((SLAB, ROWS, COLS), jnp.bfloat16),
            pltpu.SemaphoreType.DMA((SENDS,)),
            pltpu.SemaphoreType.DMA((SLAB,)),
        ],
        compiler_params=pltpu.CompilerParams(vmem_limit_bytes=VMEM_LIMIT),
        name="shear_rows",
    )(meta, *parts)


def pairs_of(c):
    found = [(s, s - c) for s in range(SCANS) if 0 <= s - c < SCANS]
    if c < 0:
        found.append((SCANS - 1, -c - 1))
    return found


def local(raw, offsets):
    device = lax.axis_index("scan")
    up = [(i, i + 1) for i in range(SCANS - 1)]
    down = [((i + 1) % SCANS, i) for i in range(SCANS)]
    right = [(i, i + 1) for i in range(3)]
    left = [(i + 1, i) for i in range(3)]
    after = lax.ppermute(raw[:2], "scan", down)
    before = lax.ppermute(raw[SLAB - 1 :], "scan", up)
    offsets_after = lax.ppermute(offsets[:2], "scan", down)
    offsets_before = lax.ppermute(offsets[SLAB - 1 :], "scan", up)
    own = pack_edges(raw)
    from_left = lax.ppermute(own, "col", right)
    from_right = lax.ppermute(own, "col", left)
    lane = lax.broadcasted_iota(jnp.int32, own.shape, 1)
    edges = jnp.where(lane % 32 < 16, from_left, from_right)
    edges_after = lax.ppermute(edges, "scan", down)
    edges_before = lax.ppermute(edges, "scan", up)
    meta = jnp.concatenate([offsets_before, offsets, offsets_after, device[None].astype(jnp.int32)])
    parts = list(shear(meta, raw, before, after, edges, edges_before, edges_after))
    moved = [lax.ppermute(parts[c + 8], "scan", pairs_of(c)) for c in ORDER]
    return shear_rows(meta, moved + [parts[8]])


def solution(mesh):
    placed = (P("scan", None, "col"), P("scan"))
    return jax.shard_map(local, mesh=mesh, in_specs=placed, out_specs=P("scan", None, "col"), check_vma=False)
```

time: 633 us -> 176 us (0.28)
  the two profiles are of different devices: /device:TPU:0 before, /device:TPU:39 now
where the time goes in v1:
time: 176 us; the launch traced here: 175 us
  starting transfers between devices  71.6 us (41%)
  waiting for transfers between devices  59.9 us (34%)
  Pallas kernels  36.8 us (21%)
  local copies, waits for them, and re-layouts  4.82 us (3%)
    ppermute x16, waiting for transfers between devices, local(): moved = [lax.ppermute(parts[c + 8], 'scan', pairs_of(c)) for c in ORDER]  57.3 us
    ppermute x16, starting transfers between devices, local(): moved = [lax.ppermute(parts[c + 8], 'scan', pairs_of(c)) for c in ORDER]  51.8 us
    pallas_call x1, Pallas kernels, shear(): pl.pallas_call(shear_kernel, out_shape=(part,) * SENDS, in_specs=[pl.Bloc...  20.2 us
    pallas_call x1, Pallas kernels, shear_rows(): pl.pallas_call(rows_kernel, out_shape=jax.ShapeDtypeStruct((SLAB, ROWS, C...  9.98 us
    pallas_call x1, Pallas kernels, pack_edges(): pl.pallas_call(pack_edges_kernel, out_shape=jax.ShapeDtypeStruct((EDGE_RO...  6.62 us
    ppermute x1, starting transfers between devices, local(): offsets_after = lax.ppermute(offsets[:2], 'scan', down)  4.27 us
  transfers between devices with their start and end apart: 24, of which 9 were waited for; matrix products, arithmetic and copies ran while one was open for 2% of the time, Pallas kernels for 4%

profile of v1, /device:TPU:39, one launch (start us, length us, event | category | flops | bytes accessed | tf_op | source)
XLA Modules:
  0.0 174.9 jit_solution(15347552637468042000)
XLA Ops:
  0.0 1.3 slice.15
  1.3 0.7 collective-permute-start.3
  2.1 6.6 %pack_edges.1 = bf16[512,128]{1,0:T(8,128)(2,1)} custom-call(bf16[16,2048,128]{2,1,0:T(8,128)(2,1)} %raw_ref.3), custom_call_target="tpu_custom_call" | custom-call | flops 1073741824 | bytes 8388608 | tf_op jit(solution)/shard_map/pack_edges/pallas_call | solution.py:53
  8.7 2.5 %collective-permute-start.5 = (bf16[512,128]{1,0:T(8,128)(2,1)}, bf16[512,128]{1,0:T(8,128)(2,1)S(1)}, u32[]{:S(2)}, u32[]{:S(2)}) collective-permute-start(bf16[512,128]{1,0:T(8,128)(2,1)} %pack_edges.1), channel_id=1, source_target_pairs={{1,0},{2,1},{3,2},{5,4},{6,5},{7,6},{9,8},{10,9},{11,10},{13,12},{... | collective-permute-start | bytes 393224 | tf_op jit(solution)/shard_map/ppermute | solution.py:298
  11.2 1.3 collective-permute-start.4
  12.4 1.1 slice.14
  13.5 3.4 %collective-permute-start.2 = (bf16[1,2048,128]{2,1,0:T(8,128)(2,1)S(1)}, bf16[1,2048,128]{2,1,0:T(8,128)(2,1)S(1)}, u32[]{:S(2)}, u32[]{:S(2)}) collective-permute-start(bf16[1,2048,128]{2,1,0:T(8,128)(2,1)S(1)} %slice.14), channel_id=1, source_target_pairs={{0,4},{4,8},{8,12},{12,16},{16,20},{20,24},{24,28},{28,32},{32,36}... | collective-permute-start | bytes 1572872 | tf_op jit(solution)/shard_map/ppermute | solution.py:293
  17.0 0.1 collective-permute-done.4
  17.1 3.5 %collective-permute-start.7 = (bf16[512,128]{1,0:T(8,128)(2,1)S(1)}, bf16[512,128]{1,0:T(8,128)(2,1)S(1)}, u32[]{:S(2)}, u32[]{:S(2)}) collective-permute-start(bf16[512,128]{1,0:T(8,128)(2,1)S(1)} %fusion.edge_ref), channel_id=1, source_target_pairs={{4,0},{8,4},{12,8},{16,12},{20,16},{24,20},{28,24},{32,28},{36,32}... | collective-permute-start | bytes 393224 | tf_op jit(solution)/shard_map/ppermute | solution.py:301
  20.6 1.9 %collective-permute-start.6 = (bf16[512,128]{1,0:T(8,128)(2,1)S(1)}, bf16[512,128]{1,0:T(8,128)(2,1)S(1)}, u32[]{:S(2)}, u32[]{:S(2)}) collective-permute-start(bf16[512,128]{1,0:T(8,128)(2,1)S(1)} %fusion.edge_ref), channel_id=1, source_target_pairs={{0,4},{4,8},{8,12},{12,16},{16,20},{20,24},{24,28},{28,32},{32,36}... | collective-permute-start | bytes 393224 | tf_op jit(solution)/shard_map/ppermute | solution.py:302
  22.6 0.6 slice.12
  23.1 2.2 %collective-permute-start = (s32[1]{0:T(128)}, s32[1]{0:T(128)}, u32[]{:S(2)}, u32[]{:S(2)}) collective-permute-start(s32[1]{0:T(128)} %slice.12), channel_id=1, source_target_pairs={{0,4},{4,8},{8,12},{12,16},{16,20},{20,24},{24,28},{28,32},{32,36}... | collective-permute-start | bytes 20 | tf_op jit(solution)/shard_map/ppermute | solution.py:295
  25.4 1.7 collective-permute-done
  27.1 4.3 %collective-permute-start.1 = (s32[2]{0:T(128)S(1)}, s32[2]{0:T(128)S(1)}, u32[]{:S(2)}, u32[]{:S(2)}) collective-permute-start(s32[2]{0:T(128)S(1)} %bitcast.2), channel_id=1, source_target_pairs={{4,0},{8,4},{12,8},{16,12},{20,16},{24,20},{28,24},{32,28},{36,32}... | collective-permute-start | bytes 32 | tf_op jit(solution)/shard_map/ppermute | solution.py:294
  31.4 0.8 collective-permute-done.1
  32.2 1.3 pad_add_fusion.meta
  33.5 0.0 collective-permute-done.2.before_ref
  33.5 0.6 copy-done.10
  34.2 0.0 copy-done.11
  34.2 0.2 copy-done.8
  34.4 1.0 copy-done
  35.4 20.2 %shear_planes.1 = (bf16[16,128,128]{2,1,0:T(8,128)(2,1)}, bf16[16,128,128]{2,1,0:T(8,128)(2,1)}, bf16[16,128,128]{2,1,0:T(8,128)(2,1)}, bf16[16,128,128]{2,1,0:T...) custom-call(s32[20]{0:T(128)} %pad_add_fusion.meta, ...), custom_call_target="tpu_custom_call" | custom-call | tf_op jit(solution)/shard_map/shear_planes/pallas_call | solution.py:179
  55.6 3.2 %collective-permute-start.8 = (bf16[16,128,128]{2,1,0:T(8,128)(2,1)}, bf16[16,128,128]{2,1,0:T(8,128)(2,1)S(1)}, u32[]{:S(2)}, u32[]{:S(2)}) collective-permute-start(bf16[16,128,128]{2,1,0:T(8,128)(2,1)} %get-tuple-element.22), channel_id=1, source_target_pairs={{16,0},{20,4},{24,8},{28,12},{32,16},{36,20},{40,24},{44,28},{48,3... | collective-permute-start | bytes 1572872 | tf_op jit(solution)/shard_map/ppermute | solution.py:305
  58.8 3.5 %collective-permute-start.9 = (bf16[16,128,128]{2,1,0:T(8,128)(2,1)}, bf16[16,128,128]{2,1,0:T(8,128)(2,1)S(1)}, u32[]{:S(2)}, u32[]{:S(2)}) collective-permute-start(bf16[16,128,128]{2,1,0:T(8,128)(2,1)} %get-tuple-element.23), channel_id=1, source_target_pairs={{0,16},{4,20},{8,24},{12,28},{16,32},{20,36},{24,40},{28,44},{32,4... | collective-permute-start | bytes 1572872 | tf_op jit(solution)/shard_map/ppermute | solution.py:305
  62.4 3.0 %collective-permute-start.10 = (bf16[16,128,128]{2,1,0:T(8,128)(2,1)}, bf16[16,128,128]{2,1,0:T(8,128)(2,1)S(1)}, u32[]{:S(2)}, u32[]{:S(2)}) collective-permute-start(bf16[16,128,128]{2,1,0:T(8,128)(2,1)} %get-tuple-element.24), channel_id=1, source_target_pairs={{32,0},{36,4},{40,8},{44,12},{48,16},{52,20},{56,24},{60,28},{64,3... | collective-permute-start | bytes 1572872 | tf_op jit(solution)/shard_map/ppermute | solution.py:305
  65.3 2.5 %collective-permute-start.11 = (bf16[16,128,128]{2,1,0:T(8,128)(2,1)}, bf16[16,128,128]{2,1,0:T(8,128)(2,1)S(1)}, u32[]{:S(2)}, u32[]{:S(2)}) collective-permute-start(bf16[16,128,128]{2,1,0:T(8,128)(2,1)} %get-tuple-element.25), channel_id=1, source_target_pairs={{0,32},{4,36},{8,40},{12,44},{16,48},{20,52},{24,56},{28,60},{32,6... | collective-permute-start | bytes 1572872 | tf_op jit(solution)/shard_map/ppermute | solution.py:305
  67.9 4.0 %collective-permute-start.12 = (bf16[16,128,128]{2,1,0:T(8,128)(2,1)}, bf16[16,128,128]{2,1,0:T(8,128)(2,1)S(1)}, u32[]{:S(2)}, u32[]{:S(2)}) collective-permute-start(bf16[16,128,128]{2,1,0:T(8,128)(2,1)} %get-tuple-element.26), channel_id=1, source_target_pairs={{12,0},{16,4},{20,8},{24,12},{28,16},{32,20},{36,24},{40,28},{44,3... | collective-permute-start | bytes 1572872 | tf_op jit(solution)/shard_map/ppermute | solution.py:305
  71.8 0.3 collective-permute-done.8.rest_0_
  72.1 4.8 %collective-permute-start.13 = (bf16[16,128,128]{2,1,0:T(8,128)(2,1)}, bf16[16,128,128]{2,1,0:T(8,128)(2,1)S(1)}, u32[]{:S(2)}, u32[]{:S(2)}) collective-permute-start(bf16[16,128,128]{2,1,0:T(8,128)(2,1)} %get-tuple-element.27), channel_id=1, source_target_pairs={{0,12},{4,16},{8,20},{12,24},{16,28},{20,32},{24,36},{28,40},{32,4... | collective-permute-start | bytes 1572872 | tf_op jit(solution)/shard_map/ppermute | solution.py:305
  77.0 8.1 %collective-permute-done.9.rest_1_ = bf16[16,128,128]{2,1,0:T(8,128)(2,1)S(1)} collective-permute-done((bf16[16,128,128]{2,1,0:T(8,128)(2,1)}, bf16[16,128,128]{2,1,0:T(8,128)(2,1)S(1)}, u32[]{:S(2)}, u32[]{:S(2)}) %collective-permute-start.9) | collective-permute-done | bytes 524320 | tf_op jit(solution)/shard_map/ppermute | solution.py:305
  85.1 1.9 %collective-permute-start.14 = (bf16[16,128,128]{2,1,0:T(8,128)(2,1)}, bf16[16,128,128]{2,1,0:T(8,128)(2,1)S(1)}, u32[]{:S(2)}, u32[]{:S(2)}) collective-permute-start(bf16[16,128,128]{2,1,0:T(8,128)(2,1)} %get-tuple-element.28), channel_id=1, source_target_pairs={{28,0},{32,4},{36,8},{40,12},{44,16},{48,20},{52,24},{56,28},{60,3... | collective-permute-start | bytes 1572872 | tf_op jit(solution)/shard_map/ppermute | solution.py:305
  87.0 3.8 %collective-permute-start.15 = (bf16[16,128,128]{2,1,0:T(8,128)(2,1)}, bf16[16,128,128]{2,1,0:T(8,128)(2,1)}, u32[]{:S(2)}, u32[]{:S(2)}) collective-permute-start(bf16[16,128,128]{2,1,0:T(8,128)(2,1)} %get-tuple-element.29), channel_id=1, source_target_pairs={{0,28},{4,32},{8,36},{12,40},{16,44},{20,48},{24,52},{28,56},{32,6... | collective-permute-start | bytes 1572872 | tf_op jit(solution)/shard_map/ppermute | solution.py:305
  90.9 17.7 %collective-permute-done.11.rest_3_ = bf16[16,128,128]{2,1,0:T(8,128)(2,1)S(1)} collective-permute-done((bf16[16,128,128]{2,1,0:T(8,128)(2,1)}, bf16[16,128,128]{2,1,0:T(8,128)(2,1)S(1)}, u32[]{:S(2)}, u32[]{:S(2)}) %collective-permute-start.11) | collective-permute-done | bytes 524320 | tf_op jit(solution)/shard_map/ppermute | solution.py:305
  108.6 1.9 %collective-permute-start.16 = (bf16[16,128,128]{2,1,0:T(8,128)(2,1)}, bf16[16,128,128]{2,1,0:T(8,128)(2,1)}, u32[]{:S(2)}, u32[]{:S(2)}) collective-permute-start(bf16[16,128,128]{2,1,0:T(8,128)(2,1)} %get-tuple-element.30), channel_id=1, source_target_pairs={{20,0},{24,4},{28,8},{32,12},{36,16},{40,20},{44,24},{48,28},{52,3... | collective-permute-start | bytes 1572872 | tf_op jit(solution)/shard_map/ppermute | solution.py:305
  110.5 0.0 collective-permute-done.12.rest_4_
  110.5 4.9 %collective-permute-start.17 = (bf16[16,128,128]{2,1,0:T(8,128)(2,1)}, bf16[16,128,128]{2,1,0:T(8,128)(2,1)}, u32[]{:S(2)}, u32[]{:S(2)}) collective-permute-start(bf16[16,128,128]{2,1,0:T(8,128)(2,1)} %get-tuple-element.31), channel_id=1, source_target_pairs={{0,20},{4,24},{8,28},{12,32},{16,36},{20,40},{24,44},{28,48},{32,5... | collective-permute-start | bytes 1572872 | tf_op jit(solution)/shard_map/ppermute | solution.py:305
  115.4 0.0 collective-permute-done.13.rest_5_
  115.4 4.4 %collective-permute-start.18 = (bf16[16,128,128]{2,1,0:T(8,128)(2,1)}, bf16[16,128,128]{2,1,0:T(8,128)(2,1)}, u32[]{:S(2)}, u32[]{:S(2)}) collective-permute-start(bf16[16,128,128]{2,1,0:T(8,128)(2,1)} %get-tuple-element.32), channel_id=1, source_target_pairs={{4,0},{8,4},{12,8},{16,12},{20,16},{24,20},{28,24},{32,28},{36,32}... | collective-permute-start | bytes 1572872 | tf_op jit(solution)/shard_map/ppermute | solution.py:305
  119.8 0.1 collective-permute-start.19
  119.9 0.0 collective-permute-done.15.rest_7_
  119.9 5.3 %collective-permute-start.20 = (bf16[16,128,128]{2,1,0:T(8,128)(2,1)}, bf16[16,128,128]{2,1,0:T(8,128)(2,1)}, u32[]{:S(2)}, u32[]{:S(2)}) collective-permute-start(bf16[16,128,128]{2,1,0:T(8,128)(2,1)} %get-tuple-element.34), channel_id=1, source_target_pairs={{8,0},{12,4},{16,8},{20,12},{24,16},{28,20},{32,24},{36,28},{40,32... | collective-permute-start | bytes 1572872 | tf_op jit(solution)/shard_map/ppermute | solution.py:305
  125.2 10.5 %collective-permute-done.16.rest_8_ = bf16[16,128,128]{2,1,0:T(8,128)(2,1)} collective-permute-done((bf16[16,128,128]{2,1,0:T(8,128)(2,1)}, bf16[16,128,128]{2,1,0:T(8,128)(2,1)}, u32[]{:S(2)}, u32[]{:S(2)}) %collective-permute-start.16) | collective-permute-done | bytes 524320 | tf_op jit(solution)/shard_map/ppermute | solution.py:305
  135.8 1.9 %collective-permute-start.21 = (bf16[16,128,128]{2,1,0:T(8,128)(2,1)}, bf16[16,128,128]{2,1,0:T(8,128)(2,1)}, u32[]{:S(2)}, u32[]{:S(2)}) collective-permute-start(bf16[16,128,128]{2,1,0:T(8,128)(2,1)} %get-tuple-element.35), channel_id=1, source_target_pairs={{0,8},{4,12},{8,16},{12,20},{16,24},{20,28},{24,32},{28,36},{32,40... | collective-permute-start | bytes 1572872 | tf_op jit(solution)/shard_map/ppermute | solution.py:305
  137.7 1.9 %collective-permute-start.22 = (bf16[16,128,128]{2,1,0:T(8,128)(2,1)}, bf16[16,128,128]{2,1,0:T(8,128)(2,1)}, u32[]{:S(2)}, u32[]{:S(2)}) collective-permute-start(bf16[16,128,128]{2,1,0:T(8,128)(2,1)} %get-tuple-element.36), channel_id=1, source_target_pairs={{24,0},{28,4},{32,8},{36,12},{40,16},{44,20},{48,24},{52,28},{56,3... | collective-permute-start | bytes 1572872 | tf_op jit(solution)/shard_map/ppermute | solution.py:305
  139.6 4.6 %collective-permute-start.23 = (bf16[16,128,128]{2,1,0:T(8,128)(2,1)}, bf16[16,128,128]{2,1,0:T(8,128)(2,1)}, u32[]{:S(2)}, u32[]{:S(2)}) collective-permute-start(bf16[16,128,128]{2,1,0:T(8,128)(2,1)} %get-tuple-element.37), channel_id=1, source_target_pairs={{0,24},{4,28},{8,32},{12,36},{16,40},{20,44},{24,48},{28,52},{32,5... | collective-permute-start | bytes 1572872 | tf_op jit(solution)/shard_map/ppermute | solution.py:305
  144.2 11.5 %collective-permute-done.21.rest_13_ = bf16[16,128,128]{2,1,0:T(8,128)(2,1)} collective-permute-done((bf16[16,128,128]{2,1,0:T(8,128)(2,1)}, bf16[16,128,128]{2,1,0:T(8,128)(2,1)}, u32[]{:S(2)}, u32[]{:S(2)}) %collective-permute-start.21) | collective-permute-done | bytes 524320 | tf_op jit(solution)/shard_map/ppermute | solution.py:305
  155.7 9.2 %collective-permute-done.22.rest_14_ = bf16[16,128,128]{2,1,0:T(8,128)(2,1)} collective-permute-done((bf16[16,128,128]{2,1,0:T(8,128)(2,1)}, bf16[16,128,128]{2,1,0:T(8,128)(2,1)}, u32[]{:S(2)}, u32[]{:S(2)}) %collective-permute-start.22) | collective-permute-done | bytes 524320 | tf_op jit(solution)/shard_map/ppermute | solution.py:305
  164.9 10.0 %shear_rows.1 = bf16[16,2048,128]{2,1,0:T(8,128)(2,1)} custom-call(s32[20]{0:T(128)} %pad_add_fusion.meta, bf16[16,128,128]{2,1,0:T(8,128)(2,1)} %copy-done.1, bf16[16,128,128]{2,1,0:T(8,128)(2,1)} %copy-done.2, bf16[16,128,128]{2,1,0:T(8,128)(2,1)} %copy-done.3, bf16[16,128,128]{2,1,0:T(8,128)(2,1)} %copy-done.4, bf16[16,128,128]{2,1,0:T(8,128)(2,1)} %copy-done.5, ...), custom_call_target="tpu_custom_call" | custom-call | tf_op jit(solution)/shard_map/shear_rows/pallas_call | solution.py:262
  (36 shorter events, 0.1 us)
Async XLA Ops:
  0.0 22.5 %copy-start.12 = (s32[16]{0:T(128)S(1)}, s32[16]{0:T(128)}, u32[]{:S(2)}) copy-start(s32[16]{0:T(128)} %param.3) | copy-start | bytes 196
  1.3 32.2 %collective-permute-start.3 = (bf16[2,2048,128]{2,1,0:T(8,128)(2,1)S(1)}, bf16[2,2048,128]{2,1,0:T(8,128)(2,1)S(1)}, u32[]{:S(2)}, u32[]{:S(2)}) collective-permute-start(bf16[2,2048,128]{2,1,0:T(8,128)(2,1)S(1)} %slice.15), channel_id=1, source_target_pairs={{4,0},{8,4},{12,8},{16,12},{20,16},{24,20},{28,24},{32,28},{36,32}... | collective-permute-start | bytes 3145736 | tf_op jit(solution)/shard_map/ppermute | solution.py:292
  8.7 8.3 %collective-permute-start.5 = (bf16[512,128]{1,0:T(8,128)(2,1)}, bf16[512,128]{1,0:T(8,128)(2,1)S(1)}, u32[]{:S(2)}, u32[]{:S(2)}) collective-permute-start(bf16[512,128]{1,0:T(8,128)(2,1)} %pack_edges.1), channel_id=1, source_target_pairs={{1,0},{2,1},{3,2},{5,4},{6,5},{7,6},{9,8},{10,9},{11,10},{13,12},{... | collective-permute-start | bytes 393224 | tf_op jit(solution)/shard_map/ppermute | solution.py:298
  11.2 5.9 %collective-permute-start.4 = (bf16[512,128]{1,0:T(8,128)(2,1)}, bf16[512,128]{1,0:T(8,128)(2,1)S(1)}, u32[]{:S(2)}, u32[]{:S(2)}) collective-permute-start(bf16[512,128]{1,0:T(8,128)(2,1)} %pack_edges.1), channel_id=1, source_target_pairs={{0,1},{1,2},{2,3},{4,5},{5,6},{6,7},{8,9},{9,10},{10,11},{12,13},{... | collective-permute-start | bytes 393224 | tf_op jit(solution)/shard_map/ppermute | solution.py:297
  13.5 20.0 %collective-permute-start.2 = (bf16[1,2048,128]{2,1,0:T(8,128)(2,1)S(1)}, bf16[1,2048,128]{2,1,0:T(8,128)(2,1)S(1)}, u32[]{:S(2)}, u32[]{:S(2)}) collective-permute-start(bf16[1,2048,128]{2,1,0:T(8,128)(2,1)S(1)} %slice.14), channel_id=1, source_target_pairs={{0,4},{4,8},{8,12},{12,16},{16,20},{20,24},{24,28},{28,32},{32,36}... | collective-permute-start | bytes 1572872 | tf_op jit(solution)/shard_map/ppermute | solution.py:293
  17.1 16.4 %copy-start.9 = (bf16[512,128]{1,0:T(8,128)(2,1)}, bf16[512,128]{1,0:T(8,128)(2,1)S(1)}, u32[]{:S(2)}) copy-start(bf16[512,128]{1,0:T(8,128)(2,1)S(1)} %fusion.edge_ref) | copy-start | bytes 393220
  17.1 16.4 %collective-permute-start.7 = (bf16[512,128]{1,0:T(8,128)(2,1)S(1)}, bf16[512,128]{1,0:T(8,128)(2,1)S(1)}, u32[]{:S(2)}, u32[]{:S(2)}) collective-permute-start(bf16[512,128]{1,0:T(8,128)(2,1)S(1)} %fusion.edge_ref), channel_id=1, source_target_pairs={{4,0},{8,4},{12,8},{16,12},{20,16},{24,20},{28,24},{32,28},{36,32}... | collective-permute-start | bytes 393224 | tf_op jit(solution)/shard_map/ppermute | solution.py:301
  20.6 12.9 %collective-permute-start.6 = (bf16[512,128]{1,0:T(8,128)(2,1)S(1)}, bf16[512,128]{1,0:T(8,128)(2,1)S(1)}, u32[]{:S(2)}, u32[]{:S(2)}) collective-permute-start(bf16[512,128]{1,0:T(8,128)(2,1)S(1)} %fusion.edge_ref), channel_id=1, source_target_pairs={{0,4},{4,8},{8,12},{12,16},{16,20},{20,24},{24,28},{28,32},{32,36}... | collective-permute-start | bytes 393224 | tf_op jit(solution)/shard_map/ppermute | solution.py:302
  23.1 4.0 %collective-permute-start = (s32[1]{0:T(128)}, s32[1]{0:T(128)}, u32[]{:S(2)}, u32[]{:S(2)}) collective-permute-start(s32[1]{0:T(128)} %slice.12), channel_id=1, source_target_pairs={{0,4},{4,8},{8,12},{12,16},{16,20},{20,24},{24,28},{28,32},{32,36}... | collective-permute-start | bytes 20 | tf_op jit(solution)/shard_map/ppermute | solution.py:295
  27.1 5.1 %collective-permute-start.1 = (s32[2]{0:T(128)S(1)}, s32[2]{0:T(128)S(1)}, u32[]{:S(2)}, u32[]{:S(2)}) collective-permute-start(s32[2]{0:T(128)S(1)} %bitcast.2), channel_id=1, source_target_pairs={{4,0},{8,4},{12,8},{16,12},{20,16},{24,20},{28,24},{32,28},{36,32}... | collective-permute-start | bytes 32 | tf_op jit(solution)/shard_map/ppermute | solution.py:294
  33.5 0.7 copy-start.10
  33.5 0.7 copy-start.11
  33.5 0.9 copy-start.8
  34.4 1.0 copy-start
  55.6 16.6 %collective-permute-start.8 = (bf16[16,128,128]{2,1,0:T(8,128)(2,1)}, bf16[16,128,128]{2,1,0:T(8,128)(2,1)S(1)}, u32[]{:S(2)}, u32[]{:S(2)}) collective-permute-start(bf16[16,128,128]{2,1,0:T(8,128)(2,1)} %get-tuple-element.22), channel_id=1, source_target_pairs={{16,0},{20,4},{24,8},{28,12},{32,16},{36,20},{40,24},{44,28},{48,3... | collective-permute-start | bytes 1572872 | tf_op jit(solution)/shard_map/ppermute | solution.py:305
  58.8 26.3 %collective-permute-start.9 = (bf16[16,128,128]{2,1,0:T(8,128)(2,1)}, bf16[16,128,128]{2,1,0:T(8,128)(2,1)S(1)}, u32[]{:S(2)}, u32[]{:S(2)}) collective-permute-start(bf16[16,128,128]{2,1,0:T(8,128)(2,1)} %get-tuple-element.23), channel_id=1, source_target_pairs={{0,16},{4,20},{8,24},{12,28},{16,32},{20,36},{24,40},{28,44},{32,4... | collective-permute-start | bytes 1572872 | tf_op jit(solution)/shard_map/ppermute | solution.py:305
  62.4 24.6 %collective-permute-start.10 = (bf16[16,128,128]{2,1,0:T(8,128)(2,1)}, bf16[16,128,128]{2,1,0:T(8,128)(2,1)S(1)}, u32[]{:S(2)}, u32[]{:S(2)}) collective-permute-start(bf16[16,128,128]{2,1,0:T(8,128)(2,1)} %get-tuple-element.24), channel_id=1, source_target_pairs={{32,0},{36,4},{40,8},{44,12},{48,16},{52,20},{56,24},{60,28},{64,3... | collective-permute-start | bytes 1572872 | tf_op jit(solution)/shard_map/ppermute | solution.py:305
  65.3 43.2 %collective-permute-start.11 = (bf16[16,128,128]{2,1,0:T(8,128)(2,1)}, bf16[16,128,128]{2,1,0:T(8,128)(2,1)S(1)}, u32[]{:S(2)}, u32[]{:S(2)}) collective-permute-start(bf16[16,128,128]{2,1,0:T(8,128)(2,1)} %get-tuple-element.25), channel_id=1, source_target_pairs={{0,32},{4,36},{8,40},{12,44},{16,48},{20,52},{24,56},{28,60},{32,6... | collective-permute-start | bytes 1572872 | tf_op jit(solution)/shard_map/ppermute | solution.py:305
  67.9 42.6 %collective-permute-start.12 = (bf16[16,128,128]{2,1,0:T(8,128)(2,1)}, bf16[16,128,128]{2,1,0:T(8,128)(2,1)S(1)}, u32[]{:S(2)}, u32[]{:S(2)}) collective-permute-start(bf16[16,128,128]{2,1,0:T(8,128)(2,1)} %get-tuple-element.26), channel_id=1, source_target_pairs={{12,0},{16,4},{20,8},{24,12},{28,16},{32,20},{36,24},{40,28},{44,3... | collective-permute-start | bytes 1572872 | tf_op jit(solution)/shard_map/ppermute | solution.py:305
  72.1 92.7 %copy-start.1 = (bf16[16,128,128]{2,1,0:T(8,128)(2,1)}, bf16[16,128,128]{2,1,0:T(8,128)(2,1)S(1)}, u32[]{:S(2)}) copy-start(bf16[16,128,128]{2,1,0:T(8,128)(2,1)S(1)} %collective-permute-done.8.rest_0_) | copy-start | bytes 1572868
  72.1 43.2 %collective-permute-start.13 = (bf16[16,128,128]{2,1,0:T(8,128)(2,1)}, bf16[16,128,128]{2,1,0:T(8,128)(2,1)S(1)}, u32[]{:S(2)}, u32[]{:S(2)}) collective-permute-start(bf16[16,128,128]{2,1,0:T(8,128)(2,1)} %get-tuple-element.27), channel_id=1, source_target_pairs={{0,12},{4,16},{8,20},{12,24},{16,28},{20,32},{24,36},{28,40},{32,4... | collective-permute-start | bytes 1572872 | tf_op jit(solution)/shard_map/ppermute | solution.py:305
  85.1 79.8 %copy-start.2 = (bf16[16,128,128]{2,1,0:T(8,128)(2,1)}, bf16[16,128,128]{2,1,0:T(8,128)(2,1)S(1)}, u32[]{:S(2)}) copy-start(bf16[16,128,128]{2,1,0:T(8,128)(2,1)S(1)} %collective-permute-done.9.rest_1_) | copy-start | bytes 1572868
  85.1 34.7 %collective-permute-start.14 = (bf16[16,128,128]{2,1,0:T(8,128)(2,1)}, bf16[16,128,128]{2,1,0:T(8,128)(2,1)S(1)}, u32[]{:S(2)}, u32[]{:S(2)}) collective-permute-start(bf16[16,128,128]{2,1,0:T(8,128)(2,1)} %get-tuple-element.28), channel_id=1, source_target_pairs={{28,0},{32,4},{36,8},{40,12},{44,16},{48,20},{52,24},{56,28},{60,3... | collective-permute-start | bytes 1572872 | tf_op jit(solution)/shard_map/ppermute | solution.py:305
  87.0 77.9 %copy-start.3 = (bf16[16,128,128]{2,1,0:T(8,128)(2,1)}, bf16[16,128,128]{2,1,0:T(8,128)(2,1)S(1)}, u32[]{:S(2)}) copy-start(bf16[16,128,128]{2,1,0:T(8,128)(2,1)S(1)} %collective-permute-done.10.rest_2_) | copy-start | bytes 1572868
  87.0 32.9 %collective-permute-start.15 = (bf16[16,128,128]{2,1,0:T(8,128)(2,1)}, bf16[16,128,128]{2,1,0:T(8,128)(2,1)}, u32[]{:S(2)}, u32[]{:S(2)}) collective-permute-start(bf16[16,128,128]{2,1,0:T(8,128)(2,1)} %get-tuple-element.29), channel_id=1, source_target_pairs={{0,28},{4,32},{8,36},{12,40},{16,44},{20,48},{24,52},{28,56},{32,6... | collective-permute-start | bytes 1572872 | tf_op jit(solution)/shard_map/ppermute | solution.py:305
  108.6 56.3 %copy-start.4 = (bf16[16,128,128]{2,1,0:T(8,128)(2,1)}, bf16[16,128,128]{2,1,0:T(8,128)(2,1)S(1)}, u32[]{:S(2)}) copy-start(bf16[16,128,128]{2,1,0:T(8,128)(2,1)S(1)} %collective-permute-done.11.rest_3_) | copy-start | bytes 1572868
  108.6 27.2 %collective-permute-start.16 = (bf16[16,128,128]{2,1,0:T(8,128)(2,1)}, bf16[16,128,128]{2,1,0:T(8,128)(2,1)}, u32[]{:S(2)}, u32[]{:S(2)}) collective-permute-start(bf16[16,128,128]{2,1,0:T(8,128)(2,1)} %get-tuple-element.30), channel_id=1, source_target_pairs={{20,0},{24,4},{28,8},{32,12},{36,16},{40,20},{44,24},{48,28},{52,3... | collective-permute-start | bytes 1572872 | tf_op jit(solution)/shard_map/ppermute | solution.py:305
  110.5 54.4 %copy-start.5 = (bf16[16,128,128]{2,1,0:T(8,128)(2,1)}, bf16[16,128,128]{2,1,0:T(8,128)(2,1)S(1)}, u32[]{:S(2)}) copy-start(bf16[16,128,128]{2,1,0:T(8,128)(2,1)S(1)} %collective-permute-done.12.rest_4_) | copy-start | bytes 1572868
  110.5 27.2 %collective-permute-start.17 = (bf16[16,128,128]{2,1,0:T(8,128)(2,1)}, bf16[16,128,128]{2,1,0:T(8,128)(2,1)}, u32[]{:S(2)}, u32[]{:S(2)}) collective-permute-start(bf16[16,128,128]{2,1,0:T(8,128)(2,1)} %get-tuple-element.31), channel_id=1, source_target_pairs={{0,20},{4,24},{8,28},{12,32},{16,36},{20,40},{24,44},{28,48},{32,5... | collective-permute-start | bytes 1572872 | tf_op jit(solution)/shard_map/ppermute | solution.py:305
  115.4 49.5 %copy-start.6 = (bf16[16,128,128]{2,1,0:T(8,128)(2,1)}, bf16[16,128,128]{2,1,0:T(8,128)(2,1)S(1)}, u32[]{:S(2)}) copy-start(bf16[16,128,128]{2,1,0:T(8,128)(2,1)S(1)} %collective-permute-done.13.rest_5_) | copy-start | bytes 1572868
  115.4 24.3 %collective-permute-start.18 = (bf16[16,128,128]{2,1,0:T(8,128)(2,1)}, bf16[16,128,128]{2,1,0:T(8,128)(2,1)}, u32[]{:S(2)}, u32[]{:S(2)}) collective-permute-start(bf16[16,128,128]{2,1,0:T(8,128)(2,1)} %get-tuple-element.32), channel_id=1, source_target_pairs={{4,0},{8,4},{12,8},{16,12},{20,16},{24,20},{28,24},{32,28},{36,32}... | collective-permute-start | bytes 1572872 | tf_op jit(solution)/shard_map/ppermute | solution.py:305
  119.8 45.1 %copy-start.7 = (bf16[16,128,128]{2,1,0:T(8,128)(2,1)}, bf16[16,128,128]{2,1,0:T(8,128)(2,1)S(1)}, u32[]{:S(2)}) copy-start(bf16[16,128,128]{2,1,0:T(8,128)(2,1)S(1)} %collective-permute-done.14.rest_6_) | copy-start | bytes 1572868
  119.8 24.4 %collective-permute-start.19 = (bf16[16,128,128]{2,1,0:T(8,128)(2,1)}, bf16[16,128,128]{2,1,0:T(8,128)(2,1)}, u32[]{:S(2)}, u32[]{:S(2)}) collective-permute-start(bf16[16,128,128]{2,1,0:T(8,128)(2,1)} %get-tuple-element.33), channel_id=1, source_target_pairs={{0,4},{4,8},{8,12},{12,16},{16,20},{20,24},{24,28},{28,32},{32,36}... | collective-permute-start | bytes 1572872 | tf_op jit(solution)/shard_map/ppermute | solution.py:305
  119.9 24.3 %collective-permute-start.20 = (bf16[16,128,128]{2,1,0:T(8,128)(2,1)}, bf16[16,128,128]{2,1,0:T(8,128)(2,1)}, u32[]{:S(2)}, u32[]{:S(2)}) collective-permute-start(bf16[16,128,128]{2,1,0:T(8,128)(2,1)} %get-tuple-element.34), channel_id=1, source_target_pairs={{8,0},{12,4},{16,8},{20,12},{24,16},{28,20},{32,24},{36,28},{40,32... | collective-permute-start | bytes 1572872 | tf_op jit(solution)/shard_map/ppermute | solution.py:305
  135.8 19.9 %collective-permute-start.21 = (bf16[16,128,128]{2,1,0:T(8,128)(2,1)}, bf16[16,128,128]{2,1,0:T(8,128)(2,1)}, u32[]{:S(2)}, u32[]{:S(2)}) collective-permute-start(bf16[16,128,128]{2,1,0:T(8,128)(2,1)} %get-tuple-element.35), channel_id=1, source_target_pairs={{0,8},{4,12},{8,16},{12,20},{16,24},{20,28},{24,32},{28,36},{32,40... | collective-permute-start | bytes 1572872 | tf_op jit(solution)/shard_map/ppermute | solution.py:305
  137.7 27.2 %collective-permute-start.22 = (bf16[16,128,128]{2,1,0:T(8,128)(2,1)}, bf16[16,128,128]{2,1,0:T(8,128)(2,1)}, u32[]{:S(2)}, u32[]{:S(2)}) collective-permute-start(bf16[16,128,128]{2,1,0:T(8,128)(2,1)} %get-tuple-element.36), channel_id=1, source_target_pairs={{24,0},{28,4},{32,8},{36,12},{40,16},{44,20},{48,24},{52,28},{56,3... | collective-permute-start | bytes 1572872 | tf_op jit(solution)/shard_map/ppermute | solution.py:305
  139.6 25.2 %collective-permute-start.23 = (bf16[16,128,128]{2,1,0:T(8,128)(2,1)}, bf16[16,128,128]{2,1,0:T(8,128)(2,1)}, u32[]{:S(2)}, u32[]{:S(2)}) collective-permute-start(bf16[16,128,128]{2,1,0:T(8,128)(2,1)} %get-tuple-element.37), channel_id=1, source_target_pairs={{0,24},{4,28},{8,32},{12,36},{16,40},{20,44},{24,48},{28,52},{32,5... | collective-permute-start | bytes 1572872 | tf_op jit(solution)/shard_map/ppermute | solution.py:305

commit v2 on v1

v2 whole, which is shorter than its diff:
```python
import functools

import jax
import jax.numpy as jnp
import numpy as np
from jax import lax
from jax.experimental import pallas as pl
from jax.experimental.pallas import tpu as pltpu
from jax.sharding import PartitionSpec as P

SLAB = 16
ROWS = 2048
COLS = 128
BLOCK = 128
SENDS = ROWS // BLOCK + 1
HALF_SKEW = 894
SCANS = 32
HELD = SLAB + 3
PAD = 128
EDGE_ROWS = 512
MARGIN = 144
VMEM_LIMIT = 60 * 1024 * 1024

ORDER = (4, -4, 8, -8, 3, -3, 7, -7, 5, -5, 1, -1, 2, -2, 6, -6)
EARLY = ORDER[:8]
LATE = ORDER[8:] + (0,)
CODED = ROWS + 16
FIRST, STOP = 3, 13

HBM = pl.BlockSpec(memory_space=pl.ANY)
VMEM = pl.BlockSpec(memory_space=pltpu.VMEM)
SMEM = pl.BlockSpec(memory_space=pltpu.SMEM)

COST = pl.CostEstimate(flops=1000, bytes_accessed=1000, transcendentals=0)


def dot(a, b):
    return jnp.dot(a, b, preferred_element_type=jnp.float32)


def halos_kernel(offsets, raw_ref, first_ref, final_ref, planes, sem, out_sem):
    sides = ((first_ref, 0, 0), (first_ref, 1, 1), (final_ref, 0, SLAB - 1))
    loads = [pltpu.make_async_copy(raw_ref.at[p], planes.at[n, pl.ds(0, ROWS)], sem.at[n]) for n, (_, _, p) in enumerate(sides)]
    for load in loads:
        load.start()
    lane = lax.broadcasted_iota(jnp.int32, (16, COLS), 1)
    for n, (_, _, p) in enumerate(sides):
        shift = offsets[p]
        code = jnp.where(lane == 0, lax.shift_right_logical(shift, 4), jnp.where(lane == 1, shift & 15, 0))
        planes[n, ROWS:CODED, :] = code.astype(jnp.float32).astype(jnp.bfloat16)
    stores = []
    for n, (ref, at, _) in enumerate(sides):
        loads[n].wait()
        stores.append(pltpu.make_async_copy(planes.at[n], ref.at[at], out_sem.at[n]))
        stores[-1].start()
    for store in stores:
        store.wait()


def halos(offsets, raw):
    return pl.pallas_call(
        halos_kernel,
        out_shape=tuple(jax.ShapeDtypeStruct((n, CODED, COLS), jnp.bfloat16) for n in (2, 1)),
        in_specs=[SMEM, HBM],
        out_specs=(HBM, HBM),
        scratch_shapes=[pltpu.VMEM((3, CODED, COLS), jnp.bfloat16), pltpu.SemaphoreType.DMA((3,)), pltpu.SemaphoreType.DMA((3,))],
        cost_estimate=COST,
        name="halos",
    )(offsets, raw)


def pack_edges_kernel(raw_ref, out_ref, planes, sem):
    def fetch(g):
        rows = pl.ds(EDGE_ROWS * g, EDGE_ROWS)
        return pltpu.make_async_copy(raw_ref.at[:, rows], planes.at[:, rows], sem.at[g])

    for g in range(4):
        fetch(g).start()
    src = lax.broadcasted_iota(jnp.int32, (SLAB * COLS, COLS), 0)
    dst = lax.broadcasted_iota(jnp.int32, (SLAB * COLS, COLS), 1)
    pick = (src == COLS * dst + COLS - 1) | (src == COLS * (dst - 16))
    pick = jnp.where(pick & (dst < 32), 1.0, 0.0).astype(jnp.bfloat16)
    total = None
    for g in range(4):
        fetch(g).wait()
        rows = slice(EDGE_ROWS * g, EDGE_ROWS * (g + 1))
        values = jnp.concatenate([planes[p, rows, :] for p in range(SLAB)], axis=1)
        found = dot(values, pick)
        total = found if g == 0 else total + pltpu.roll(found, 32 * g, 1)
    out_ref[...] = total.astype(jnp.bfloat16)


def pack_edges(raw):
    return pl.pallas_call(
        pack_edges_kernel,
        out_shape=jax.ShapeDtypeStruct((EDGE_ROWS, COLS), jnp.bfloat16),
        in_specs=[HBM],
        out_specs=VMEM,
        scratch_shapes=[
            pltpu.VMEM((SLAB, ROWS, COLS), jnp.bfloat16),
            pltpu.SemaphoreType.DMA((4,)),
        ],
        compiler_params=pltpu.CompilerParams(vmem_limit_bytes=VMEM_LIMIT),
        cost_estimate=COST,
        name="pack_edges",
    )(raw)


def column_weights():
    held = np.zeros((SLAB, 2 * COLS, COLS), np.float32)
    for at in range(COLS):
        held[:, at, at] = 0.125
        held[:, at, [n for n in (at - 1, at + 1) if 0 <= n < COLS]] = 0.0625
    for p in range(SLAB):
        for g in range(4):
            held[p, COLS + 32 * g + p, 0] = 0.0625
            held[p, COLS + 32 * g + 16 + p, COLS - 1] = 0.0625
    return jnp.asarray(held, jnp.bfloat16)


def shear_kernel(group, offsets, raw_ref, before_ref, after_ref, *rest):
    count = len(group)
    late = group == LATE
    if late:
        weights_ref, edges_before, edges_own, edges_after, *rest = rest
    outs, rest = rest[:count], rest[count:]
    planes, held, packed, codes, offs, sem, out_sem, code_sem, *rest = rest
    device = lax.axis_index("scan")
    last = device == SCANS - 1
    beside_refs = ((0, before_ref, 0), (SLAB + 1, after_ref, 0), (SLAB + 2, after_ref, 1))

    code_copies = [
        pltpu.make_async_copy(ref.at[p, pl.ds(ROWS, 16)], codes.at[n], code_sem.at[n])
        for n, (_, ref, p) in enumerate(beside_refs)
    ]
    loads = []
    for slot in range(HELD):
        ref, p = (before_ref, 0) if slot == 0 else (raw_ref, slot - 1) if slot <= SLAB else (after_ref, slot - SLAB - 1)
        loads.append(pltpu.make_async_copy(ref.at[p, pl.ds(0, ROWS)], planes.at[slot], sem.at[slot]))
    for load in loads + code_copies:
        load.start()
    for p in range(SLAB):
        offs[p + 1] = offsets[p]
    zeros = jnp.zeros((PAD, COLS), jnp.float32)
    for slot in range(HELD):
        held[slot, 0:PAD, :] = zeros
        held[slot, PAD + ROWS : PAD + ROWS + PAD, :] = zeros
    if late:
        beside, weights, weights_sem = rest
        weights_copy = pltpu.make_async_copy(weights_ref, weights, weights_sem)
        weights_copy.start()
        lane = lax.broadcasted_iota(jnp.int32, (EDGE_ROWS, COLS), 1)
        for e, edges in enumerate((edges_before, edges_own, edges_after)):
            values = edges[...].astype(jnp.float32)
            for g in range(4):
                mine = (lane >= 32 * g) & (lane < 32 * g + 32)
                beside[e, EDGE_ROWS * g : EDGE_ROWS * (g + 1), :] = jnp.where(mine, values, 0.0).astype(jnp.bfloat16)
        weights_copy.wait()
    for slot in range(HELD):
        loads[slot].wait()
        if late:
            e = 0 if slot == 0 else 1 if slot <= SLAB else 2
            values = jnp.concatenate([planes[slot], beside[e]], axis=1)
            held[slot, PAD : PAD + ROWS, :] = dot(values, weights[(slot + SLAB - 1) % SLAB])
        else:
            held[slot, PAD : PAD + ROWS, :] = planes[slot].astype(jnp.float32) * 0.25
    row = lax.broadcasted_iota(jnp.int32, (16, COLS), 0)
    lane = lax.broadcasted_iota(jnp.int32, (16, COLS), 1)
    scale = jnp.where(row == 0, jnp.where(lane == 0, 16.0, jnp.where(lane == 1, 1.0, 0.0)), 0.0)
    for n, (slot, _, _) in enumerate(beside_refs):
        code_copies[n].wait()
        offs[slot] = jnp.sum(codes[n].astype(jnp.float32) * scale).astype(jnp.int32)

    def block_of(i):
        found = jnp.int32(group[0] + 8)
        for at, c in enumerate(group[1:]):
            found = jnp.where(i == at + 1, c + 8, found)
        return found

    share = (2 * lax.broadcasted_iota(jnp.int32, (8, COLS), 0) + 1).astype(jnp.float32) * 0.0625

    def send(i, _):
        b = block_of(i)
        low = b < SENDS // 2
        role = jnp.logical_and(last, low)
        end = jnp.logical_and(last, jnp.logical_not(low))
        keep_15 = jnp.where(role, 0.0, 1.0).astype(jnp.float32)
        keep_16 = jnp.where(end, 0.0, 1.0).astype(jnp.float32)

        def starts(block, none):
            found = []
            for slot in range(HELD):
                dead = jnp.logical_or(none, role if slot <= SLAB else end)
                start = jnp.clip(PAD + HALF_SKEW + block * BLOCK - offs[slot], 0, PAD + ROWS)
                found.append(jnp.where(dead, 0, start))
            return found

        here = starts(b, b == SENDS - 1)
        above = starts(b - 1, b == 0)

        def mixed(r, bases, first, stop):
            x = {p: held[p + 1, pl.ds(bases[p + 1] + 8 * r, 8), :] for p in range(first - 1, stop + 2)}
            v = {p: x[p] + x[p + 1] for p in range(first - 1, stop + 1)}
            u = {}
            for p in range(first, stop + 1):
                u[p] = v[p - 1] + v[p]
                if p == SLAB - 1:
                    u[p] = u[p] * keep_15
                if p == SLAB:
                    u[p] = u[p] * keep_16
            return {p: u[p] + share * (u[p + 1] - u[p]) for p in range(first, stop)}

        def both(r):
            got = dict(mixed(r, here, r, SLAB))
            if r:
                got.update({p + SLAB: v for p, v in mixed(r, above, 0, r).items()})
            got = [got[q + r] for q in range(SLAB)]
            return got

        for t in range(8):
            even, odd = both(2 * t), both(2 * t + 1)
            for q in range(SLAB):
                tile = jnp.concatenate([even[q], odd[q]], axis=0)
                packed[i, q, 16 * t : 16 * t + 16, :] = tile.astype(jnp.bfloat16)
        for at in range(count):

            @pl.when(i == at)
            def _():
                pltpu.make_async_copy(packed.at[at], outs[at], out_sem.at[at]).start()

        return 0

    lax.fori_loop(0, count, send, 0)
    for at in range(count):
        pltpu.make_async_copy(packed.at[at], outs[at], out_sem.at[at]).wait()


PART = jax.ShapeDtypeStruct((SLAB, BLOCK, COLS), jnp.bfloat16)


def shear(group, *operands):
    count = len(group)
    late = group == LATE
    extra = [
        pltpu.VMEM((3, ROWS, COLS), jnp.bfloat16),
        pltpu.VMEM((SLAB, 2 * COLS, COLS), jnp.bfloat16),
        pltpu.SemaphoreType.DMA,
    ]
    return pl.pallas_call(
        functools.partial(shear_kernel, group),
        out_shape=(PART,) * count,
        in_specs=[SMEM, HBM, HBM, HBM] + ([HBM, VMEM, VMEM, VMEM] if late else []),
        out_specs=(HBM,) * count,
        scratch_shapes=[
            pltpu.VMEM((HELD, ROWS, COLS), jnp.bfloat16),
            pltpu.VMEM((HELD, PAD + ROWS + PAD, COLS), jnp.float32),
            pltpu.VMEM((count, SLAB, BLOCK, COLS), jnp.bfloat16),
            pltpu.VMEM((3, 16, COLS), jnp.bfloat16),
            pltpu.SMEM((HELD,), jnp.int32),
            pltpu.SemaphoreType.DMA((HELD,)),
            pltpu.SemaphoreType.DMA((count,)),
            pltpu.SemaphoreType.DMA((3,)),
        ]
        + (extra if late else []),
        compiler_params=pltpu.CompilerParams(vmem_limit_bytes=VMEM_LIMIT),
        cost_estimate=COST,
        name="shear_planes",
    )(*operands)


def pack_parts_kernel(*refs):
    parts, out_ref = refs[:-1], refs[-1]
    pair = lax.shift_right_logical(lax.broadcasted_iota(jnp.int32, (16, COLS), 1), 1)
    for first in range(0, len(parts), 4):
        for t in range(8):
            rows = slice(16 * t, 16 * t + 16)
            total = jnp.zeros((16, COLS), jnp.float32)
            for n, part in enumerate(parts[first : first + 4]):
                for q in range(SLAB):
                    found = pltpu.roll(part[q, rows, :].astype(jnp.float32), (32 * n + 2 * q + 1) % COLS, 1)
                    total = jnp.where(pair == 16 * n + q, found, total)
            out_ref[32 * first + 16 * t : 32 * first + 16 * t + 16, :] = total.astype(jnp.bfloat16)


def pack_parts(*parts):
    return pl.pallas_call(
        pack_parts_kernel,
        out_shape=jax.ShapeDtypeStruct((BLOCK * len(parts) // 4, COLS), jnp.bfloat16),
        in_specs=[VMEM] * len(parts),
        out_specs=VMEM,
        compiler_params=pltpu.CompilerParams(vmem_limit_bytes=VMEM_LIMIT),
        cost_estimate=COST,
        name="pack_parts",
    )(*parts)


def smooth_parts_kernel(from_left, from_right, *refs):
    count = len(refs) // 2
    parts, outs = refs[:count], refs[count:]
    src = lax.broadcasted_iota(jnp.int32, (COLS, COLS), 0)
    dst = lax.broadcasted_iota(jnp.int32, (COLS, COLS), 1)
    tri = jnp.where(src == dst, 0.5, jnp.where(jnp.abs(src - dst) == 1, 0.25, 0.0)).astype(jnp.bfloat16)
    left_lane = (lax.broadcasted_iota(jnp.int32, from_left.shape, 1) & 1) == 0
    edges = jnp.where(left_lane, from_left[...].astype(jnp.float32), from_right[...].astype(jnp.float32)).astype(jnp.bfloat16)
    for n in range(count):
        for q in range(SLAB):
            lane = 32 * (n % 4) + 2 * q
            hit = ((src == lane) & (dst == 0)) | ((src == lane + 1) & (dst == COLS - 1))
            weights = jnp.concatenate([tri, jnp.where(hit, 0.25, 0.0).astype(jnp.bfloat16)], axis=0)
            values = jnp.concatenate([parts[n][q], edges[BLOCK * (n // 4) : BLOCK * (n // 4 + 1)]], axis=1)
            outs[n][q] = dot(values, weights).astype(jnp.bfloat16)


def smooth_parts(from_left, from_right, *parts):
    return pl.pallas_call(
        smooth_parts_kernel,
        out_shape=(jax.ShapeDtypeStruct((SLAB, BLOCK, COLS), jnp.bfloat16),) * len(parts),
        in_specs=[VMEM] * (2 + len(parts)),
        out_specs=(VMEM,) * len(parts),
        compiler_params=pltpu.CompilerParams(vmem_limit_bytes=VMEM_LIMIT),
        cost_estimate=COST,
        name="smooth_parts",
    )(from_left, from_right, *parts)


def merge(got, full, at, blocks, top):
    upper = lax.broadcasted_iota(jnp.int32, (16, COLS), 0) < 8

    def one(b, _):
        for q in range(SLAB):
            for t in range(8):
                rows = slice(16 * t, 16 * t + 16)
                if q + 2 * t + 1 < SLAB:
                    tile = got[at + b, q, rows, :].astype(jnp.float32)
                elif q + 2 * t >= SLAB:
                    tile = got[at + b + 1, q, rows, :].astype(jnp.float32)
                else:
                    ours = got[at + b, q, rows, :].astype(jnp.float32)
                    tile = jnp.where(upper, ours, got[at + b + 1, q, rows, :].astype(jnp.float32))
                full[q, pl.ds(pl.multiple_of(top + b * BLOCK + 16 * t, 16), 16), :] = tile
        return 0

    lax.fori_loop(0, blocks, one, 0)


def shift_of(q):
    numerator = 17 * (2 * (lax.axis_index("scan") * SLAB + q) - (SLAB * SCANS - 1))
    whole = lax.shift_right_arithmetic(numerator, 6)
    share = (numerator & 63).astype(jnp.float32) * (1.0 / 64.0)
    tile = -lax.shift_right_arithmetic(whole, 4)
    return whole, share, tile


def interpolate(full, done, q, source, target, tiles, share):
    for t in range(tiles):
        a = full[q, pl.ds(source + 16 * t, 16), :]
        c = full[q, pl.ds(source + 1 + 16 * t, 16), :]
        done[q, pl.ds(pl.multiple_of(target + 16 * t, 16), 16), :] = (a + share * (c - a)).astype(jnp.bfloat16)


INNER = (STOP - FIRST) * BLOCK - 16
OUTER = 272
LOW = FIRST * BLOCK
HIGH = LOW + INNER


def inner_kernel(*refs):
    count = STOP - FIRST + 1
    parts = refs[:count]
    out_ref, got, full, done, sem, out_sem = refs[count:]

    def fetch(i):
        return pltpu.make_async_copy(parts[i], got.at[i], sem.at[i])

    for i in range(count):
        fetch(i).start()
    for i in range(count):
        fetch(i).wait()
    merge(got, full, 0, STOP - FIRST, 0)

    def put(q, tile):
        return pltpu.make_async_copy(done.at[q], out_ref.at[q, pl.ds(pl.multiple_of(LOW + 16 * tile, 16), INNER)], out_sem.at[q])

    def plane(q, _):
        whole, share, tile = shift_of(q)
        interpolate(full, done, q, 16 * tile + whole, 0, INNER // 16, share)
        put(q, tile).start()
        return 0

    lax.fori_loop(0, SLAB, plane, 0)
    for q in range(SLAB):
        put(q, shift_of(q)[2]).wait()


def outer_kernel(*refs):
    top, bottom = FIRST + 2, SENDS - STOP + 1
    count = top + bottom
    parts = refs[:count]
    _, out_ref, got, full, done, sem, out_sem = refs[count:]

    def fetch(i):
        return pltpu.make_async_copy(parts[i], got.at[i], sem.at[i])

    for i in range(count):
        fetch(i).start()
    zeros = jnp.zeros((MARGIN, COLS), jnp.float32)
    low_rows, high_rows = (top - 1) * BLOCK, (bottom - 1) * BLOCK
    base = MARGIN + low_rows
    first_row = ROWS - high_rows

    def clear(q, _):
        full[q, 0:MARGIN, :] = zeros
        full[q, base + high_rows : base + high_rows + MARGIN, :] = zeros
        return 0

    lax.fori_loop(0, SLAB, clear, 0)
    for i in range(count):
        fetch(i).wait()
    merge(got, full, 0, top - 1, MARGIN)
    merge(got, full, top, bottom - 1, base)

    def targets(tile):
        low = jnp.maximum(LOW + 16 * tile - OUTER, 0)
        high = jnp.minimum(HIGH + 16 * tile, ROWS - OUTER)
        return 0, low, high, ROWS - OUTER

    def puts(q, tile):
        return [
            pltpu.make_async_copy(
                done.at[q, pl.ds(OUTER * n, OUTER)], out_ref.at[q, pl.ds(pl.multiple_of(row, 16), OUTER)], out_sem.at[q, n]
            )
            for n, row in enumerate(targets(tile))
        ]

    def plane(q, _):
        whole, share, tile = shift_of(q)
        for n, row in enumerate(targets(tile)):
            source = row + whole + (MARGIN if n < 2 else base - first_row)
            interpolate(full, done, q, source, OUTER * n, OUTER // 16, share)
        for put in puts(q, tile)[::3]:
            put.start()

        @pl.when(q >= 2)
        def _():
            inward(q - 2)

        return 0

    def inward(q):
        first, low, high, final = puts(q, shift_of(q)[2])
        first.wait()
        final.wait()
        low.start()
        high.start()

    lax.fori_loop(0, SLAB, plane, 0)
    for q in range(SLAB - 2, SLAB):
        inward(q)
    for q in range(SLAB):
        for put in puts(q, shift_of(q)[2])[1:3]:
            put.wait()


def row_shear(kernel, parts, rows, full_rows, puts, into=None):
    count = len(parts)
    operands = list(parts) + ([] if into is None else [into])
    return pl.pallas_call(
        kernel,
        out_shape=jax.ShapeDtypeStruct((SLAB, ROWS, COLS), jnp.bfloat16),
        in_specs=[HBM] * len(operands),
        out_specs=HBM,
        scratch_shapes=[
            pltpu.VMEM((count, SLAB, BLOCK, COLS), jnp.bfloat16),
            pltpu.VMEM((SLAB, full_rows, COLS), jnp.float32),
            pltpu.VMEM((SLAB, rows, COLS), jnp.bfloat16),
            pltpu.SemaphoreType.DMA((count,)),
            pltpu.SemaphoreType.DMA((SLAB,) + puts),
        ],
        input_output_aliases={} if into is None else {count: 0},
        compiler_params=pltpu.CompilerParams(vmem_limit_bytes=VMEM_LIMIT),
        cost_estimate=COST,
        name="shear_rows",
    )(*operands)


def pairs_of(c):
    found = [(s, s - c) for s in range(SCANS) if 0 <= s - c < SCANS]
    if c < 0:
        found.append((SCANS - 1, -c - 1))
    return found


def local(raw, offsets):
    up = [(i, i + 1) for i in range(SCANS - 1)]
    down = [((i + 1) % SCANS, i) for i in range(SCANS)]
    right = [(i, i + 1) for i in range(3)]
    left = [(i + 1, i) for i in range(3)]
    first, final = halos(offsets, raw)
    after = lax.ppermute(first, "scan", down)
    before = lax.ppermute(final, "scan", up)
    own = pack_edges(raw)
    from_left = lax.ppermute(own, "col", right)
    from_right = lax.ppermute(own, "col", left)
    raw, _ = lax.optimization_barrier((raw, own))
    made = shear(EARLY, offsets, raw, before, after)
    moved = {c: lax.ppermute(part, "scan", pairs_of(c)) for c, part in zip(EARLY, made)}
    lane = lax.broadcasted_iota(jnp.int32, own.shape, 1)
    edges = jnp.where(lane % 32 < 16, from_left, from_right)
    edges, _ = lax.optimization_barrier((edges, made[0]))
    edges_after = lax.ppermute(edges, "scan", down)
    edges_before = lax.ppermute(edges, "scan", up)
    made = shear(LATE, offsets, raw, before, after, column_weights(), edges_before, edges, edges_after)
    parts = dict(zip(LATE, made))
    for c in ORDER[len(EARLY) :]:
        moved[c] = lax.ppermute(parts[c], "scan", pairs_of(c))
    arrived = [moved[c] for c in EARLY]
    own = pack_parts(*arrived)
    arrived = smooth_parts(lax.ppermute(own, "col", right), lax.ppermute(own, "col", left), *arrived)
    moved.update(zip(EARLY, arrived))
    moved[0] = parts[0]
    ready = [moved[b - 8] for b in range(FIRST, STOP + 1)]
    result = row_shear(inner_kernel, ready, INNER, (STOP - FIRST) * BLOCK, ())
    rest = [moved[b - 8] for b in list(range(FIRST + 2)) + list(range(STOP - 1, SENDS))]
    full_rows = (FIRST + 1 + SENDS - STOP) * BLOCK + 2 * MARGIN
    return row_shear(outer_kernel, rest, 4 * OUTER, full_rows, (4,), result)


def solution(mesh):
    placed = (P("scan", None, "col"), P("scan"))
    return jax.shard_map(local, mesh=mesh, in_specs=placed, out_specs=P("scan", None, "col"), check_vma=False)
```

time: 176 us -> 167 us (0.949)
  the two profiles are of different devices: /device:TPU:39 before, /device:TPU:62 now
where the time goes in v2:
time: 167 us; the launch traced here: 166 us
  starting transfers between devices  74.8 us (45%)
  Pallas kernels  63.5 us (38%)
  waiting for transfers between devices  23.4 us (14%)
  local copies, waits for them, and re-layouts  3.63 us (2%)
    ppermute x8, starting transfers between devices, local(): moved[c] = lax.ppermute(parts[c], 'scan', pairs_of(c))  32.7 us
    pallas_call x2, Pallas kernels, shear(): pl.pallas_call(functools.partial(shear_kernel, group), out_shape=(PART,)...  29.9 us
    ppermute x8, starting transfers between devices, local(): lax.ppermute(part, 'scan', pairs_of(c))  27.4 us
    ppermute x8, waiting for transfers between devices, local(): moved[c] = lax.ppermute(parts[c], 'scan', pairs_of(c))  17.1 us
    pallas_call x2, Pallas kernels, row_shear(): pl.pallas_call(kernel, out_shape=jax.ShapeDtypeStruct((SLAB, ROWS, COLS),...  14.6 us
    pallas_call x1, Pallas kernels, pack_edges(): pl.pallas_call(pack_edges_kernel, out_shape=jax.ShapeDtypeStruct((EDGE_RO...  6.82 us
    pallas_call x1, Pallas kernels, smooth_parts(): pl.pallas_call(smooth_parts_kernel, out_shape=(jax.ShapeDtypeStruct((SLAB...  5.35 us
    ppermute x1, waiting for transfers between devices, local(): edges_after = lax.ppermute(edges, 'scan', down)  5.34 us
  transfers between devices with their start and end apart: 24, of which 4 were waited for; matrix products, arithmetic and copies ran while one was open for 0% of the time, Pallas kernels for 31%

profile of v2, /device:TPU:62, one launch (start us, length us, event | category | flops | bytes accessed | tf_op | source)
XLA Modules:
  0.0 166.1 jit_solution(3276413282315511388)
XLA Ops:
  0.0 2.9 %halos.1 = (bf16[2,2064,128]{2,1,0:T(8,128)(2,1)}, bf16[1,2064,128]{2,1,0:T(8,128)(2,1)}) custom-call(s32[16]{0:T(128)} %offsets.5, bf16[16,2048,128]{2,1,0:T(8,128)(2,1)} %raw_ref.5), custom_call_target="tpu_custom_call" | custom-call | flops 1000 | bytes 1000 | tf_op jit(solution)/shard_map/halos/pallas_call | solution.py:61
  2.9 0.3 collective-permute-start.1
  3.2 2.2 %collective-permute-start = (bf16[1,2064,128]{2,1,0:T(8,128)(2,1)}, bf16[1,2064,128]{2,1,0:T(8,128)(2,1)S(1)}, u32[]{:S(2)}, u32[]{:S(2)}) collective-permute-start(bf16[1,2064,128]{2,1,0:T(8,128)(2,1)} %get-tuple-element.35), channel_id=1, source_target_pairs={{0,4},{4,8},{8,12},{12,16},{16,20},{20,24},{24,28},{28,32},{32,36}... | collective-permute-start | bytes 1585160 | tf_op jit(solution)/shard_map/ppermute | solution.py:500
  5.4 6.8 %pack_edges.1 = bf16[512,128]{1,0:T(8,128)(2,1)} custom-call(bf16[16,2048,128]{2,1,0:T(8,128)(2,1)} %raw_ref.5), custom_call_target="tpu_custom_call" | custom-call | flops 1000 | bytes 1000 | tf_op jit(solution)/shard_map/pack_edges/pallas_call | solution.py:94
  12.2 2.7 %collective-permute-start.13 = (bf16[512,128]{1,0:T(8,128)(2,1)}, bf16[512,128]{1,0:T(8,128)(2,1)S(1)}, u32[]{:S(2)}, u32[]{:S(2)}) collective-permute-start(bf16[512,128]{1,0:T(8,128)(2,1)} %pack_edges.1), channel_id=1, source_target_pairs={{1,0},{2,1},{3,2},{5,4},{6,5},{7,6},{9,8},{10,9},{11,10},{13,12},{... | collective-permute-start | bytes 393224 | tf_op jit(solution)/shard_map/ppermute | solution.py:503
  15.0 1.3 collective-permute-start.12
  16.3 0.0 collective-permute-done.1.after_ref
  16.3 0.8 copy-done.1
  17.1 1.0 copy-done
  18.1 8.0 %shear_planes.2 = (bf16[16,128,128]{2,1,0:T(8,128)(2,1)}, bf16[16,128,128]{2,1,0:T(8,128)(2,1)}, bf16[16,128,128]{2,1,0:T(8,128)(2,1)}, bf16[16,128,128]{2,1,0:T...) custom-call(s32[16]{0:T(128)} %offsets.5, ...), custom_call_target="tpu_custom_call" | custom-call | flops 1000 | bytes 1000 | tf_op jit(solution)/shard_map/shear_planes/pallas_call | solution.py:249
  26.1 4.5 %collective-permute-start.3 = (bf16[16,128,128]{2,1,0:T(8,128)(2,1)}, bf16[16,128,128]{2,1,0:T(8,128)(2,1)S(1)}, u32[]{:S(2)}, u32[]{:S(2)}) collective-permute-start(bf16[16,128,128]{2,1,0:T(8,128)(2,1)} %get-tuple-element.38), channel_id=1, source_target_pairs={{0,16},{4,20},{8,24},{12,28},{16,32},{20,36},{24,40},{28,44},{32,4... | collective-permute-start | bytes 1572872 | tf_op jit(solution)/shard_map/ppermute | solution.py:506
  30.7 0.0 collective-permute-done.13
  30.7 0.2 collective-permute-start.15
  30.9 2.5 %collective-permute-start.14 = (bf16[512,128]{1,0:T(8,128)(2,1)S(1)}, bf16[512,128]{1,0:T(8,128)(2,1)S(1)}, u32[]{:S(2)}, u32[]{:S(2)}) collective-permute-start(bf16[512,128]{1,0:T(8,128)(2,1)S(1)} %fusion.rest_2_), channel_id=1, source_target_pairs={{0,4},{4,8},{8,12},{12,16},{16,20},{20,24},{24,28},{28,32},{32,36}... | collective-permute-start | bytes 393224 | tf_op jit(solution)/shard_map/ppermute | solution.py:511
  33.4 2.0 %collective-permute-start.4 = (bf16[16,128,128]{2,1,0:T(8,128)(2,1)}, bf16[16,128,128]{2,1,0:T(8,128)(2,1)S(1)}, u32[]{:S(2)}, u32[]{:S(2)}) collective-permute-start(bf16[16,128,128]{2,1,0:T(8,128)(2,1)} %get-tuple-element.39), channel_id=1, source_target_pairs={{32,0},{36,4},{40,8},{44,12},{48,16},{52,20},{56,24},{60,28},{64,3... | collective-permute-start | bytes 1572872 | tf_op jit(solution)/shard_map/ppermute | solution.py:506
  35.4 3.8 %collective-permute-start.5 = (bf16[16,128,128]{2,1,0:T(8,128)(2,1)}, bf16[16,128,128]{2,1,0:T(8,128)(2,1)S(1)}, u32[]{:S(2)}, u32[]{:S(2)}) collective-permute-start(bf16[16,128,128]{2,1,0:T(8,128)(2,1)} %get-tuple-element.40), channel_id=1, source_target_pairs={{0,32},{4,36},{8,40},{12,44},{16,48},{20,52},{24,56},{28,60},{32,6... | collective-permute-start | bytes 1572872 | tf_op jit(solution)/shard_map/ppermute | solution.py:506
  39.2 5.3 %collective-permute-done.15.rest_3_ = bf16[512,128]{1,0:T(8,128)(2,1)S(1)} collective-permute-done((bf16[512,128]{1,0:T(8,128)(2,1)S(1)}, bf16[512,128]{1,0:T(8,128)(2,1)S(1)}, u32[]{:S(2)}, u32[]{:S(2)}) %collective-permute-start.15) | collective-permute-done | bytes 131104 | tf_op jit(solution)/shard_map/ppermute | solution.py:510
  44.6 5.5 %collective-permute-start.6 = (bf16[16,128,128]{2,1,0:T(8,128)(2,1)}, bf16[16,128,128]{2,1,0:T(8,128)(2,1)S(1)}, u32[]{:S(2)}, u32[]{:S(2)}) collective-permute-start(bf16[16,128,128]{2,1,0:T(8,128)(2,1)} %get-tuple-element.41), channel_id=1, source_target_pairs={{12,0},{16,4},{20,8},{24,12},{28,16},{32,20},{36,24},{40,28},{44,3... | collective-permute-start | bytes 1572872 | tf_op jit(solution)/shard_map/ppermute | solution.py:506
  50.1 0.0 collective-permute-done.14.rest_1_
  50.1 2.1 %collective-permute-start.7 = (bf16[16,128,128]{2,1,0:T(8,128)(2,1)}, bf16[16,128,128]{2,1,0:T(8,128)(2,1)S(1)}, u32[]{:S(2)}, u32[]{:S(2)}) collective-permute-start(bf16[16,128,128]{2,1,0:T(8,128)(2,1)} %get-tuple-element.42), channel_id=1, source_target_pairs={{0,12},{4,16},{8,20},{12,24},{16,28},{20,32},{24,36},{28,40},{32,4... | collective-permute-start | bytes 1572872 | tf_op jit(solution)/shard_map/ppermute | solution.py:506
  52.3 0.0 collective-permute-done.3.refs_1_
  52.3 3.8 %collective-permute-start.8 = (bf16[16,128,128]{2,1,0:T(8,128)(2,1)}, bf16[16,128,128]{2,1,0:T(8,128)(2,1)}, u32[]{:S(2)}, u32[]{:S(2)}) collective-permute-start(bf16[16,128,128]{2,1,0:T(8,128)(2,1)} %get-tuple-element.43), channel_id=1, source_target_pairs={{28,0},{32,4},{36,8},{40,12},{44,16},{48,20},{52,24},{56,28},{60,3... | collective-permute-start | bytes 1572872 | tf_op jit(solution)/shard_map/ppermute | solution.py:506
  56.1 0.0 collective-permute-done.4.refs_2_
  56.1 3.5 %collective-permute-start.9 = (bf16[16,128,128]{2,1,0:T(8,128)(2,1)}, bf16[16,128,128]{2,1,0:T(8,128)(2,1)}, u32[]{:S(2)}, u32[]{:S(2)}) collective-permute-start(bf16[16,128,128]{2,1,0:T(8,128)(2,1)} %get-tuple-element.44), channel_id=1, source_target_pairs={{0,28},{4,32},{8,36},{12,40},{16,44},{20,48},{24,52},{28,56},{32,6... | collective-permute-start | bytes 1572872 | tf_op jit(solution)/shard_map/ppermute | solution.py:506
  59.7 0.0 collective-permute-done.5.refs_3_
  59.7 2.1 %collective-permute-start.2 = (bf16[16,128,128]{2,1,0:T(8,128)(2,1)}, bf16[16,128,128]{2,1,0:T(8,128)(2,1)}, u32[]{:S(2)}, u32[]{:S(2)}) collective-permute-start(bf16[16,128,128]{2,1,0:T(8,128)(2,1)} %get-tuple-element.37), channel_id=1, source_target_pairs={{16,0},{20,4},{24,8},{28,12},{32,16},{36,20},{40,24},{44,28},{48,3... | collective-permute-start | bytes 1572872 | tf_op jit(solution)/shard_map/ppermute | solution.py:506
  61.8 21.9 %shear_planes.3 = (bf16[16,128,128]{2,1,0:T(8,128)(2,1)}, bf16[16,128,128]{2,1,0:T(8,128)(2,1)}, bf16[16,128,128]{2,1,0:T(8,128)(2,1)}, bf16[16,128,128]{2,1,0:T...) custom-call(s32[16]{0:T(128)} %offsets.5, ...), custom_call_target="tpu_custom_call" | custom-call | flops 1000 | bytes 1000 | tf_op jit(solution)/shard_map/shear_planes/pallas_call | solution.py:249
  83.7 0.0 copy-start.7
  83.7 6.1 %collective-permute-start.17 = (bf16[16,128,128]{2,1,0:T(8,128)(2,1)}, bf16[16,128,128]{2,1,0:T(8,128)(2,1)S(1)}, u32[]{:S(2)}, u32[]{:S(2)}) collective-permute-start(bf16[16,128,128]{2,1,0:T(8,128)(2,1)} %get-tuple-element.49), channel_id=1, source_target_pairs={{0,20},{4,24},{8,28},{12,32},{16,36},{20,40},{24,44},{28,48},{32,5... | collective-permute-start | bytes 1572872 | tf_op jit(solution)/shard_map/ppermute | solution.py:515
  89.9 1.9 %collective-permute-start.18 = (bf16[16,128,128]{2,1,0:T(8,128)(2,1)}, bf16[16,128,128]{2,1,0:T(8,128)(2,1)S(1)}, u32[]{:S(2)}, u32[]{:S(2)}) collective-permute-start(bf16[16,128,128]{2,1,0:T(8,128)(2,1)} %get-tuple-element.52), channel_id=1, source_target_pairs={{20,0},{24,4},{28,8},{32,12},{36,16},{40,20},{44,24},{48,28},{52,3... | collective-permute-start | bytes 1572872 | tf_op jit(solution)/shard_map/ppermute | solution.py:515
  91.8 4.4 %collective-permute-start.20 = (bf16[16,128,128]{2,1,0:T(8,128)(2,1)}, bf16[16,128,128]{2,1,0:T(8,128)(2,1)}, u32[]{:S(2)}, u32[]{:S(2)}) collective-permute-start(bf16[16,128,128]{2,1,0:T(8,128)(2,1)} %get-tuple-element.57), channel_id=1, source_target_pairs={{0,8},{4,12},{8,16},{12,20},{16,24},{20,28},{24,32},{28,36},{32,40... | collective-permute-start | bytes 1572872 | tf_op jit(solution)/shard_map/ppermute | solution.py:515
  96.3 3.9 %pack_parts.1 = bf16[256,128]{1,0:T(8,128)(2,1)} custom-call(bf16[16,128,128]{2,1,0:T(8,128)(2,1)} %collective-permute-done.2.refs_0_, bf16[16,128,128]{2,1,0:T(8,128)(2,1)} %copy-done.4, bf16[16,128,128]{2,1,0:T(8,128)(2,1)} %copy-done.5, bf16[16,128,128]{2,1,0:T(8,128)(2,1)} %copy-done.6, bf16[16,128,128]{2,1,0:T(8,128)(2,1)} %copy-done.7, ...), custom_call_target="tpu_custom_call" | custom-call | flops 1000 | bytes 1000 | tf_op jit(solution)/shard_map/pack_parts/pallas_call | solution.py:286
  100.2 4.3 %collective-permute-start.11 = (bf16[256,128]{1,0:T(8,128)(2,1)}, bf16[256,128]{1,0:T(8,128)(2,1)S(1)}, u32[]{:S(2)}, u32[]{:S(2)}) collective-permute-start(bf16[256,128]{1,0:T(8,128)(2,1)} %pack_parts.1), channel_id=1, source_target_pairs={{1,0},{2,1},{3,2},{5,4},{6,5},{7,6},{9,8},{10,9},{11,10},{13,12},{... | collective-permute-start | bytes 196616 | tf_op jit(solution)/shard_map/ppermute | solution.py:518
  104.5 1.3 collective-permute-start.10
  105.8 0.9 collective-permute-done.11.from_right
  106.7 7.1 %collective-permute-start.21 = (bf16[16,128,128]{2,1,0:T(8,128)(2,1)}, bf16[16,128,128]{2,1,0:T(8,128)(2,1)S(1)}, u32[]{:S(2)}, u32[]{:S(2)}) collective-permute-start(bf16[16,128,128]{2,1,0:T(8,128)(2,1)} %get-tuple-element.58), channel_id=1, source_target_pairs={{0,4},{4,8},{8,12},{12,16},{16,20},{20,24},{24,28},{28,32},{32,36}... | collective-permute-start | bytes 1572872 | tf_op jit(solution)/shard_map/ppermute | solution.py:515
  113.8 2.1 %collective-permute-start.22 = (bf16[16,128,128]{2,1,0:T(8,128)(2,1)}, bf16[16,128,128]{2,1,0:T(8,128)(2,1)S(1)}, u32[]{:S(2)}, u32[]{:S(2)}) collective-permute-start(bf16[16,128,128]{2,1,0:T(8,128)(2,1)} %get-tuple-element.60), channel_id=1, source_target_pairs={{4,0},{8,4},{12,8},{16,12},{20,16},{24,20},{28,24},{32,28},{36,32}... | collective-permute-start | bytes 1572872 | tf_op jit(solution)/shard_map/ppermute | solution.py:515
  115.9 5.7 %collective-permute-start.23 = (bf16[16,128,128]{2,1,0:T(8,128)(2,1)}, bf16[16,128,128]{2,1,0:T(8,128)(2,1)S(1)}, u32[]{:S(2)}, u32[]{:S(2)}) collective-permute-start(bf16[16,128,128]{2,1,0:T(8,128)(2,1)} %get-tuple-element.61), channel_id=1, source_target_pairs={{8,0},{12,4},{16,8},{20,12},{24,16},{28,20},{32,24},{36,28},{40,32... | collective-permute-start | bytes 1572872 | tf_op jit(solution)/shard_map/ppermute | solution.py:515
  121.6 3.2 %collective-permute-start.16 = (bf16[16,128,128]{2,1,0:T(8,128)(2,1)}, bf16[16,128,128]{2,1,0:T(8,128)(2,1)S(1)}, u32[]{:S(2)}, u32[]{:S(2)}) collective-permute-start(bf16[16,128,128]{2,1,0:T(8,128)(2,1)} %get-tuple-element.48), channel_id=1, source_target_pairs={{0,24},{4,28},{8,32},{12,36},{16,40},{20,44},{24,48},{28,52},{32,5... | collective-permute-start | bytes 1572872 | tf_op jit(solution)/shard_map/ppermute | solution.py:515
  124.8 9.4 %collective-permute-done.20.refs_3_ = bf16[16,128,128]{2,1,0:T(8,128)(2,1)} collective-permute-done((bf16[16,128,128]{2,1,0:T(8,128)(2,1)}, bf16[16,128,128]{2,1,0:T(8,128)(2,1)}, u32[]{:S(2)}, u32[]{:S(2)}) %collective-permute-start.20) | collective-permute-done | bytes 524320 | tf_op jit(solution)/shard_map/ppermute | solution.py:515
  134.2 2.1 %collective-permute-start.19 = (bf16[16,128,128]{2,1,0:T(8,128)(2,1)}, bf16[16,128,128]{2,1,0:T(8,128)(2,1)S(1)}, u32[]{:S(2)}, u32[]{:S(2)}) collective-permute-start(bf16[16,128,128]{2,1,0:T(8,128)(2,1)} %get-tuple-element.53), channel_id=1, source_target_pairs={{24,0},{28,4},{32,8},{36,12},{40,16},{44,20},{48,24},{52,28},{56,3... | collective-permute-start | bytes 1572872 | tf_op jit(solution)/shard_map/ppermute | solution.py:515
  136.4 5.3 %smooth_parts.1 = (bf16[16,128,128]{2,1,0:T(8,128)(2,1)}, bf16[16,128,128]{2,1,0:T(8,128)(2,1)}, bf16[16,128,128]{2,1,0:T(8,128)(2,1)}, bf16[16,128,128]{2,1,0:T...) custom-call(bf16[256,128]{1,0:T(8,128)(2,1)} %copy-done.18, ...), custom_call_target="tpu_custom_call" | custom-call | flops 1000 | bytes 1000 | tf_op jit(solution)/shard_map/smooth_parts/pallas_call | solution.py:315
  141.8 7.7 %collective-permute-done.23.refs_7_ = bf16[16,128,128]{2,1,0:T(8,128)(2,1)S(1)} collective-permute-done((bf16[16,128,128]{2,1,0:T(8,128)(2,1)}, bf16[16,128,128]{2,1,0:T(8,128)(2,1)S(1)}, u32[]{:S(2)}, u32[]{:S(2)}) %collective-permute-start.23) | collective-permute-done | bytes 524320 | tf_op jit(solution)/shard_map/ppermute | solution.py:515
  149.5 0.8 copy-done.11
  150.3 5.9 %shear_rows.2.refs_10_ = bf16[16,2048,128]{2,1,0:T(8,128)(2,1)} custom-call(bf16[16,128,128]{2,1,0:T(8,128)(2,1)} %copy-done.2, bf16[16,128,128]{2,1,0:T(8,128)(2,1)} %get-tuple-element.50.refs_1_.refs_4_, bf16[16,128,128]{2,1,0:T(8,128)(2,1)} %get-tuple-element.56.refs_2_, bf16[16,128,128]{2,1,0:T(8,128)(2,1)} %collective-permute-done.20.refs_3_, ...), custom_call_target="tpu_custom_call" | custom-call | flops 1000 | bytes 1000 | tf_op jit(solution)/shard_map/shear_rows/pallas_call | solution.py:467
  156.3 0.8 copy-done.13
  157.1 0.2 copy-done.14
  157.3 8.7 %shear_rows.3 = bf16[16,2048,128]{2,1,0:T(8,128)(2,1)} custom-call(bf16[16,128,128]{2,1,0:T(8,128)(2,1)} %get-tuple-element.45.refs_0_, bf16[16,128,128]{2,1,0:T(8,128)(2,1)} %get-tuple-element.46.refs_1_, bf16[16,128,128]{2,1,0:T(8,128)(2,1)} %copy-done.13, bf16[16,128,128]{2,1,0:T(8,128)(2,1)} %copy-done.2, ...), custom_call_target="tpu_custom_call", output_to_operand_aliasing={{}: (10, {})} | custom-call | flops 1000 | bytes 1000 | tf_op jit(solution)/shard_map/shear_rows/pallas_call | solution.py:467
  (49 shorter events, 0.1 us)
Async XLA Ops:
  2.9 13.4 %collective-permute-start.1 = (bf16[2,2064,128]{2,1,0:T(8,128)(2,1)}, bf16[2,2064,128]{2,1,0:T(8,128)(2,1)S(1)}, u32[]{:S(2)}, u32[]{:S(2)}) collective-permute-start(bf16[2,2064,128]{2,1,0:T(8,128)(2,1)} %get-tuple-element.36), channel_id=1, source_target_pairs={{4,0},{8,4},{12,8},{16,12},{20,16},{24,20},{28,24},{32,28},{36,32}... | collective-permute-start | bytes 3170312 | tf_op jit(solution)/shard_map/ppermute | solution.py:499
  3.2 13.1 %collective-permute-start = (bf16[1,2064,128]{2,1,0:T(8,128)(2,1)}, bf16[1,2064,128]{2,1,0:T(8,128)(2,1)S(1)}, u32[]{:S(2)}, u32[]{:S(2)}) collective-permute-start(bf16[1,2064,128]{2,1,0:T(8,128)(2,1)} %get-tuple-element.35), channel_id=1, source_target_pairs={{0,4},{4,8},{8,12},{12,16},{16,20},{20,24},{24,28},{28,32},{32,36}... | collective-permute-start | bytes 1585160 | tf_op jit(solution)/shard_map/ppermute | solution.py:500
  12.2 18.4 %collective-permute-start.13 = (bf16[512,128]{1,0:T(8,128)(2,1)}, bf16[512,128]{1,0:T(8,128)(2,1)S(1)}, u32[]{:S(2)}, u32[]{:S(2)}) collective-permute-start(bf16[512,128]{1,0:T(8,128)(2,1)} %pack_edges.1), channel_id=1, source_target_pairs={{1,0},{2,1},{3,2},{5,4},{6,5},{7,6},{9,8},{10,9},{11,10},{13,12},{... | collective-permute-start | bytes 393224 | tf_op jit(solution)/shard_map/ppermute | solution.py:503
  15.0 15.7 %collective-permute-start.12 = (bf16[512,128]{1,0:T(8,128)(2,1)}, bf16[512,128]{1,0:T(8,128)(2,1)S(1)}, u32[]{:S(2)}, u32[]{:S(2)}) collective-permute-start(bf16[512,128]{1,0:T(8,128)(2,1)} %pack_edges.1), channel_id=1, source_target_pairs={{0,1},{1,2},{2,3},{4,5},{5,6},{6,7},{8,9},{9,10},{10,11},{12,13},{... | collective-permute-start | bytes 393224 | tf_op jit(solution)/shard_map/ppermute | solution.py:502
  16.3 0.8 copy-start.1
  17.1 1.0 copy-start
  26.1 26.1 %collective-permute-start.3 = (bf16[16,128,128]{2,1,0:T(8,128)(2,1)}, bf16[16,128,128]{2,1,0:T(8,128)(2,1)S(1)}, u32[]{:S(2)}, u32[]{:S(2)}) collective-permute-start(bf16[16,128,128]{2,1,0:T(8,128)(2,1)} %get-tuple-element.38), channel_id=1, source_target_pairs={{0,16},{4,20},{8,24},{12,28},{16,32},{20,36},{24,40},{28,44},{32,4... | collective-permute-start | bytes 1572872 | tf_op jit(solution)/shard_map/ppermute | solution.py:506
  30.7 31.1 %copy-start.12 = (bf16[512,128]{1,0:T(8,128)(2,1)}, bf16[512,128]{1,0:T(8,128)(2,1)S(1)}, u32[]{:S(2)}) copy-start(bf16[512,128]{1,0:T(8,128)(2,1)S(1)} %fusion.rest_2_) | copy-start | bytes 393220
  30.7 13.8 %collective-permute-start.15 = (bf16[512,128]{1,0:T(8,128)(2,1)S(1)}, bf16[512,128]{1,0:T(8,128)(2,1)S(1)}, u32[]{:S(2)}, u32[]{:S(2)}) collective-permute-start(bf16[512,128]{1,0:T(8,128)(2,1)S(1)} %fusion.rest_2_), channel_id=1, source_target_pairs={{4,0},{8,4},{12,8},{16,12},{20,16},{24,20},{28,24},{32,28},{36,32}... | collective-permute-start | bytes 393224 | tf_op jit(solution)/shard_map/ppermute | solution.py:510
  30.9 19.2 %collective-permute-start.14 = (bf16[512,128]{1,0:T(8,128)(2,1)S(1)}, bf16[512,128]{1,0:T(8,128)(2,1)S(1)}, u32[]{:S(2)}, u32[]{:S(2)}) collective-permute-start(bf16[512,128]{1,0:T(8,128)(2,1)S(1)} %fusion.rest_2_), channel_id=1, source_target_pairs={{0,4},{4,8},{8,12},{12,16},{16,20},{20,24},{24,28},{28,32},{32,36}... | collective-permute-start | bytes 393224 | tf_op jit(solution)/shard_map/ppermute | solution.py:511
  33.4 22.8 %collective-permute-start.4 = (bf16[16,128,128]{2,1,0:T(8,128)(2,1)}, bf16[16,128,128]{2,1,0:T(8,128)(2,1)S(1)}, u32[]{:S(2)}, u32[]{:S(2)}) collective-permute-start(bf16[16,128,128]{2,1,0:T(8,128)(2,1)} %get-tuple-element.39), channel_id=1, source_target_pairs={{32,0},{36,4},{40,8},{44,12},{48,16},{52,20},{56,24},{60,28},{64,3... | collective-permute-start | bytes 1572872 | tf_op jit(solution)/shard_map/ppermute | solution.py:506
  35.4 24.3 %collective-permute-start.5 = (bf16[16,128,128]{2,1,0:T(8,128)(2,1)}, bf16[16,128,128]{2,1,0:T(8,128)(2,1)S(1)}, u32[]{:S(2)}, u32[]{:S(2)}) collective-permute-start(bf16[16,128,128]{2,1,0:T(8,128)(2,1)} %get-tuple-element.40), channel_id=1, source_target_pairs={{0,32},{4,36},{8,40},{12,44},{16,48},{20,52},{24,56},{28,60},{32,6... | collective-permute-start | bytes 1572872 | tf_op jit(solution)/shard_map/ppermute | solution.py:506
  44.6 17.2 %copy-start.15 = (bf16[512,128]{1,0:T(8,128)(2,1)}, bf16[512,128]{1,0:T(8,128)(2,1)S(1)}, u32[]{:S(2)}) copy-start(bf16[512,128]{1,0:T(8,128)(2,1)S(1)} %collective-permute-done.15.rest_3_) | copy-start | bytes 393220
  44.6 39.2 %collective-permute-start.6 = (bf16[16,128,128]{2,1,0:T(8,128)(2,1)}, bf16[16,128,128]{2,1,0:T(8,128)(2,1)S(1)}, u32[]{:S(2)}, u32[]{:S(2)}) collective-permute-start(bf16[16,128,128]{2,1,0:T(8,128)(2,1)} %get-tuple-element.41), channel_id=1, source_target_pairs={{12,0},{16,4},{20,8},{24,12},{28,16},{32,20},{36,24},{40,28},{44,3... | collective-permute-start | bytes 1572872 | tf_op jit(solution)/shard_map/ppermute | solution.py:506
  50.1 11.7 %copy-start.16 = (bf16[512,128]{1,0:T(8,128)(2,1)}, bf16[512,128]{1,0:T(8,128)(2,1)S(1)}, u32[]{:S(2)}) copy-start(bf16[512,128]{1,0:T(8,128)(2,1)S(1)} %collective-permute-done.14.rest_1_) | copy-start | bytes 393220
  50.1 39.7 %collective-permute-start.7 = (bf16[16,128,128]{2,1,0:T(8,128)(2,1)}, bf16[16,128,128]{2,1,0:T(8,128)(2,1)S(1)}, u32[]{:S(2)}, u32[]{:S(2)}) collective-permute-start(bf16[16,128,128]{2,1,0:T(8,128)(2,1)} %get-tuple-element.42), channel_id=1, source_target_pairs={{0,12},{4,16},{8,20},{12,24},{16,28},{20,32},{24,36},{28,40},{32,4... | collective-permute-start | bytes 1572872 | tf_op jit(solution)/shard_map/ppermute | solution.py:506
  52.3 44.0 %copy-start.4 = (bf16[16,128,128]{2,1,0:T(8,128)(2,1)}, bf16[16,128,128]{2,1,0:T(8,128)(2,1)S(1)}, u32[]{:S(2)}) copy-start(bf16[16,128,128]{2,1,0:T(8,128)(2,1)S(1)} %collective-permute-done.3.refs_1_) | copy-start | bytes 1572868
  52.3 39.5 %collective-permute-start.8 = (bf16[16,128,128]{2,1,0:T(8,128)(2,1)}, bf16[16,128,128]{2,1,0:T(8,128)(2,1)}, u32[]{:S(2)}, u32[]{:S(2)}) collective-permute-start(bf16[16,128,128]{2,1,0:T(8,128)(2,1)} %get-tuple-element.43), channel_id=1, source_target_pairs={{28,0},{32,4},{36,8},{40,12},{44,16},{48,20},{52,24},{56,28},{60,3... | collective-permute-start | bytes 1572872 | tf_op jit(solution)/shard_map/ppermute | solution.py:506
  56.1 40.2 %copy-start.5 = (bf16[16,128,128]{2,1,0:T(8,128)(2,1)}, bf16[16,128,128]{2,1,0:T(8,128)(2,1)S(1)}, u32[]{:S(2)}) copy-start(bf16[16,128,128]{2,1,0:T(8,128)(2,1)S(1)} %collective-permute-done.4.refs_2_) | copy-start | bytes 1572868
  56.1 40.1 %collective-permute-start.9 = (bf16[16,128,128]{2,1,0:T(8,128)(2,1)}, bf16[16,128,128]{2,1,0:T(8,128)(2,1)}, u32[]{:S(2)}, u32[]{:S(2)}) collective-permute-start(bf16[16,128,128]{2,1,0:T(8,128)(2,1)} %get-tuple-element.44), channel_id=1, source_target_pairs={{0,28},{4,32},{8,36},{12,40},{16,44},{20,48},{24,52},{28,56},{32,6... | collective-permute-start | bytes 1572872 | tf_op jit(solution)/shard_map/ppermute | solution.py:506
  59.7 36.6 %copy-start.6 = (bf16[16,128,128]{2,1,0:T(8,128)(2,1)}, bf16[16,128,128]{2,1,0:T(8,128)(2,1)S(1)}, u32[]{:S(2)}) copy-start(bf16[16,128,128]{2,1,0:T(8,128)(2,1)S(1)} %collective-permute-done.5.refs_3_) | copy-start | bytes 1572868
  59.7 36.6 %collective-permute-start.2 = (bf16[16,128,128]{2,1,0:T(8,128)(2,1)}, bf16[16,128,128]{2,1,0:T(8,128)(2,1)}, u32[]{:S(2)}, u32[]{:S(2)}) collective-permute-start(bf16[16,128,128]{2,1,0:T(8,128)(2,1)} %get-tuple-element.37), channel_id=1, source_target_pairs={{16,0},{20,4},{24,8},{28,12},{32,16},{36,20},{40,24},{44,28},{48,3... | collective-permute-start | bytes 1572872 | tf_op jit(solution)/shard_map/ppermute | solution.py:506
  83.7 12.6 %copy-start.7 = (bf16[16,128,128]{2,1,0:T(8,128)(2,1)}, bf16[16,128,128]{2,1,0:T(8,128)(2,1)S(1)}, u32[]{:S(2)}) copy-start(bf16[16,128,128]{2,1,0:T(8,128)(2,1)S(1)} %collective-permute-done.6.refs_4_) | copy-start | bytes 1572868
  83.7 32.1 %collective-permute-start.17 = (bf16[16,128,128]{2,1,0:T(8,128)(2,1)}, bf16[16,128,128]{2,1,0:T(8,128)(2,1)S(1)}, u32[]{:S(2)}, u32[]{:S(2)}) collective-permute-start(bf16[16,128,128]{2,1,0:T(8,128)(2,1)} %get-tuple-element.49), channel_id=1, source_target_pairs={{0,20},{4,24},{8,28},{12,32},{16,36},{20,40},{24,44},{28,48},{32,5... | collective-permute-start | bytes 1572872 | tf_op jit(solution)/shard_map/ppermute | solution.py:515
  89.8 6.5 %copy-start.8 = (bf16[16,128,128]{2,1,0:T(8,128)(2,1)}, bf16[16,128,128]{2,1,0:T(8,128)(2,1)S(1)}, u32[]{:S(2)}) copy-start(bf16[16,128,128]{2,1,0:T(8,128)(2,1)S(1)} %collective-permute-done.7.refs_5_) | copy-start | bytes 1572868
  89.9 31.7 %collective-permute-start.18 = (bf16[16,128,128]{2,1,0:T(8,128)(2,1)}, bf16[16,128,128]{2,1,0:T(8,128)(2,1)S(1)}, u32[]{:S(2)}, u32[]{:S(2)}) collective-permute-start(bf16[16,128,128]{2,1,0:T(8,128)(2,1)} %get-tuple-element.52), channel_id=1, source_target_pairs={{20,0},{24,4},{28,8},{32,12},{36,16},{40,20},{44,24},{48,28},{52,3... | collective-permute-start | bytes 1572872 | tf_op jit(solution)/shard_map/ppermute | solution.py:515
  91.8 42.4 %collective-permute-start.20 = (bf16[16,128,128]{2,1,0:T(8,128)(2,1)}, bf16[16,128,128]{2,1,0:T(8,128)(2,1)}, u32[]{:S(2)}, u32[]{:S(2)}) collective-permute-start(bf16[16,128,128]{2,1,0:T(8,128)(2,1)} %get-tuple-element.57), channel_id=1, source_target_pairs={{0,8},{4,12},{8,16},{12,20},{16,24},{20,28},{24,32},{28,36},{32,40... | collective-permute-start | bytes 1572872 | tf_op jit(solution)/shard_map/ppermute | solution.py:515
  100.2 6.5 %collective-permute-start.11 = (bf16[256,128]{1,0:T(8,128)(2,1)}, bf16[256,128]{1,0:T(8,128)(2,1)S(1)}, u32[]{:S(2)}, u32[]{:S(2)}) collective-permute-start(bf16[256,128]{1,0:T(8,128)(2,1)} %pack_parts.1), channel_id=1, source_target_pairs={{1,0},{2,1},{3,2},{5,4},{6,5},{7,6},{9,8},{10,9},{11,10},{13,12},{... | collective-permute-start | bytes 196616 | tf_op jit(solution)/shard_map/ppermute | solution.py:518
  104.5 9.3 %collective-permute-start.10 = (bf16[256,128]{1,0:T(8,128)(2,1)}, bf16[256,128]{1,0:T(8,128)(2,1)S(1)}, u32[]{:S(2)}, u32[]{:S(2)}) collective-permute-start(bf16[256,128]{1,0:T(8,128)(2,1)} %pack_parts.1), channel_id=1, source_target_pairs={{0,1},{1,2},{2,3},{4,5},{5,6},{6,7},{8,9},{9,10},{10,11},{12,13},{... | collective-permute-start | bytes 196616 | tf_op jit(solution)/shard_map/ppermute | solution.py:518
  106.7 29.7 %copy-start.17 = (bf16[256,128]{1,0:T(8,128)(2,1)}, bf16[256,128]{1,0:T(8,128)(2,1)S(1)}, u32[]{:S(2)}) copy-start(bf16[256,128]{1,0:T(8,128)(2,1)S(1)} %collective-permute-done.11.from_right) | copy-start | bytes 196612
  106.7 35.0 %collective-permute-start.21 = (bf16[16,128,128]{2,1,0:T(8,128)(2,1)}, bf16[16,128,128]{2,1,0:T(8,128)(2,1)S(1)}, u32[]{:S(2)}, u32[]{:S(2)}) collective-permute-start(bf16[16,128,128]{2,1,0:T(8,128)(2,1)} %get-tuple-element.58), channel_id=1, source_target_pairs={{0,4},{4,8},{8,12},{12,16},{16,20},{20,24},{24,28},{28,32},{32,36}... | collective-permute-start | bytes 1572872 | tf_op jit(solution)/shard_map/ppermute | solution.py:515
  113.8 22.6 %copy-start.18 = (bf16[256,128]{1,0:T(8,128)(2,1)}, bf16[256,128]{1,0:T(8,128)(2,1)S(1)}, u32[]{:S(2)}) copy-start(bf16[256,128]{1,0:T(8,128)(2,1)S(1)} %collective-permute-done.10.from_left) | copy-start | bytes 196612
  113.8 28.0 %collective-permute-start.22 = (bf16[16,128,128]{2,1,0:T(8,128)(2,1)}, bf16[16,128,128]{2,1,0:T(8,128)(2,1)S(1)}, u32[]{:S(2)}, u32[]{:S(2)}) collective-permute-start(bf16[16,128,128]{2,1,0:T(8,128)(2,1)} %get-tuple-element.60), channel_id=1, source_target_pairs={{4,0},{8,4},{12,8},{16,12},{20,16},{24,20},{28,24},{32,28},{36,32}... | collective-permute-start | bytes 1572872 | tf_op jit(solution)/shard_map/ppermute | solution.py:515
  115.9 33.6 %copy-start.2 = (bf16[16,128,128]{2,1,0:T(8,128)(2,1)}, bf16[16,128,128]{2,1,0:T(8,128)(2,1)S(1)}, u32[]{:S(2)}) copy-start(bf16[16,128,128]{2,1,0:T(8,128)(2,1)S(1)} %collective-permute-done.17.refs_0_.refs_3_) | copy-start | bytes 1572868
  115.9 33.6 %collective-permute-start.23 = (bf16[16,128,128]{2,1,0:T(8,128)(2,1)}, bf16[16,128,128]{2,1,0:T(8,128)(2,1)S(1)}, u32[]{:S(2)}, u32[]{:S(2)}) collective-permute-start(bf16[16,128,128]{2,1,0:T(8,128)(2,1)} %get-tuple-element.61), channel_id=1, source_target_pairs={{8,0},{12,4},{16,8},{20,12},{24,16},{28,20},{32,24},{36,28},{40,32... | collective-permute-start | bytes 1572872 | tf_op jit(solution)/shard_map/ppermute | solution.py:515
  121.6 27.9 %copy-start.3 = (bf16[16,128,128]{2,1,0:T(8,128)(2,1)}, bf16[16,128,128]{2,1,0:T(8,128)(2,1)S(1)}, u32[]{:S(2)}) copy-start(bf16[16,128,128]{2,1,0:T(8,128)(2,1)S(1)} %collective-permute-done.18.refs_10_.refs_6_) | copy-start | bytes 1572868
  121.6 34.6 %collective-permute-start.16 = (bf16[16,128,128]{2,1,0:T(8,128)(2,1)}, bf16[16,128,128]{2,1,0:T(8,128)(2,1)S(1)}, u32[]{:S(2)}, u32[]{:S(2)}) collective-permute-start(bf16[16,128,128]{2,1,0:T(8,128)(2,1)} %get-tuple-element.48), channel_id=1, source_target_pairs={{0,24},{4,28},{8,32},{12,36},{16,40},{20,44},{24,48},{28,52},{32,5... | collective-permute-start | bytes 1572872 | tf_op jit(solution)/shard_map/ppermute | solution.py:515
  134.2 22.0 %collective-permute-start.19 = (bf16[16,128,128]{2,1,0:T(8,128)(2,1)}, bf16[16,128,128]{2,1,0:T(8,128)(2,1)S(1)}, u32[]{:S(2)}, u32[]{:S(2)}) collective-permute-start(bf16[16,128,128]{2,1,0:T(8,128)(2,1)} %get-tuple-element.53), channel_id=1, source_target_pairs={{24,0},{28,4},{32,8},{36,12},{40,16},{44,20},{48,24},{52,28},{56,3... | collective-permute-start | bytes 1572872 | tf_op jit(solution)/shard_map/ppermute | solution.py:515
  141.7 7.8 %copy-start.9 = (bf16[16,128,128]{2,1,0:T(8,128)(2,1)}, bf16[16,128,128]{2,1,0:T(8,128)(2,1)S(1)}, u32[]{:S(2)}) copy-start(bf16[16,128,128]{2,1,0:T(8,128)(2,1)S(1)} %collective-permute-done.21.refs_4_) | copy-start | bytes 1572868
  141.7 7.7 %copy-start.10 = (bf16[16,128,128]{2,1,0:T(8,128)(2,1)}, bf16[16,128,128]{2,1,0:T(8,128)(2,1)S(1)}, u32[]{:S(2)}) copy-start(bf16[16,128,128]{2,1,0:T(8,128)(2,1)S(1)} %collective-permute-done.22.refs_6_) | copy-start | bytes 1572868
  149.5 0.8 copy-start.11
  156.2 0.8 copy-start.13
  156.3 1.0 copy-start.14

commit v3 on v2

--- a/solution.py
+++ b/solution.py
@@ -25,7 +25,7 @@
 EARLY = ORDER[:8]
 LATE = ORDER[8:] + (0,)
 CODED = ROWS + 16
-FIRST, STOP = 3, 13
+FIRST, STOP = 5, 11
 
 HBM = pl.BlockSpec(memory_space=pl.ANY)
 VMEM = pl.BlockSpec(memory_space=pltpu.VMEM)
@@ -359,14 +359,19 @@
 
 
 INNER = (STOP - FIRST) * BLOCK - 16
-OUTER = 272
+OUTER = 400
 LOW = FIRST * BLOCK
+LAG = 8
 HIGH = LOW + INNER
+
+
+INNER_PARTS = [c for c in ORDER + (0,) if FIRST <= c + 8 <= STOP]
+OUTER_PARTS = [c for c in ORDER + (0,) if c + 8 <= FIRST + 1 or c + 8 >= STOP - 1]
 
 
 def inner_kernel(*refs):
     count = STOP - FIRST + 1
-    parts = refs[:count]
+    parts = [refs[INNER_PARTS.index(b - 8)] for b in range(FIRST, STOP + 1)]
     out_ref, got, full, done, sem, out_sem = refs[count:]
 
     def fetch(i):
@@ -395,7 +400,8 @@
 def outer_kernel(*refs):
     top, bottom = FIRST + 2, SENDS - STOP + 1
     count = top + bottom
-    parts = refs[:count]
+    wanted = list(range(top)) + list(range(STOP - 1, SENDS))
+    parts = [refs[OUTER_PARTS.index(b - 8)] for b in wanted]
     _, out_ref, got, full, done, sem, out_sem = refs[count:]
 
     def fetch(i):
@@ -440,9 +446,9 @@
         for put in puts(q, tile)[::3]:
             put.start()
 
-        @pl.when(q >= 2)
+        @pl.when(q >= LAG)
         def _():
-            inward(q - 2)
+            inward(q - LAG)
 
         return 0
 
@@ -454,7 +460,7 @@
         high.start()
 
     lax.fori_loop(0, SLAB, plane, 0)
-    for q in range(SLAB - 2, SLAB):
+    for q in range(SLAB - LAG, SLAB):
         inward(q)
     for q in range(SLAB):
         for put in puts(q, shift_of(q)[2])[1:3]:
@@ -518,9 +524,11 @@
     arrived = smooth_parts(lax.ppermute(own, "col", right), lax.ppermute(own, "col", left), *arrived)
     moved.update(zip(EARLY, arrived))
     moved[0] = parts[0]
-    ready = [moved[b - 8] for b in range(FIRST, STOP + 1)]
+    sooner = ORDER[:-2]
+    moved.update(zip(sooner, lax.optimization_barrier([moved[c] for c in sooner])))
+    ready = [moved[c] for c in INNER_PARTS]
     result = row_shear(inner_kernel, ready, INNER, (STOP - FIRST) * BLOCK, ())
-    rest = [moved[b - 8] for b in list(range(FIRST + 2)) + list(range(STOP - 1, SENDS))]
+    rest = [moved[c] for c in OUTER_PARTS]
     full_rows = (FIRST + 1 + SENDS - STOP) * BLOCK + 2 * MARGIN
     return row_shear(outer_kernel, rest, 4 * OUTER, full_rows, (4,), result)
 

time: 167 us -> 165 us (0.988)
  the two profiles are of different devices: /device:TPU:62 before, /device:TPU:6 now
where the time goes in v3:
time: 165 us; the launch traced here: 164 us
  starting transfers between devices  80 us (48%)
  Pallas kernels  61.2 us (37%)
  waiting for transfers between devices  17.6 us (11%)
  local copies, waits for them, and re-layouts  4.8 us (3%)
    ppermute x8, starting transfers between devices, local(): moved[c] = lax.ppermute(parts[c], 'scan', pairs_of(c))  31.2 us
    pallas_call x2, Pallas kernels, shear(): pl.pallas_call(functools.partial(shear_kernel, group), out_shape=(PART,)...  29.9 us
    ppermute x8, starting transfers between devices, local(): lax.ppermute(part, 'scan', pairs_of(c))  24.6 us
    pallas_call x2, Pallas kernels, row_shear(): pl.pallas_call(kernel, out_shape=jax.ShapeDtypeStruct((SLAB, ROWS, COLS),...  12.3 us
    ppermute x8, waiting for transfers between devices, local(): moved[c] = lax.ppermute(parts[c], 'scan', pairs_of(c))  11.7 us
    pallas_call x1, Pallas kernels, pack_edges(): pl.pallas_call(pack_edges_kernel, out_shape=jax.ShapeDtypeStruct((EDGE_RO...  6.83 us
    ppermute x1, starting transfers between devices, local(): after = lax.ppermute(first, 'scan', down)  6 us
    ppermute x1, starting transfers between devices, local(): edges_after = lax.ppermute(edges, 'scan', down)  5.46 us
  transfers between devices with their start and end apart: 24, of which 4 were waited for; matrix products, arithmetic and copies ran while one was open for 0% of the time, Pallas kernels for 31%

profile of v3, /device:TPU:6, one launch (start us, length us, event | category | flops | bytes accessed | tf_op | source)
XLA Modules:
  0.0 164.4 jit_solution(15751323499579906709)
XLA Ops:
  0.0 2.9 %halos.1 = (bf16[2,2064,128]{2,1,0:T(8,128)(2,1)}, bf16[1,2064,128]{2,1,0:T(8,128)(2,1)}) custom-call(s32[16]{0:T(128)} %offsets.5, bf16[16,2048,128]{2,1,0:T(8,128)(2,1)} %raw_ref.5), custom_call_target="tpu_custom_call" | custom-call | flops 1000 | bytes 1000 | tf_op jit(solution)/shard_map/halos/pallas_call | solution.py:61
  2.9 6.0 %collective-permute-start.1 = (bf16[2,2064,128]{2,1,0:T(8,128)(2,1)}, bf16[2,2064,128]{2,1,0:T(8,128)(2,1)S(1)}, u32[]{:S(2)}, u32[]{:S(2)}) collective-permute-start(bf16[2,2064,128]{2,1,0:T(8,128)(2,1)} %get-tuple-element.50), channel_id=1, source_target_pairs={{4,0},{8,4},{12,8},{16,12},{20,16},{24,20},{28,24},{32,28},{36,32}... | collective-permute-start | bytes 3170312 | tf_op jit(solution)/shard_map/ppermute | solution.py:505
  8.9 1.3 collective-permute-start
  10.2 6.8 %pack_edges.1 = bf16[512,128]{1,0:T(8,128)(2,1)} custom-call(bf16[16,2048,128]{2,1,0:T(8,128)(2,1)} %raw_ref.5), custom_call_target="tpu_custom_call" | custom-call | flops 1000 | bytes 1000 | tf_op jit(solution)/shard_map/pack_edges/pallas_call | solution.py:94
  17.1 2.7 %collective-permute-start.13 = (bf16[512,128]{1,0:T(8,128)(2,1)}, bf16[512,128]{1,0:T(8,128)(2,1)S(1)}, u32[]{:S(2)}, u32[]{:S(2)}) collective-permute-start(bf16[512,128]{1,0:T(8,128)(2,1)} %pack_edges.1), channel_id=1, source_target_pairs={{1,0},{2,1},{3,2},{5,4},{6,5},{7,6},{9,8},{10,9},{11,10},{13,12},{... | collective-permute-start | bytes 393224 | tf_op jit(solution)/shard_map/ppermute | solution.py:509
  19.8 1.3 collective-permute-start.12
  21.1 0.0 collective-permute-done.before_ref
  21.1 0.5 collective-permute-done.1.after_ref
  21.6 0.3 copy-done.1
  22.0 1.0 copy-done
  22.9 8.1 %shear_planes.2 = (bf16[16,128,128]{2,1,0:T(8,128)(2,1)}, bf16[16,128,128]{2,1,0:T(8,128)(2,1)}, bf16[16,128,128]{2,1,0:T(8,128)(2,1)}, bf16[16,128,128]{2,1,0:T...) custom-call(s32[16]{0:T(128)} %offsets.5, ...), custom_call_target="tpu_custom_call" | custom-call | flops 1000 | bytes 1000 | tf_op jit(solution)/shard_map/shear_planes/pallas_call | solution.py:249
  31.0 1.3 collective-permute-start.3
  32.4 0.0 collective-permute-done.13
  32.4 5.5 %collective-permute-start.15 = (bf16[512,128]{1,0:T(8,128)(2,1)S(1)}, bf16[512,128]{1,0:T(8,128)(2,1)S(1)}, u32[]{:S(2)}, u32[]{:S(2)}) collective-permute-start(bf16[512,128]{1,0:T(8,128)(2,1)S(1)} %fusion.rest_2_), channel_id=1, source_target_pairs={{4,0},{8,4},{12,8},{16,12},{20,16},{24,20},{28,24},{32,28},{36,32}... | collective-permute-start | bytes 393224 | tf_op jit(solution)/shard_map/ppermute | solution.py:516
  37.9 1.3 collective-permute-start.14
  39.2 1.3 collective-permute-start.4
  40.5 4.6 %collective-permute-start.5 = (bf16[16,128,128]{2,1,0:T(8,128)(2,1)}, bf16[16,128,128]{2,1,0:T(8,128)(2,1)S(1)}, u32[]{:S(2)}, u32[]{:S(2)}) collective-permute-start(bf16[16,128,128]{2,1,0:T(8,128)(2,1)} %get-tuple-element.54), channel_id=1, source_target_pairs={{0,32},{4,36},{8,40},{12,44},{16,48},{20,52},{24,56},{28,60},{32,6... | collective-permute-start | bytes 1572872 | tf_op jit(solution)/shard_map/ppermute | solution.py:512
  45.1 1.3 collective-permute-start.6
  46.4 0.0 collective-permute-done.14.rest_1_
  46.4 6.1 %collective-permute-start.7 = (bf16[16,128,128]{2,1,0:T(8,128)(2,1)}, bf16[16,128,128]{2,1,0:T(8,128)(2,1)S(1)}, u32[]{:S(2)}, u32[]{:S(2)}) collective-permute-start(bf16[16,128,128]{2,1,0:T(8,128)(2,1)} %get-tuple-element.56), channel_id=1, source_target_pairs={{0,12},{4,16},{8,20},{12,24},{16,28},{20,32},{24,36},{28,40},{32,4... | collective-permute-start | bytes 1572872 | tf_op jit(solution)/shard_map/ppermute | solution.py:512
  52.5 1.3 collective-permute-start.8
  53.8 7.2 %collective-permute-start.9 = (bf16[16,128,128]{2,1,0:T(8,128)(2,1)}, bf16[16,128,128]{2,1,0:T(8,128)(2,1)S(1)}, u32[]{:S(2)}, u32[]{:S(2)}) collective-permute-start(bf16[16,128,128]{2,1,0:T(8,128)(2,1)} %get-tuple-element.58), channel_id=1, source_target_pairs={{0,28},{4,32},{8,36},{12,40},{16,44},{20,48},{24,52},{28,56},{32,6... | collective-permute-start | bytes 1572872 | tf_op jit(solution)/shard_map/ppermute | solution.py:512
  61.1 1.5 collective-permute-start.2
  62.6 21.9 %shear_planes.3 = (bf16[16,128,128]{2,1,0:T(8,128)(2,1)}, bf16[16,128,128]{2,1,0:T(8,128)(2,1)}, bf16[16,128,128]{2,1,0:T(8,128)(2,1)}, bf16[16,128,128]{2,1,0:T...) custom-call(s32[16]{0:T(128)} %offsets.5, ...), custom_call_target="tpu_custom_call" | custom-call | flops 1000 | bytes 1000 | tf_op jit(solution)/shard_map/shear_planes/pallas_call | solution.py:249
  84.5 0.0 copy-start.7
  84.5 1.3 collective-permute-start.16
  85.8 6.6 %collective-permute-start.17 = (bf16[16,128,128]{2,1,0:T(8,128)(2,1)}, bf16[16,128,128]{2,1,0:T(8,128)(2,1)}, u32[]{:S(2)}, u32[]{:S(2)}) collective-permute-start(bf16[16,128,128]{2,1,0:T(8,128)(2,1)} %get-tuple-element.69), channel_id=1, source_target_pairs={{0,20},{4,24},{8,28},{12,32},{16,36},{20,40},{24,44},{28,48},{32,5... | collective-permute-start | bytes 1572872 | tf_op jit(solution)/shard_map/ppermute | solution.py:521
  92.4 1.3 collective-permute-start.18
  93.8 0.7 copy-done.10
  94.5 3.9 %pack_parts.1 = bf16[256,128]{1,0:T(8,128)(2,1)} custom-call(bf16[16,128,128]{2,1,0:T(8,128)(2,1)} %collective-permute-done.2.refs_0_, bf16[16,128,128]{2,1,0:T(8,128)(2,1)} %copy-done.4, bf16[16,128,128]{2,1,0:T(8,128)(2,1)} %copy-done.5, bf16[16,128,128]{2,1,0:T(8,128)(2,1)} %copy-done.6, bf16[16,128,128]{2,1,0:T(8,128)(2,1)} %copy-done.7, ...), custom_call_target="tpu_custom_call" | custom-call | flops 1000 | bytes 1000 | tf_op jit(solution)/shard_map/pack_parts/pallas_call | solution.py:286
  98.4 4.8 %collective-permute-start.11 = (bf16[256,128]{1,0:T(8,128)(2,1)}, bf16[256,128]{1,0:T(8,128)(2,1)S(1)}, u32[]{:S(2)}, u32[]{:S(2)}) collective-permute-start(bf16[256,128]{1,0:T(8,128)(2,1)} %pack_parts.1), channel_id=1, source_target_pairs={{1,0},{2,1},{3,2},{5,4},{6,5},{7,6},{9,8},{10,9},{11,10},{13,12},{... | collective-permute-start | bytes 196616 | tf_op jit(solution)/shard_map/ppermute | solution.py:524
  103.3 1.3 collective-permute-start.10
  104.6 1.3 collective-permute-done.11.from_right
  105.9 0.3 collective-permute-start.19
  106.2 4.0 %collective-permute-done.10.from_left = bf16[256,128]{1,0:T(8,128)(2,1)S(1)} collective-permute-done((bf16[256,128]{1,0:T(8,128)(2,1)}, bf16[256,128]{1,0:T(8,128)(2,1)S(1)}, u32[]{:S(2)}, u32[]{:S(2)}) %collective-permute-start.10) | collective-permute-done | bytes 65568 | tf_op jit(solution)/shard_map/ppermute | solution.py:524
  110.2 1.3 collective-permute-start.20
  111.5 6.7 %collective-permute-start.21 = (bf16[16,128,128]{2,1,0:T(8,128)(2,1)}, bf16[16,128,128]{2,1,0:T(8,128)(2,1)S(1)}, u32[]{:S(2)}, u32[]{:S(2)}) collective-permute-start(bf16[16,128,128]{2,1,0:T(8,128)(2,1)} %get-tuple-element.73), channel_id=1, source_target_pairs={{0,8},{4,12},{8,16},{12,20},{16,24},{20,28},{24,32},{28,36},{32,40... | collective-permute-start | bytes 1572872 | tf_op jit(solution)/shard_map/ppermute | solution.py:521
  118.3 1.3 collective-permute-start.22
  119.6 12.5 %collective-permute-start.23 = (bf16[16,128,128]{2,1,0:T(8,128)(2,1)}, bf16[16,128,128]{2,1,0:T(8,128)(2,1)S(1)}, u32[]{:S(2)}, u32[]{:S(2)}) collective-permute-start(bf16[16,128,128]{2,1,0:T(8,128)(2,1)} %get-tuple-element.87), channel_id=1, source_target_pairs={{0,24},{4,28},{8,32},{12,36},{16,40},{20,44},{24,48},{28,52},{32,5... | collective-permute-start | bytes 1572872 | tf_op jit(solution)/shard_map/ppermute | solution.py:521
  132.1 5.3 %smooth_parts.1 = (bf16[16,128,128]{2,1,0:T(8,128)(2,1)}, bf16[16,128,128]{2,1,0:T(8,128)(2,1)}, bf16[16,128,128]{2,1,0:T(8,128)(2,1)}, bf16[16,128,128]{2,1,0:T...) custom-call(bf16[256,128]{1,0:T(8,128)(2,1)} %copy-done.18, ...), custom_call_target="tpu_custom_call" | custom-call | flops 1000 | bytes 1000 | tf_op jit(solution)/shard_map/smooth_parts/pallas_call | solution.py:315
  137.5 0.7 copy-done.12
  138.3 0.2 copy-done.2
  138.5 0.1 copy-done.3
  138.6 4.3 %shear_rows.2.refs_14_ = bf16[16,2048,128]{2,1,0:T(8,128)(2,1)} custom-call(bf16[16,128,128]{2,1,0:T(8,128)(2,1)} %get-tuple-element.78.refs_0_.refs_4_, bf16[16,128,128]{2,1,0:T(8,128)(2,1)} %get-tuple-element.79.refs_1_.refs_5_, bf16[16,128,128]{2,1,0:T(8,128)(2,1)} %collective-permute-done.18.refs_2_, bf16[16,128,128]{2,1,0:T(8,128)(2,1)} %copy-done.12, ...), custom_call_target="tpu_custom_call" | custom-call | flops 1000 | bytes 1000 | tf_op jit(solution)/shard_map/shear_rows/pallas_call | solution.py:473
  143.0 11.7 %collective-permute-done.22.refs_12_ = bf16[16,128,128]{2,1,0:T(8,128)(2,1)S(1)} collective-permute-done((bf16[16,128,128]{2,1,0:T(8,128)(2,1)}, bf16[16,128,128]{2,1,0:T(8,128)(2,1)S(1)}, u32[]{:S(2)}, u32[]{:S(2)}) %collective-permute-start.22) | collective-permute-done | bytes 524320 | tf_op jit(solution)/shard_map/ppermute | solution.py:521
  154.6 0.8 copy-done.13
  155.4 0.8 copy-done.14
  156.2 8.0 %shear_rows.3 = bf16[16,2048,128]{2,1,0:T(8,128)(2,1)} custom-call(bf16[16,128,128]{2,1,0:T(8,128)(2,1)} %get-tuple-element.74.refs_0_, bf16[16,128,128]{2,1,0:T(8,128)(2,1)} %get-tuple-element.75.refs_1_, bf16[16,128,128]{2,1,0:T(8,128)(2,1)} %get-tuple-element.76.refs_2_, ...), custom_call_target="tpu_custom_call", output_to_operand_aliasing={{}: (14, {})} | custom-call | flops 1000 | bytes 1000 | tf_op jit(solution)/shard_map/shear_rows/pallas_call | solution.py:473
  (49 shorter events, 0.2 us)
Async XLA Ops:
  2.9 18.7 %collective-permute-start.1 = (bf16[2,2064,128]{2,1,0:T(8,128)(2,1)}, bf16[2,2064,128]{2,1,0:T(8,128)(2,1)S(1)}, u32[]{:S(2)}, u32[]{:S(2)}) collective-permute-start(bf16[2,2064,128]{2,1,0:T(8,128)(2,1)} %get-tuple-element.50), channel_id=1, source_target_pairs={{4,0},{8,4},{12,8},{16,12},{20,16},{24,20},{28,24},{32,28},{36,32}... | collective-permute-start | bytes 3170312 | tf_op jit(solution)/shard_map/ppermute | solution.py:505
  8.9 12.2 %collective-permute-start = (bf16[1,2064,128]{2,1,0:T(8,128)(2,1)}, bf16[1,2064,128]{2,1,0:T(8,128)(2,1)S(1)}, u32[]{:S(2)}, u32[]{:S(2)}) collective-permute-start(bf16[1,2064,128]{2,1,0:T(8,128)(2,1)} %get-tuple-element.49), channel_id=1, source_target_pairs={{0,4},{4,8},{8,12},{12,16},{16,20},{20,24},{24,28},{28,32},{32,36}... | collective-permute-start | bytes 1585160 | tf_op jit(solution)/shard_map/ppermute | solution.py:506
  17.1 15.3 %collective-permute-start.13 = (bf16[512,128]{1,0:T(8,128)(2,1)}, bf16[512,128]{1,0:T(8,128)(2,1)S(1)}, u32[]{:S(2)}, u32[]{:S(2)}) collective-permute-start(bf16[512,128]{1,0:T(8,128)(2,1)} %pack_edges.1), channel_id=1, source_target_pairs={{1,0},{2,1},{3,2},{5,4},{6,5},{7,6},{9,8},{10,9},{11,10},{13,12},{... | collective-permute-start | bytes 393224 | tf_op jit(solution)/shard_map/ppermute | solution.py:509
  19.8 12.6 %collective-permute-start.12 = (bf16[512,128]{1,0:T(8,128)(2,1)}, bf16[512,128]{1,0:T(8,128)(2,1)S(1)}, u32[]{:S(2)}, u32[]{:S(2)}) collective-permute-start(bf16[512,128]{1,0:T(8,128)(2,1)} %pack_edges.1), channel_id=1, source_target_pairs={{0,1},{1,2},{2,3},{4,5},{5,6},{6,7},{8,9},{9,10},{10,11},{12,13},{... | collective-permute-start | bytes 393224 | tf_op jit(solution)/shard_map/ppermute | solution.py:508
  21.1 0.8 copy-start.1
  22.0 1.0 copy-start
  31.0 21.5 %collective-permute-start.3 = (bf16[16,128,128]{2,1,0:T(8,128)(2,1)}, bf16[16,128,128]{2,1,0:T(8,128)(2,1)S(1)}, u32[]{:S(2)}, u32[]{:S(2)}) collective-permute-start(bf16[16,128,128]{2,1,0:T(8,128)(2,1)} %get-tuple-element.52), channel_id=1, source_target_pairs={{0,16},{4,20},{8,24},{12,28},{16,32},{20,36},{24,40},{28,44},{32,4... | collective-permute-start | bytes 1572872 | tf_op jit(solution)/shard_map/ppermute | solution.py:512
  32.4 30.2 %copy-start.11 = (bf16[512,128]{1,0:T(8,128)(2,1)}, bf16[512,128]{1,0:T(8,128)(2,1)S(1)}, u32[]{:S(2)}) copy-start(bf16[512,128]{1,0:T(8,128)(2,1)S(1)} %fusion.rest_2_) | copy-start | bytes 393220
  32.4 12.6 %collective-permute-start.15 = (bf16[512,128]{1,0:T(8,128)(2,1)S(1)}, bf16[512,128]{1,0:T(8,128)(2,1)S(1)}, u32[]{:S(2)}, u32[]{:S(2)}) collective-permute-start(bf16[512,128]{1,0:T(8,128)(2,1)S(1)} %fusion.rest_2_), channel_id=1, source_target_pairs={{4,0},{8,4},{12,8},{16,12},{20,16},{24,20},{28,24},{32,28},{36,32}... | collective-permute-start | bytes 393224 | tf_op jit(solution)/shard_map/ppermute | solution.py:516
  37.9 8.5 %collective-permute-start.14 = (bf16[512,128]{1,0:T(8,128)(2,1)S(1)}, bf16[512,128]{1,0:T(8,128)(2,1)S(1)}, u32[]{:S(2)}, u32[]{:S(2)}) collective-permute-start(bf16[512,128]{1,0:T(8,128)(2,1)S(1)} %fusion.rest_2_), channel_id=1, source_target_pairs={{0,4},{4,8},{8,12},{12,16},{16,20},{20,24},{24,28},{28,32},{32,36}... | collective-permute-start | bytes 393224 | tf_op jit(solution)/shard_map/ppermute | solution.py:517
  39.2 14.6 %collective-permute-start.4 = (bf16[16,128,128]{2,1,0:T(8,128)(2,1)}, bf16[16,128,128]{2,1,0:T(8,128)(2,1)S(1)}, u32[]{:S(2)}, u32[]{:S(2)}) collective-permute-start(bf16[16,128,128]{2,1,0:T(8,128)(2,1)} %get-tuple-element.53), channel_id=1, source_target_pairs={{32,0},{36,4},{40,8},{44,12},{48,16},{52,20},{56,24},{60,28},{64,3... | collective-permute-start | bytes 1572872 | tf_op jit(solution)/shard_map/ppermute | solution.py:512
  40.5 20.6 %collective-permute-start.5 = (bf16[16,128,128]{2,1,0:T(8,128)(2,1)}, bf16[16,128,128]{2,1,0:T(8,128)(2,1)S(1)}, u32[]{:S(2)}, u32[]{:S(2)}) collective-permute-start(bf16[16,128,128]{2,1,0:T(8,128)(2,1)} %get-tuple-element.54), channel_id=1, source_target_pairs={{0,32},{4,36},{8,40},{12,44},{16,48},{20,52},{24,56},{28,60},{32,6... | collective-permute-start | bytes 1572872 | tf_op jit(solution)/shard_map/ppermute | solution.py:512
  45.1 17.5 %copy-start.15 = (bf16[512,128]{1,0:T(8,128)(2,1)}, bf16[512,128]{1,0:T(8,128)(2,1)S(1)}, u32[]{:S(2)}) copy-start(bf16[512,128]{1,0:T(8,128)(2,1)S(1)} %collective-permute-done.15.rest_3_) | copy-start | bytes 393220
  45.1 39.4 %collective-permute-start.6 = (bf16[16,128,128]{2,1,0:T(8,128)(2,1)}, bf16[16,128,128]{2,1,0:T(8,128)(2,1)S(1)}, u32[]{:S(2)}, u32[]{:S(2)}) collective-permute-start(bf16[16,128,128]{2,1,0:T(8,128)(2,1)} %get-tuple-element.55), channel_id=1, source_target_pairs={{12,0},{16,4},{20,8},{24,12},{28,16},{32,20},{36,24},{40,28},{44,3... | collective-permute-start | bytes 1572872 | tf_op jit(solution)/shard_map/ppermute | solution.py:512
  46.4 16.2 %copy-start.16 = (bf16[512,128]{1,0:T(8,128)(2,1)}, bf16[512,128]{1,0:T(8,128)(2,1)S(1)}, u32[]{:S(2)}) copy-start(bf16[512,128]{1,0:T(8,128)(2,1)S(1)} %collective-permute-done.14.rest_1_) | copy-start | bytes 393220
  46.4 39.4 %collective-permute-start.7 = (bf16[16,128,128]{2,1,0:T(8,128)(2,1)}, bf16[16,128,128]{2,1,0:T(8,128)(2,1)S(1)}, u32[]{:S(2)}, u32[]{:S(2)}) collective-permute-start(bf16[16,128,128]{2,1,0:T(8,128)(2,1)} %get-tuple-element.56), channel_id=1, source_target_pairs={{0,12},{4,16},{8,20},{12,24},{16,28},{20,32},{24,36},{28,40},{32,4... | collective-permute-start | bytes 1572872 | tf_op jit(solution)/shard_map/ppermute | solution.py:512
  52.5 41.2 %copy-start.4 = (bf16[16,128,128]{2,1,0:T(8,128)(2,1)}, bf16[16,128,128]{2,1,0:T(8,128)(2,1)S(1)}, u32[]{:S(2)}) copy-start(bf16[16,128,128]{2,1,0:T(8,128)(2,1)S(1)} %collective-permute-done.3.refs_1_) | copy-start | bytes 1572868
  52.5 39.9 %collective-permute-start.8 = (bf16[16,128,128]{2,1,0:T(8,128)(2,1)}, bf16[16,128,128]{2,1,0:T(8,128)(2,1)S(1)}, u32[]{:S(2)}, u32[]{:S(2)}) collective-permute-start(bf16[16,128,128]{2,1,0:T(8,128)(2,1)} %get-tuple-element.57), channel_id=1, source_target_pairs={{28,0},{32,4},{36,8},{40,12},{44,16},{48,20},{52,24},{56,28},{60,3... | collective-permute-start | bytes 1572872 | tf_op jit(solution)/shard_map/ppermute | solution.py:512
  53.8 39.9 %copy-start.5 = (bf16[16,128,128]{2,1,0:T(8,128)(2,1)}, bf16[16,128,128]{2,1,0:T(8,128)(2,1)S(1)}, u32[]{:S(2)}) copy-start(bf16[16,128,128]{2,1,0:T(8,128)(2,1)S(1)} %collective-permute-done.4.refs_2_) | copy-start | bytes 1572868
  53.8 39.9 %collective-permute-start.9 = (bf16[16,128,128]{2,1,0:T(8,128)(2,1)}, bf16[16,128,128]{2,1,0:T(8,128)(2,1)S(1)}, u32[]{:S(2)}, u32[]{:S(2)}) collective-permute-start(bf16[16,128,128]{2,1,0:T(8,128)(2,1)} %get-tuple-element.58), channel_id=1, source_target_pairs={{0,28},{4,32},{8,36},{12,40},{16,44},{20,48},{24,52},{28,56},{32,6... | collective-permute-start | bytes 1572872 | tf_op jit(solution)/shard_map/ppermute | solution.py:512
  61.1 32.7 %copy-start.6 = (bf16[16,128,128]{2,1,0:T(8,128)(2,1)}, bf16[16,128,128]{2,1,0:T(8,128)(2,1)S(1)}, u32[]{:S(2)}) copy-start(bf16[16,128,128]{2,1,0:T(8,128)(2,1)S(1)} %collective-permute-done.5.refs_3_) | copy-start | bytes 1572868
  61.1 32.6 %collective-permute-start.2 = (bf16[16,128,128]{2,1,0:T(8,128)(2,1)}, bf16[16,128,128]{2,1,0:T(8,128)(2,1)}, u32[]{:S(2)}, u32[]{:S(2)}) collective-permute-start(bf16[16,128,128]{2,1,0:T(8,128)(2,1)} %get-tuple-element.51), channel_id=1, source_target_pairs={{16,0},{20,4},{24,8},{28,12},{32,16},{36,20},{40,24},{44,28},{48,3... | collective-permute-start | bytes 1572872 | tf_op jit(solution)/shard_map/ppermute | solution.py:512
  84.5 9.3 %copy-start.7 = (bf16[16,128,128]{2,1,0:T(8,128)(2,1)}, bf16[16,128,128]{2,1,0:T(8,128)(2,1)S(1)}, u32[]{:S(2)}) copy-start(bf16[16,128,128]{2,1,0:T(8,128)(2,1)S(1)} %collective-permute-done.6.refs_4_) | copy-start | bytes 1572868
  84.5 27.0 %collective-permute-start.16 = (bf16[16,128,128]{2,1,0:T(8,128)(2,1)}, bf16[16,128,128]{2,1,0:T(8,128)(2,1)}, u32[]{:S(2)}, u32[]{:S(2)}) collective-permute-start(bf16[16,128,128]{2,1,0:T(8,128)(2,1)} %get-tuple-element.68), channel_id=1, source_target_pairs={{20,0},{24,4},{28,8},{32,12},{36,16},{40,20},{44,24},{48,28},{52,3... | collective-permute-start | bytes 1572872 | tf_op jit(solution)/shard_map/ppermute | solution.py:521
  85.8 8.0 %copy-start.8 = (bf16[16,128,128]{2,1,0:T(8,128)(2,1)}, bf16[16,128,128]{2,1,0:T(8,128)(2,1)S(1)}, u32[]{:S(2)}) copy-start(bf16[16,128,128]{2,1,0:T(8,128)(2,1)S(1)} %collective-permute-done.7.refs_5_) | copy-start | bytes 1572868
  85.8 32.4 %collective-permute-start.17 = (bf16[16,128,128]{2,1,0:T(8,128)(2,1)}, bf16[16,128,128]{2,1,0:T(8,128)(2,1)}, u32[]{:S(2)}, u32[]{:S(2)}) collective-permute-start(bf16[16,128,128]{2,1,0:T(8,128)(2,1)} %get-tuple-element.69), channel_id=1, source_target_pairs={{0,20},{4,24},{8,28},{12,32},{16,36},{20,40},{24,44},{28,48},{32,5... | collective-permute-start | bytes 1572872 | tf_op jit(solution)/shard_map/ppermute | solution.py:521
  92.4 1.4 copy-start.9
  92.4 27.2 %collective-permute-start.18 = (bf16[16,128,128]{2,1,0:T(8,128)(2,1)}, bf16[16,128,128]{2,1,0:T(8,128)(2,1)}, u32[]{:S(2)}, u32[]{:S(2)}) collective-permute-start(bf16[16,128,128]{2,1,0:T(8,128)(2,1)} %get-tuple-element.70), channel_id=1, source_target_pairs={{4,0},{8,4},{12,8},{16,12},{20,16},{24,20},{28,24},{32,28},{36,32}... | collective-permute-start | bytes 1572872 | tf_op jit(solution)/shard_map/ppermute | solution.py:521
  93.7 0.8 copy-start.10
  98.4 7.5 %collective-permute-start.11 = (bf16[256,128]{1,0:T(8,128)(2,1)}, bf16[256,128]{1,0:T(8,128)(2,1)S(1)}, u32[]{:S(2)}, u32[]{:S(2)}) collective-permute-start(bf16[256,128]{1,0:T(8,128)(2,1)} %pack_parts.1), channel_id=1, source_target_pairs={{1,0},{2,1},{3,2},{5,4},{6,5},{7,6},{9,8},{10,9},{11,10},{13,12},{... | collective-permute-start | bytes 196616 | tf_op jit(solution)/shard_map/ppermute | solution.py:524
  103.3 6.9 %collective-permute-start.10 = (bf16[256,128]{1,0:T(8,128)(2,1)}, bf16[256,128]{1,0:T(8,128)(2,1)S(1)}, u32[]{:S(2)}, u32[]{:S(2)}) collective-permute-start(bf16[256,128]{1,0:T(8,128)(2,1)} %pack_parts.1), channel_id=1, source_target_pairs={{0,1},{1,2},{2,3},{4,5},{5,6},{6,7},{8,9},{9,10},{10,11},{12,13},{... | collective-permute-start | bytes 196616 | tf_op jit(solution)/shard_map/ppermute | solution.py:524
  105.9 26.2 %copy-start.17 = (bf16[256,128]{1,0:T(8,128)(2,1)}, bf16[256,128]{1,0:T(8,128)(2,1)S(1)}, u32[]{:S(2)}) copy-start(bf16[256,128]{1,0:T(8,128)(2,1)S(1)} %collective-permute-done.11.from_right) | copy-start | bytes 196612
  105.9 31.6 %collective-permute-start.19 = (bf16[16,128,128]{2,1,0:T(8,128)(2,1)}, bf16[16,128,128]{2,1,0:T(8,128)(2,1)S(1)}, u32[]{:S(2)}, u32[]{:S(2)}) collective-permute-start(bf16[16,128,128]{2,1,0:T(8,128)(2,1)} %get-tuple-element.71), channel_id=1, source_target_pairs={{0,4},{4,8},{8,12},{12,16},{16,20},{20,24},{24,28},{28,32},{32,36}... | collective-permute-start | bytes 1572872 | tf_op jit(solution)/shard_map/ppermute | solution.py:521
  110.2 21.9 %copy-start.18 = (bf16[256,128]{1,0:T(8,128)(2,1)}, bf16[256,128]{1,0:T(8,128)(2,1)S(1)}, u32[]{:S(2)}) copy-start(bf16[256,128]{1,0:T(8,128)(2,1)S(1)} %collective-permute-done.10.from_left) | copy-start | bytes 196612
  110.2 27.3 %collective-permute-start.20 = (bf16[16,128,128]{2,1,0:T(8,128)(2,1)}, bf16[16,128,128]{2,1,0:T(8,128)(2,1)S(1)}, u32[]{:S(2)}, u32[]{:S(2)}) collective-permute-start(bf16[16,128,128]{2,1,0:T(8,128)(2,1)} %get-tuple-element.72), channel_id=1, source_target_pairs={{8,0},{12,4},{16,8},{20,12},{24,16},{28,20},{32,24},{36,28},{40,32... | collective-permute-start | bytes 1572872 | tf_op jit(solution)/shard_map/ppermute | solution.py:521
  111.5 26.0 %collective-permute-start.21 = (bf16[16,128,128]{2,1,0:T(8,128)(2,1)}, bf16[16,128,128]{2,1,0:T(8,128)(2,1)S(1)}, u32[]{:S(2)}, u32[]{:S(2)}) collective-permute-start(bf16[16,128,128]{2,1,0:T(8,128)(2,1)} %get-tuple-element.73), channel_id=1, source_target_pairs={{0,8},{4,12},{8,16},{12,20},{16,24},{20,28},{24,32},{28,36},{32,40... | collective-permute-start | bytes 1572872 | tf_op jit(solution)/shard_map/ppermute | solution.py:521
  118.3 36.4 %collective-permute-start.22 = (bf16[16,128,128]{2,1,0:T(8,128)(2,1)}, bf16[16,128,128]{2,1,0:T(8,128)(2,1)S(1)}, u32[]{:S(2)}, u32[]{:S(2)}) collective-permute-start(bf16[16,128,128]{2,1,0:T(8,128)(2,1)} %get-tuple-element.86), channel_id=1, source_target_pairs={{24,0},{28,4},{32,8},{36,12},{40,16},{44,20},{48,24},{52,28},{56,3... | collective-permute-start | bytes 1572872 | tf_op jit(solution)/shard_map/ppermute | solution.py:521
  119.6 35.1 %collective-permute-start.23 = (bf16[16,128,128]{2,1,0:T(8,128)(2,1)}, bf16[16,128,128]{2,1,0:T(8,128)(2,1)S(1)}, u32[]{:S(2)}, u32[]{:S(2)}) collective-permute-start(bf16[16,128,128]{2,1,0:T(8,128)(2,1)} %get-tuple-element.87), channel_id=1, source_target_pairs={{0,24},{4,28},{8,32},{12,36},{16,40},{20,44},{24,48},{28,52},{32,5... | collective-permute-start | bytes 1572872 | tf_op jit(solution)/shard_map/ppermute | solution.py:521
  137.5 0.8 copy-start.12
  137.5 1.0 copy-start.2
  137.5 1.1 copy-start.3
  154.6 0.8 copy-start.13
  155.4 0.8 copy-start.14

commit v4 on v3

--- a/solution.py
+++ b/solution.py
@@ -21,7 +21,7 @@
 MARGIN = 144
 VMEM_LIMIT = 60 * 1024 * 1024
 
-ORDER = (4, -4, 8, -8, 3, -3, 7, -7, 5, -5, 1, -1, 2, -2, 6, -6)
+ORDER = (4, -4, 8, -8, 3, -3, 7, -7, 5, -5, 2, -2, 1, -1, 6, -6)
 EARLY = ORDER[:8]
 LATE = ORDER[8:] + (0,)
 CODED = ROWS + 16

time: 165 us -> 162 us (0.982)
  the two profiles are of different devices: /device:TPU:6 before, /device:TPU:39 now
where the time goes in v4:
time: 162 us; the launch traced here: 161 us
  starting transfers between devices  73.4 us (45%)
  Pallas kernels  61.2 us (38%)
  waiting for transfers between devices  22.1 us (14%)
  local copies, waits for them, and re-layouts  3.69 us (2%)
    ppermute x8, starting transfers between devices, local(): moved[c] = lax.ppermute(parts[c], 'scan', pairs_of(c))  32.2 us
    pallas_call x2, Pallas kernels, shear(): pl.pallas_call(functools.partial(shear_kernel, group), out_shape=(PART,)...  30 us
    ppermute x8, starting transfers between devices, local(): lax.ppermute(part, 'scan', pairs_of(c))  27.3 us
    pallas_call x2, Pallas kernels, row_shear(): pl.pallas_call(kernel, out_shape=jax.ShapeDtypeStruct((SLAB, ROWS, COLS),...  12.3 us
    ppermute x8, waiting for transfers between devices, local(): moved[c] = lax.ppermute(parts[c], 'scan', pairs_of(c))  12.1 us
    pallas_call x1, Pallas kernels, pack_edges(): pl.pallas_call(pack_edges_kernel, out_shape=jax.ShapeDtypeStruct((EDGE_RO...  6.81 us
    pallas_call x1, Pallas kernels, smooth_parts(): pl.pallas_call(smooth_parts_kernel, out_shape=(jax.ShapeDtypeStruct((SLAB...  5.34 us
    ppermute x1, waiting for transfers between devices, local(): edges_after = lax.ppermute(edges, 'scan', down)  4.79 us
  transfers between devices with their start and end apart: 24, of which 8 were waited for; matrix products, arithmetic and copies ran while one was open for 0% of the time, Pallas kernels for 31%

profile of v4, /device:TPU:39, one launch (start us, length us, event | category | flops | bytes accessed | tf_op | source)
XLA Modules:
  0.0 161.1 jit_solution(2371305368293998775)
XLA Ops:
  0.0 2.9 %halos.1 = (bf16[2,2064,128]{2,1,0:T(8,128)(2,1)}, bf16[1,2064,128]{2,1,0:T(8,128)(2,1)}) custom-call(s32[16]{0:T(128)} %offsets.5, bf16[16,2048,128]{2,1,0:T(8,128)(2,1)} %raw_ref.5), custom_call_target="tpu_custom_call" | custom-call | flops 1000 | bytes 1000 | tf_op jit(solution)/shard_map/halos/pallas_call | solution.py:61
  2.9 0.7 collective-permute-start.1
  3.7 3.1 %collective-permute-start = (bf16[1,2064,128]{2,1,0:T(8,128)(2,1)}, bf16[1,2064,128]{2,1,0:T(8,128)(2,1)S(1)}, u32[]{:S(2)}, u32[]{:S(2)}) collective-permute-start(bf16[1,2064,128]{2,1,0:T(8,128)(2,1)} %get-tuple-element.49), channel_id=1, source_target_pairs={{0,4},{4,8},{8,12},{12,16},{16,20},{20,24},{24,28},{28,32},{32,36}... | collective-permute-start | bytes 1585160 | tf_op jit(solution)/shard_map/ppermute | solution.py:506
  6.8 6.8 %pack_edges.1 = bf16[512,128]{1,0:T(8,128)(2,1)} custom-call(bf16[16,2048,128]{2,1,0:T(8,128)(2,1)} %raw_ref.5), custom_call_target="tpu_custom_call" | custom-call | flops 1000 | bytes 1000 | tf_op jit(solution)/shard_map/pack_edges/pallas_call | solution.py:94
  13.6 2.5 %collective-permute-start.13 = (bf16[512,128]{1,0:T(8,128)(2,1)}, bf16[512,128]{1,0:T(8,128)(2,1)S(1)}, u32[]{:S(2)}, u32[]{:S(2)}) collective-permute-start(bf16[512,128]{1,0:T(8,128)(2,1)} %pack_edges.1), channel_id=1, source_target_pairs={{1,0},{2,1},{3,2},{5,4},{6,5},{7,6},{9,8},{10,9},{11,10},{13,12},{... | collective-permute-start | bytes 393224 | tf_op jit(solution)/shard_map/ppermute | solution.py:509
  16.0 1.3 collective-permute-start.12
  17.4 0.5 collective-permute-done.1.after_ref
  17.9 0.3 copy-done.1
  18.2 1.0 copy-done
  19.2 8.1 %shear_planes.2 = (bf16[16,128,128]{2,1,0:T(8,128)(2,1)}, bf16[16,128,128]{2,1,0:T(8,128)(2,1)}, bf16[16,128,128]{2,1,0:T(8,128)(2,1)}, bf16[16,128,128]{2,1,0:T...) custom-call(s32[16]{0:T(128)} %offsets.5, ...), custom_call_target="tpu_custom_call" | custom-call | flops 1000 | bytes 1000 | tf_op jit(solution)/shard_map/shear_planes/pallas_call | solution.py:249
  27.2 4.7 %collective-permute-start.3 = (bf16[16,128,128]{2,1,0:T(8,128)(2,1)}, bf16[16,128,128]{2,1,0:T(8,128)(2,1)S(1)}, u32[]{:S(2)}, u32[]{:S(2)}) collective-permute-start(bf16[16,128,128]{2,1,0:T(8,128)(2,1)} %get-tuple-element.52), channel_id=1, source_target_pairs={{0,16},{4,20},{8,24},{12,28},{16,32},{20,36},{24,40},{28,44},{32,4... | collective-permute-start | bytes 1572872 | tf_op jit(solution)/shard_map/ppermute | solution.py:512
  32.0 0.0 collective-permute-done.12
  32.0 0.1 collective-permute-start.15
  32.1 3.6 %collective-permute-start.14 = (bf16[512,128]{1,0:T(8,128)(2,1)S(1)}, bf16[512,128]{1,0:T(8,128)(2,1)S(1)}, u32[]{:S(2)}, u32[]{:S(2)}) collective-permute-start(bf16[512,128]{1,0:T(8,128)(2,1)S(1)} %fusion.rest_2_), channel_id=1, source_target_pairs={{0,4},{4,8},{8,12},{12,16},{16,20},{20,24},{24,28},{28,32},{32,36}... | collective-permute-start | bytes 393224 | tf_op jit(solution)/shard_map/ppermute | solution.py:517
  35.8 1.9 %collective-permute-start.4 = (bf16[16,128,128]{2,1,0:T(8,128)(2,1)}, bf16[16,128,128]{2,1,0:T(8,128)(2,1)S(1)}, u32[]{:S(2)}, u32[]{:S(2)}) collective-permute-start(bf16[16,128,128]{2,1,0:T(8,128)(2,1)} %get-tuple-element.53), channel_id=1, source_target_pairs={{32,0},{36,4},{40,8},{44,12},{48,16},{52,20},{56,24},{60,28},{64,3... | collective-permute-start | bytes 1572872 | tf_op jit(solution)/shard_map/ppermute | solution.py:512
  37.7 3.5 %collective-permute-start.5 = (bf16[16,128,128]{2,1,0:T(8,128)(2,1)}, bf16[16,128,128]{2,1,0:T(8,128)(2,1)S(1)}, u32[]{:S(2)}, u32[]{:S(2)}) collective-permute-start(bf16[16,128,128]{2,1,0:T(8,128)(2,1)} %get-tuple-element.54), channel_id=1, source_target_pairs={{0,32},{4,36},{8,40},{12,44},{16,48},{20,52},{24,56},{28,60},{32,6... | collective-permute-start | bytes 1572872 | tf_op jit(solution)/shard_map/ppermute | solution.py:512
  41.2 4.8 %collective-permute-done.15.rest_3_ = bf16[512,128]{1,0:T(8,128)(2,1)S(1)} collective-permute-done((bf16[512,128]{1,0:T(8,128)(2,1)S(1)}, bf16[512,128]{1,0:T(8,128)(2,1)S(1)}, u32[]{:S(2)}, u32[]{:S(2)}) %collective-permute-start.15) | collective-permute-done | bytes 131104 | tf_op jit(solution)/shard_map/ppermute | solution.py:516
  46.0 3.3 %collective-permute-start.6 = (bf16[16,128,128]{2,1,0:T(8,128)(2,1)}, bf16[16,128,128]{2,1,0:T(8,128)(2,1)S(1)}, u32[]{:S(2)}, u32[]{:S(2)}) collective-permute-start(bf16[16,128,128]{2,1,0:T(8,128)(2,1)} %get-tuple-element.55), channel_id=1, source_target_pairs={{12,0},{16,4},{20,8},{24,12},{28,16},{32,20},{36,24},{40,28},{44,3... | collective-permute-start | bytes 1572872 | tf_op jit(solution)/shard_map/ppermute | solution.py:512
  49.3 0.0 collective-permute-done.14.rest_1_
  49.4 3.8 %collective-permute-start.7 = (bf16[16,128,128]{2,1,0:T(8,128)(2,1)}, bf16[16,128,128]{2,1,0:T(8,128)(2,1)S(1)}, u32[]{:S(2)}, u32[]{:S(2)}) collective-permute-start(bf16[16,128,128]{2,1,0:T(8,128)(2,1)} %get-tuple-element.56), channel_id=1, source_target_pairs={{0,12},{4,16},{8,20},{12,24},{16,28},{20,32},{24,36},{28,40},{32,4... | collective-permute-start | bytes 1572872 | tf_op jit(solution)/shard_map/ppermute | solution.py:512
  53.1 1.9 %collective-permute-start.8 = (bf16[16,128,128]{2,1,0:T(8,128)(2,1)}, bf16[16,128,128]{2,1,0:T(8,128)(2,1)S(1)}, u32[]{:S(2)}, u32[]{:S(2)}) collective-permute-start(bf16[16,128,128]{2,1,0:T(8,128)(2,1)} %get-tuple-element.57), channel_id=1, source_target_pairs={{28,0},{32,4},{36,8},{40,12},{44,16},{48,20},{52,24},{56,28},{60,3... | collective-permute-start | bytes 1572872 | tf_op jit(solution)/shard_map/ppermute | solution.py:512
  55.1 3.6 %collective-permute-start.9 = (bf16[16,128,128]{2,1,0:T(8,128)(2,1)}, bf16[16,128,128]{2,1,0:T(8,128)(2,1)}, u32[]{:S(2)}, u32[]{:S(2)}) collective-permute-start(bf16[16,128,128]{2,1,0:T(8,128)(2,1)} %get-tuple-element.58), channel_id=1, source_target_pairs={{0,28},{4,32},{8,36},{12,40},{16,44},{20,48},{24,52},{28,56},{32,6... | collective-permute-start | bytes 1572872 | tf_op jit(solution)/shard_map/ppermute | solution.py:512
  58.7 2.3 %collective-permute-done.5.refs_3_ = bf16[16,128,128]{2,1,0:T(8,128)(2,1)S(1)} collective-permute-done((bf16[16,128,128]{2,1,0:T(8,128)(2,1)}, bf16[16,128,128]{2,1,0:T(8,128)(2,1)S(1)}, u32[]{:S(2)}, u32[]{:S(2)}) %collective-permute-start.5) | collective-permute-done | bytes 524320 | tf_op jit(solution)/shard_map/ppermute | solution.py:512
  61.0 4.6 %collective-permute-start.2 = (bf16[16,128,128]{2,1,0:T(8,128)(2,1)}, bf16[16,128,128]{2,1,0:T(8,128)(2,1)}, u32[]{:S(2)}, u32[]{:S(2)}) collective-permute-start(bf16[16,128,128]{2,1,0:T(8,128)(2,1)} %get-tuple-element.51), channel_id=1, source_target_pairs={{16,0},{20,4},{24,8},{28,12},{32,16},{36,20},{40,24},{44,28},{48,3... | collective-permute-start | bytes 1572872 | tf_op jit(solution)/shard_map/ppermute | solution.py:512
  65.6 21.9 %shear_planes.3 = (bf16[16,128,128]{2,1,0:T(8,128)(2,1)}, bf16[16,128,128]{2,1,0:T(8,128)(2,1)}, bf16[16,128,128]{2,1,0:T(8,128)(2,1)}, bf16[16,128,128]{2,1,0:T...) custom-call(s32[16]{0:T(128)} %offsets.5, ...), custom_call_target="tpu_custom_call" | custom-call | flops 1000 | bytes 1000 | tf_op jit(solution)/shard_map/shear_planes/pallas_call | solution.py:249
  87.5 0.0 copy-start.7
  87.5 3.6 %collective-permute-start.16 = (bf16[16,128,128]{2,1,0:T(8,128)(2,1)}, bf16[16,128,128]{2,1,0:T(8,128)(2,1)}, u32[]{:S(2)}, u32[]{:S(2)}) collective-permute-start(bf16[16,128,128]{2,1,0:T(8,128)(2,1)} %get-tuple-element.68), channel_id=1, source_target_pairs={{20,0},{24,4},{28,8},{32,12},{36,16},{40,20},{44,24},{48,28},{52,3... | collective-permute-start | bytes 1572872 | tf_op jit(solution)/shard_map/ppermute | solution.py:521
  91.1 3.2 %collective-permute-start.17 = (bf16[16,128,128]{2,1,0:T(8,128)(2,1)}, bf16[16,128,128]{2,1,0:T(8,128)(2,1)}, u32[]{:S(2)}, u32[]{:S(2)}) collective-permute-start(bf16[16,128,128]{2,1,0:T(8,128)(2,1)} %get-tuple-element.69), channel_id=1, source_target_pairs={{0,20},{4,24},{8,28},{12,32},{16,36},{20,40},{24,44},{28,48},{32,5... | collective-permute-start | bytes 1572872 | tf_op jit(solution)/shard_map/ppermute | solution.py:521
  94.3 13.0 %collective-permute-start.18 = (bf16[16,128,128]{2,1,0:T(8,128)(2,1)}, bf16[16,128,128]{2,1,0:T(8,128)(2,1)S(1)}, u32[]{:S(2)}, u32[]{:S(2)}) collective-permute-start(bf16[16,128,128]{2,1,0:T(8,128)(2,1)} %get-tuple-element.70), channel_id=1, source_target_pairs={{8,0},{12,4},{16,8},{20,12},{24,16},{28,20},{32,24},{36,28},{40,32... | collective-permute-start | bytes 1572872 | tf_op jit(solution)/shard_map/ppermute | solution.py:521
  107.5 3.9 %pack_parts.1 = bf16[256,128]{1,0:T(8,128)(2,1)} custom-call(bf16[16,128,128]{2,1,0:T(8,128)(2,1)} %collective-permute-done.2.refs_0_, bf16[16,128,128]{2,1,0:T(8,128)(2,1)} %copy-done.4, bf16[16,128,128]{2,1,0:T(8,128)(2,1)} %copy-done.5, bf16[16,128,128]{2,1,0:T(8,128)(2,1)} %copy-done.6, bf16[16,128,128]{2,1,0:T(8,128)(2,1)} %copy-done.7, ...), custom_call_target="tpu_custom_call" | custom-call | flops 1000 | bytes 1000 | tf_op jit(solution)/shard_map/pack_parts/pallas_call | solution.py:286
  111.4 1.3 collective-permute-start.11
  112.7 1.3 collective-permute-start.10
  114.0 0.3 collective-permute-done.11.from_right
  114.3 1.9 %collective-permute-start.19 = (bf16[16,128,128]{2,1,0:T(8,128)(2,1)}, bf16[16,128,128]{2,1,0:T(8,128)(2,1)S(1)}, u32[]{:S(2)}, u32[]{:S(2)}) collective-permute-start(bf16[16,128,128]{2,1,0:T(8,128)(2,1)} %get-tuple-element.71), channel_id=1, source_target_pairs={{0,8},{4,12},{8,16},{12,20},{16,24},{20,28},{24,32},{28,36},{32,40... | collective-permute-start | bytes 1572872 | tf_op jit(solution)/shard_map/ppermute | solution.py:521
  116.2 2.1 %collective-permute-done.10.from_left = bf16[256,128]{1,0:T(8,128)(2,1)S(1)} collective-permute-done((bf16[256,128]{1,0:T(8,128)(2,1)}, bf16[256,128]{1,0:T(8,128)(2,1)S(1)}, u32[]{:S(2)}, u32[]{:S(2)}) %collective-permute-start.10) | collective-permute-done | bytes 65568 | tf_op jit(solution)/shard_map/ppermute | solution.py:524
  118.3 1.9 %collective-permute-start.20 = (bf16[16,128,128]{2,1,0:T(8,128)(2,1)}, bf16[16,128,128]{2,1,0:T(8,128)(2,1)S(1)}, u32[]{:S(2)}, u32[]{:S(2)}) collective-permute-start(bf16[16,128,128]{2,1,0:T(8,128)(2,1)} %get-tuple-element.72), channel_id=1, source_target_pairs={{4,0},{8,4},{12,8},{16,12},{20,16},{24,20},{28,24},{32,28},{36,32}... | collective-permute-start | bytes 1572872 | tf_op jit(solution)/shard_map/ppermute | solution.py:521
  120.2 1.8 %collective-permute-start.21 = (bf16[16,128,128]{2,1,0:T(8,128)(2,1)}, bf16[16,128,128]{2,1,0:T(8,128)(2,1)S(1)}, u32[]{:S(2)}, u32[]{:S(2)}) collective-permute-start(bf16[16,128,128]{2,1,0:T(8,128)(2,1)} %get-tuple-element.73), channel_id=1, source_target_pairs={{0,4},{4,8},{8,12},{12,16},{16,20},{20,24},{24,28},{28,32},{32,36}... | collective-permute-start | bytes 1572872 | tf_op jit(solution)/shard_map/ppermute | solution.py:521
  122.0 1.9 %collective-permute-start.22 = (bf16[16,128,128]{2,1,0:T(8,128)(2,1)}, bf16[16,128,128]{2,1,0:T(8,128)(2,1)S(1)}, u32[]{:S(2)}, u32[]{:S(2)}) collective-permute-start(bf16[16,128,128]{2,1,0:T(8,128)(2,1)} %get-tuple-element.86), channel_id=1, source_target_pairs={{24,0},{28,4},{32,8},{36,12},{40,16},{44,20},{48,24},{52,28},{56,3... | collective-permute-start | bytes 1572872 | tf_op jit(solution)/shard_map/ppermute | solution.py:521
  124.0 4.8 %collective-permute-start.23 = (bf16[16,128,128]{2,1,0:T(8,128)(2,1)}, bf16[16,128,128]{2,1,0:T(8,128)(2,1)S(1)}, u32[]{:S(2)}, u32[]{:S(2)}) collective-permute-start(bf16[16,128,128]{2,1,0:T(8,128)(2,1)} %get-tuple-element.87), channel_id=1, source_target_pairs={{0,24},{4,28},{8,32},{12,36},{16,40},{20,44},{24,48},{28,52},{32,5... | collective-permute-start | bytes 1572872 | tf_op jit(solution)/shard_map/ppermute | solution.py:521
  128.8 5.3 %smooth_parts.1 = (bf16[16,128,128]{2,1,0:T(8,128)(2,1)}, bf16[16,128,128]{2,1,0:T(8,128)(2,1)}, bf16[16,128,128]{2,1,0:T(8,128)(2,1)}, bf16[16,128,128]{2,1,0:T...) custom-call(bf16[256,128]{1,0:T(8,128)(2,1)} %copy-done.18, ...), custom_call_target="tpu_custom_call" | custom-call | flops 1000 | bytes 1000 | tf_op jit(solution)/shard_map/smooth_parts/pallas_call | solution.py:315
  134.1 0.1 collective-permute-done.19.refs_3_.refs_11_
  134.2 3.5 %collective-permute-done.21.refs_5_ = bf16[16,128,128]{2,1,0:T(8,128)(2,1)S(1)} collective-permute-done((bf16[16,128,128]{2,1,0:T(8,128)(2,1)}, bf16[16,128,128]{2,1,0:T(8,128)(2,1)S(1)}, u32[]{:S(2)}, u32[]{:S(2)}) %collective-permute-start.21) | collective-permute-done | bytes 524320 | tf_op jit(solution)/shard_map/ppermute | solution.py:521
  137.8 0.8 copy-done.13
  138.6 4.3 %shear_rows.2.refs_14_ = bf16[16,2048,128]{2,1,0:T(8,128)(2,1)} custom-call(bf16[16,128,128]{2,1,0:T(8,128)(2,1)} %get-tuple-element.78.refs_0_.refs_4_, bf16[16,128,128]{2,1,0:T(8,128)(2,1)} %get-tuple-element.79.refs_1_.refs_5_, bf16[16,128,128]{2,1,0:T(8,128)(2,1)} %copy-done.2, bf16[16,128,128]{2,1,0:T(8,128)(2,1)} %copy-done.3, ...), custom_call_target="tpu_custom_call" | custom-call | flops 1000 | bytes 1000 | tf_op jit(solution)/shard_map/shear_rows/pallas_call | solution.py:473
  142.9 8.5 %collective-permute-done.22.refs_12_ = bf16[16,128,128]{2,1,0:T(8,128)(2,1)S(1)} collective-permute-done((bf16[16,128,128]{2,1,0:T(8,128)(2,1)}, bf16[16,128,128]{2,1,0:T(8,128)(2,1)S(1)}, u32[]{:S(2)}, u32[]{:S(2)}) %collective-permute-start.22) | collective-permute-done | bytes 524320 | tf_op jit(solution)/shard_map/ppermute | solution.py:521
  151.4 0.8 copy-done.12
  152.2 0.8 copy-done.14
  153.0 8.0 %shear_rows.3 = bf16[16,2048,128]{2,1,0:T(8,128)(2,1)} custom-call(bf16[16,128,128]{2,1,0:T(8,128)(2,1)} %get-tuple-element.74.refs_0_, bf16[16,128,128]{2,1,0:T(8,128)(2,1)} %get-tuple-element.75.refs_1_, bf16[16,128,128]{2,1,0:T(8,128)(2,1)} %get-tuple-element.76.refs_2_, ...), custom_call_target="tpu_custom_call", output_to_operand_aliasing={{}: (14, {})} | custom-call | flops 1000 | bytes 1000 | tf_op jit(solution)/shard_map/shear_rows/pallas_call | solution.py:473
  (49 shorter events, 0.1 us)
Async XLA Ops:
  2.9 15.0 %collective-permute-start.1 = (bf16[2,2064,128]{2,1,0:T(8,128)(2,1)}, bf16[2,2064,128]{2,1,0:T(8,128)(2,1)S(1)}, u32[]{:S(2)}, u32[]{:S(2)}) collective-permute-start(bf16[2,2064,128]{2,1,0:T(8,128)(2,1)} %get-tuple-element.50), channel_id=1, source_target_pairs={{4,0},{8,4},{12,8},{16,12},{20,16},{24,20},{28,24},{32,28},{36,32}... | collective-permute-start | bytes 3170312 | tf_op jit(solution)/shard_map/ppermute | solution.py:505
  3.7 13.7 %collective-permute-start = (bf16[1,2064,128]{2,1,0:T(8,128)(2,1)}, bf16[1,2064,128]{2,1,0:T(8,128)(2,1)S(1)}, u32[]{:S(2)}, u32[]{:S(2)}) collective-permute-start(bf16[1,2064,128]{2,1,0:T(8,128)(2,1)} %get-tuple-element.49), channel_id=1, source_target_pairs={{0,4},{4,8},{8,12},{12,16},{16,20},{20,24},{24,28},{28,32},{32,36}... | collective-permute-start | bytes 1585160 | tf_op jit(solution)/shard_map/ppermute | solution.py:506
  13.6 18.4 %collective-permute-start.13 = (bf16[512,128]{1,0:T(8,128)(2,1)}, bf16[512,128]{1,0:T(8,128)(2,1)S(1)}, u32[]{:S(2)}, u32[]{:S(2)}) collective-permute-start(bf16[512,128]{1,0:T(8,128)(2,1)} %pack_edges.1), channel_id=1, source_target_pairs={{1,0},{2,1},{3,2},{5,4},{6,5},{7,6},{9,8},{10,9},{11,10},{13,12},{... | collective-permute-start | bytes 393224 | tf_op jit(solution)/shard_map/ppermute | solution.py:509
  16.0 15.9 %collective-permute-start.12 = (bf16[512,128]{1,0:T(8,128)(2,1)}, bf16[512,128]{1,0:T(8,128)(2,1)S(1)}, u32[]{:S(2)}, u32[]{:S(2)}) collective-permute-start(bf16[512,128]{1,0:T(8,128)(2,1)} %pack_edges.1), channel_id=1, source_target_pairs={{0,1},{1,2},{2,3},{4,5},{5,6},{6,7},{8,9},{9,10},{10,11},{12,13},{... | collective-permute-start | bytes 393224 | tf_op jit(solution)/shard_map/ppermute | solution.py:508
  17.4 0.8 copy-start.1
  18.2 1.0 copy-start
  27.2 25.9 %collective-permute-start.3 = (bf16[16,128,128]{2,1,0:T(8,128)(2,1)}, bf16[16,128,128]{2,1,0:T(8,128)(2,1)S(1)}, u32[]{:S(2)}, u32[]{:S(2)}) collective-permute-start(bf16[16,128,128]{2,1,0:T(8,128)(2,1)} %get-tuple-element.52), channel_id=1, source_target_pairs={{0,16},{4,20},{8,24},{12,28},{16,32},{20,36},{24,40},{28,44},{32,4... | collective-permute-start | bytes 1572872 | tf_op jit(solution)/shard_map/ppermute | solution.py:512
  32.0 33.5 %copy-start.10 = (bf16[512,128]{1,0:T(8,128)(2,1)}, bf16[512,128]{1,0:T(8,128)(2,1)S(1)}, u32[]{:S(2)}) copy-start(bf16[512,128]{1,0:T(8,128)(2,1)S(1)} %fusion.rest_2_) | copy-start | bytes 393220
  32.0 14.0 %collective-permute-start.15 = (bf16[512,128]{1,0:T(8,128)(2,1)S(1)}, bf16[512,128]{1,0:T(8,128)(2,1)S(1)}, u32[]{:S(2)}, u32[]{:S(2)}) collective-permute-start(bf16[512,128]{1,0:T(8,128)(2,1)S(1)} %fusion.rest_2_), channel_id=1, source_target_pairs={{4,0},{8,4},{12,8},{16,12},{20,16},{24,20},{28,24},{32,28},{36,32}... | collective-permute-start | bytes 393224 | tf_op jit(solution)/shard_map/ppermute | solution.py:516
  32.1 17.2 %collective-permute-start.14 = (bf16[512,128]{1,0:T(8,128)(2,1)S(1)}, bf16[512,128]{1,0:T(8,128)(2,1)S(1)}, u32[]{:S(2)}, u32[]{:S(2)}) collective-permute-start(bf16[512,128]{1,0:T(8,128)(2,1)S(1)} %fusion.rest_2_), channel_id=1, source_target_pairs={{0,4},{4,8},{8,12},{12,16},{16,20},{20,24},{24,28},{28,32},{32,36}... | collective-permute-start | bytes 393224 | tf_op jit(solution)/shard_map/ppermute | solution.py:517
  35.8 19.3 %collective-permute-start.4 = (bf16[16,128,128]{2,1,0:T(8,128)(2,1)}, bf16[16,128,128]{2,1,0:T(8,128)(2,1)S(1)}, u32[]{:S(2)}, u32[]{:S(2)}) collective-permute-start(bf16[16,128,128]{2,1,0:T(8,128)(2,1)} %get-tuple-element.53), channel_id=1, source_target_pairs={{32,0},{36,4},{40,8},{44,12},{48,16},{52,20},{56,24},{60,28},{64,3... | collective-permute-start | bytes 1572872 | tf_op jit(solution)/shard_map/ppermute | solution.py:512
  37.7 23.3 %collective-permute-start.5 = (bf16[16,128,128]{2,1,0:T(8,128)(2,1)}, bf16[16,128,128]{2,1,0:T(8,128)(2,1)S(1)}, u32[]{:S(2)}, u32[]{:S(2)}) collective-permute-start(bf16[16,128,128]{2,1,0:T(8,128)(2,1)} %get-tuple-element.54), channel_id=1, source_target_pairs={{0,32},{4,36},{8,40},{12,44},{16,48},{20,52},{24,56},{28,60},{32,6... | collective-permute-start | bytes 1572872 | tf_op jit(solution)/shard_map/ppermute | solution.py:512
  46.0 19.6 %copy-start.15 = (bf16[512,128]{1,0:T(8,128)(2,1)}, bf16[512,128]{1,0:T(8,128)(2,1)S(1)}, u32[]{:S(2)}) copy-start(bf16[512,128]{1,0:T(8,128)(2,1)S(1)} %collective-permute-done.15.rest_3_) | copy-start | bytes 393220
  46.0 41.5 %collective-permute-start.6 = (bf16[16,128,128]{2,1,0:T(8,128)(2,1)}, bf16[16,128,128]{2,1,0:T(8,128)(2,1)S(1)}, u32[]{:S(2)}, u32[]{:S(2)}) collective-permute-start(bf16[16,128,128]{2,1,0:T(8,128)(2,1)} %get-tuple-element.55), channel_id=1, source_target_pairs={{12,0},{16,4},{20,8},{24,12},{28,16},{32,20},{36,24},{40,28},{44,3... | collective-permute-start | bytes 1572872 | tf_op jit(solution)/shard_map/ppermute | solution.py:512
  49.3 16.2 %copy-start.16 = (bf16[512,128]{1,0:T(8,128)(2,1)}, bf16[512,128]{1,0:T(8,128)(2,1)S(1)}, u32[]{:S(2)}) copy-start(bf16[512,128]{1,0:T(8,128)(2,1)S(1)} %collective-permute-done.14.rest_1_) | copy-start | bytes 393220
  49.4 41.7 %collective-permute-start.7 = (bf16[16,128,128]{2,1,0:T(8,128)(2,1)}, bf16[16,128,128]{2,1,0:T(8,128)(2,1)S(1)}, u32[]{:S(2)}, u32[]{:S(2)}) collective-permute-start(bf16[16,128,128]{2,1,0:T(8,128)(2,1)} %get-tuple-element.56), channel_id=1, source_target_pairs={{0,12},{4,16},{8,20},{12,24},{16,28},{20,32},{24,36},{28,40},{32,4... | collective-permute-start | bytes 1572872 | tf_op jit(solution)/shard_map/ppermute | solution.py:512
  53.1 54.3 %copy-start.4 = (bf16[16,128,128]{2,1,0:T(8,128)(2,1)}, bf16[16,128,128]{2,1,0:T(8,128)(2,1)S(1)}, u32[]{:S(2)}) copy-start(bf16[16,128,128]{2,1,0:T(8,128)(2,1)S(1)} %collective-permute-done.3.refs_1_) | copy-start | bytes 1572868
  53.1 41.2 %collective-permute-start.8 = (bf16[16,128,128]{2,1,0:T(8,128)(2,1)}, bf16[16,128,128]{2,1,0:T(8,128)(2,1)S(1)}, u32[]{:S(2)}, u32[]{:S(2)}) collective-permute-start(bf16[16,128,128]{2,1,0:T(8,128)(2,1)} %get-tuple-element.57), channel_id=1, source_target_pairs={{28,0},{32,4},{36,8},{40,12},{44,16},{48,20},{52,24},{56,28},{60,3... | collective-permute-start | bytes 1572872 | tf_op jit(solution)/shard_map/ppermute | solution.py:512
  55.1 52.3 %copy-start.5 = (bf16[16,128,128]{2,1,0:T(8,128)(2,1)}, bf16[16,128,128]{2,1,0:T(8,128)(2,1)S(1)}, u32[]{:S(2)}) copy-start(bf16[16,128,128]{2,1,0:T(8,128)(2,1)S(1)} %collective-permute-done.4.refs_2_) | copy-start | bytes 1572868
  55.1 52.3 %collective-permute-start.9 = (bf16[16,128,128]{2,1,0:T(8,128)(2,1)}, bf16[16,128,128]{2,1,0:T(8,128)(2,1)}, u32[]{:S(2)}, u32[]{:S(2)}) collective-permute-start(bf16[16,128,128]{2,1,0:T(8,128)(2,1)} %get-tuple-element.58), channel_id=1, source_target_pairs={{0,28},{4,32},{8,36},{12,40},{16,44},{20,48},{24,52},{28,56},{32,6... | collective-permute-start | bytes 1572872 | tf_op jit(solution)/shard_map/ppermute | solution.py:512
  61.0 46.4 %copy-start.6 = (bf16[16,128,128]{2,1,0:T(8,128)(2,1)}, bf16[16,128,128]{2,1,0:T(8,128)(2,1)S(1)}, u32[]{:S(2)}) copy-start(bf16[16,128,128]{2,1,0:T(8,128)(2,1)S(1)} %collective-permute-done.5.refs_3_) | copy-start | bytes 1572868
  61.0 46.4 %collective-permute-start.2 = (bf16[16,128,128]{2,1,0:T(8,128)(2,1)}, bf16[16,128,128]{2,1,0:T(8,128)(2,1)}, u32[]{:S(2)}, u32[]{:S(2)}) collective-permute-start(bf16[16,128,128]{2,1,0:T(8,128)(2,1)} %get-tuple-element.51), channel_id=1, source_target_pairs={{16,0},{20,4},{24,8},{28,12},{32,16},{36,20},{40,24},{44,28},{48,3... | collective-permute-start | bytes 1572872 | tf_op jit(solution)/shard_map/ppermute | solution.py:512
  87.5 19.9 %copy-start.7 = (bf16[16,128,128]{2,1,0:T(8,128)(2,1)}, bf16[16,128,128]{2,1,0:T(8,128)(2,1)S(1)}, u32[]{:S(2)}) copy-start(bf16[16,128,128]{2,1,0:T(8,128)(2,1)S(1)} %collective-permute-done.6.refs_4_) | copy-start | bytes 1572868
  87.5 32.7 %collective-permute-start.16 = (bf16[16,128,128]{2,1,0:T(8,128)(2,1)}, bf16[16,128,128]{2,1,0:T(8,128)(2,1)}, u32[]{:S(2)}, u32[]{:S(2)}) collective-permute-start(bf16[16,128,128]{2,1,0:T(8,128)(2,1)} %get-tuple-element.68), channel_id=1, source_target_pairs={{20,0},{24,4},{28,8},{32,12},{36,16},{40,20},{44,24},{48,28},{52,3... | collective-permute-start | bytes 1572872 | tf_op jit(solution)/shard_map/ppermute | solution.py:521
  91.1 16.4 %copy-start.8 = (bf16[16,128,128]{2,1,0:T(8,128)(2,1)}, bf16[16,128,128]{2,1,0:T(8,128)(2,1)S(1)}, u32[]{:S(2)}) copy-start(bf16[16,128,128]{2,1,0:T(8,128)(2,1)S(1)} %collective-permute-done.7.refs_5_) | copy-start | bytes 1572868
  91.1 30.9 %collective-permute-start.17 = (bf16[16,128,128]{2,1,0:T(8,128)(2,1)}, bf16[16,128,128]{2,1,0:T(8,128)(2,1)}, u32[]{:S(2)}, u32[]{:S(2)}) collective-permute-start(bf16[16,128,128]{2,1,0:T(8,128)(2,1)} %get-tuple-element.69), channel_id=1, source_target_pairs={{0,20},{4,24},{8,28},{12,32},{16,36},{20,40},{24,44},{28,48},{32,5... | collective-permute-start | bytes 1572872 | tf_op jit(solution)/shard_map/ppermute | solution.py:521
  94.3 13.1 %copy-start.9 = (bf16[16,128,128]{2,1,0:T(8,128)(2,1)}, bf16[16,128,128]{2,1,0:T(8,128)(2,1)S(1)}, u32[]{:S(2)}) copy-start(bf16[16,128,128]{2,1,0:T(8,128)(2,1)S(1)} %collective-permute-done.8.refs_6_) | copy-start | bytes 1572868
  94.3 29.6 %collective-permute-start.18 = (bf16[16,128,128]{2,1,0:T(8,128)(2,1)}, bf16[16,128,128]{2,1,0:T(8,128)(2,1)S(1)}, u32[]{:S(2)}, u32[]{:S(2)}) collective-permute-start(bf16[16,128,128]{2,1,0:T(8,128)(2,1)} %get-tuple-element.70), channel_id=1, source_target_pairs={{8,0},{12,4},{16,8},{20,12},{24,16},{28,20},{32,24},{36,28},{40,32... | collective-permute-start | bytes 1572872 | tf_op jit(solution)/shard_map/ppermute | solution.py:521
  111.4 2.9 %collective-permute-start.11 = (bf16[256,128]{1,0:T(8,128)(2,1)}, bf16[256,128]{1,0:T(8,128)(2,1)S(1)}, u32[]{:S(2)}, u32[]{:S(2)}) collective-permute-start(bf16[256,128]{1,0:T(8,128)(2,1)} %pack_parts.1), channel_id=1, source_target_pairs={{1,0},{2,1},{3,2},{5,4},{6,5},{7,6},{9,8},{10,9},{11,10},{13,12},{... | collective-permute-start | bytes 196616 | tf_op jit(solution)/shard_map/ppermute | solution.py:524
  112.7 5.6 %collective-permute-start.10 = (bf16[256,128]{1,0:T(8,128)(2,1)}, bf16[256,128]{1,0:T(8,128)(2,1)S(1)}, u32[]{:S(2)}, u32[]{:S(2)}) collective-permute-start(bf16[256,128]{1,0:T(8,128)(2,1)} %pack_parts.1), channel_id=1, source_target_pairs={{0,1},{1,2},{2,3},{4,5},{5,6},{6,7},{8,9},{9,10},{10,11},{12,13},{... | collective-permute-start | bytes 196616 | tf_op jit(solution)/shard_map/ppermute | solution.py:524
  114.3 14.5 %copy-start.17 = (bf16[256,128]{1,0:T(8,128)(2,1)}, bf16[256,128]{1,0:T(8,128)(2,1)S(1)}, u32[]{:S(2)}) copy-start(bf16[256,128]{1,0:T(8,128)(2,1)S(1)} %collective-permute-done.11.from_right) | copy-start | bytes 196612
  114.3 19.9 %collective-permute-start.19 = (bf16[16,128,128]{2,1,0:T(8,128)(2,1)}, bf16[16,128,128]{2,1,0:T(8,128)(2,1)S(1)}, u32[]{:S(2)}, u32[]{:S(2)}) collective-permute-start(bf16[16,128,128]{2,1,0:T(8,128)(2,1)} %get-tuple-element.71), channel_id=1, source_target_pairs={{0,8},{4,12},{8,16},{12,20},{16,24},{20,28},{24,32},{28,36},{32,40... | collective-permute-start | bytes 1572872 | tf_op jit(solution)/shard_map/ppermute | solution.py:521
  118.3 10.5 %copy-start.18 = (bf16[256,128]{1,0:T(8,128)(2,1)}, bf16[256,128]{1,0:T(8,128)(2,1)S(1)}, u32[]{:S(2)}) copy-start(bf16[256,128]{1,0:T(8,128)(2,1)S(1)} %collective-permute-done.10.from_left) | copy-start | bytes 196612
  118.3 15.9 %collective-permute-start.20 = (bf16[16,128,128]{2,1,0:T(8,128)(2,1)}, bf16[16,128,128]{2,1,0:T(8,128)(2,1)S(1)}, u32[]{:S(2)}, u32[]{:S(2)}) collective-permute-start(bf16[16,128,128]{2,1,0:T(8,128)(2,1)} %get-tuple-element.72), channel_id=1, source_target_pairs={{4,0},{8,4},{12,8},{16,12},{20,16},{24,20},{28,24},{32,28},{36,32}... | collective-permute-start | bytes 1572872 | tf_op jit(solution)/shard_map/ppermute | solution.py:521
  120.2 17.5 %collective-permute-start.21 = (bf16[16,128,128]{2,1,0:T(8,128)(2,1)}, bf16[16,128,128]{2,1,0:T(8,128)(2,1)S(1)}, u32[]{:S(2)}, u32[]{:S(2)}) collective-permute-start(bf16[16,128,128]{2,1,0:T(8,128)(2,1)} %get-tuple-element.73), channel_id=1, source_target_pairs={{0,4},{4,8},{8,12},{12,16},{16,20},{20,24},{24,28},{28,32},{32,36}... | collective-permute-start | bytes 1572872 | tf_op jit(solution)/shard_map/ppermute | solution.py:521
  122.0 29.3 %collective-permute-start.22 = (bf16[16,128,128]{2,1,0:T(8,128)(2,1)}, bf16[16,128,128]{2,1,0:T(8,128)(2,1)S(1)}, u32[]{:S(2)}, u32[]{:S(2)}) collective-permute-start(bf16[16,128,128]{2,1,0:T(8,128)(2,1)} %get-tuple-element.86), channel_id=1, source_target_pairs={{24,0},{28,4},{32,8},{36,12},{40,16},{44,20},{48,24},{52,28},{56,3... | collective-permute-start | bytes 1572872 | tf_op jit(solution)/shard_map/ppermute | solution.py:521
  123.9 13.8 %copy-start.2 = (bf16[16,128,128]{2,1,0:T(8,128)(2,1)}, bf16[16,128,128]{2,1,0:T(8,128)(2,1)S(1)}, u32[]{:S(2)}) copy-start(bf16[16,128,128]{2,1,0:T(8,128)(2,1)S(1)} %collective-permute-done.18.refs_2_.refs_10_) | copy-start | bytes 1572868
  124.0 27.4 %collective-permute-start.23 = (bf16[16,128,128]{2,1,0:T(8,128)(2,1)}, bf16[16,128,128]{2,1,0:T(8,128)(2,1)S(1)}, u32[]{:S(2)}, u32[]{:S(2)}) collective-permute-start(bf16[16,128,128]{2,1,0:T(8,128)(2,1)} %get-tuple-element.87), channel_id=1, source_target_pairs={{0,24},{4,28},{8,32},{12,36},{16,40},{20,44},{24,48},{28,52},{32,5... | collective-permute-start | bytes 1572872 | tf_op jit(solution)/shard_map/ppermute | solution.py:521
  134.2 3.6 %copy-start.3 = (bf16[16,128,128]{2,1,0:T(8,128)(2,1)}, bf16[16,128,128]{2,1,0:T(8,128)(2,1)S(1)}, u32[]{:S(2)}) copy-start(bf16[16,128,128]{2,1,0:T(8,128)(2,1)S(1)} %collective-permute-done.19.refs_3_.refs_11_) | copy-start | bytes 1572868
  134.2 3.6 %copy-start.11 = (bf16[16,128,128]{2,1,0:T(8,128)(2,1)}, bf16[16,128,128]{2,1,0:T(8,128)(2,1)S(1)}, u32[]{:S(2)}) copy-start(bf16[16,128,128]{2,1,0:T(8,128)(2,1)S(1)} %collective-permute-done.20.refs_4_) | copy-start | bytes 1572868
  137.8 0.8 copy-start.13
  151.4 0.8 copy-start.12
  152.2 0.8 copy-start.14
